TPU v7x, 32 devices: a whole 2x2x4 slice. The times are simulated.
32 devices in a mesh: dp: 8 (over z, y), tensor: 4 (over x, core).
Axes of the slice: x: 2, y: 2, z: 4, core: 2. Of those that a mesh axis runs over, the one named last changes fastest.
Arguments:
- tokens: bfloat16 [4096, 1024], P(('dp', 'tensor')), may hold values from -6 to 6
- key_mask: int32 [4096], P('dp'), may hold values 0 or 1
- seq_lengths: int32 [8, 4], P('dp'), may hold values from 0 to 512, as said below
- w_query: bfloat16 [1024, 1024], P('dp', 'tensor'), may hold values from -0.1875 to 0.1875
- b_query: float32 [1024], P('tensor'), may hold values from -3 to 3
- w_key: bfloat16 [1024, 1024], P('dp', 'tensor'), may hold values from -0.1875 to 0.1875
- w_value: bfloat16 [1024, 1024], P('dp', 'tensor'), may hold values from -0.1875 to 0.1875
- b_value: float32 [1024], P('tensor'), may hold values from -0.625 to 0.625
- w_proj: bfloat16 [1024, 1024], P('tensor', 'dp'), may hold values from -1.5 to 1.5
- b_proj: float32 [1024], replicated, may hold values from -1.75 to 1.75
- gain_attn: float32 [1024], replicated, may hold values from 0.1 to 1.9
- shift_attn: float32 [1024], replicated, may hold values from -1.75 to 1.75
- w_inner: bfloat16 [1024, 4096], P('dp', 'tensor'), may hold values from -0.1875 to 0.1875
- b_inner: float32 [4096], P('tensor'), may hold values from -1.75 to 1.75
- w_outer: bfloat16 [4096, 1024], P('tensor', 'dp'), may hold values from -0.09375 to 0.09375
- b_outer: float32 [1024], replicated, may hold values from -1.75 to 1.75
- gain_ffn: float32 [1024], replicated, may hold values from 0.1 to 1.9
- shift_ffn: float32 [1024], replicated, may hold values from -1.75 to 1.75
- out_grad: bfloat16 [4096, 1024], P(('dp', 'tensor')), may hold values from -6 to 6
Outputs:
- layer_out: bfloat16 [4096, 1024], P(('dp', 'tensor'))
- tokens_grad: float32 [4096, 1024], P(('dp', 'tensor'))
- dw_query: float32 [1024, 1024], P('dp', 'tensor')
- db_query: float32 [1024], P('tensor')
- dw_key: float32 [1024, 1024], P('dp', 'tensor')
- dw_value: float32 [1024, 1024], P('dp', 'tensor')
- db_value: float32 [1024], P('tensor')
- dw_proj: float32 [1024, 1024], P('tensor', 'dp')
- db_proj: float32 [1024], replicated
- dgain_attn: float32 [1024], replicated
- dshift_attn: float32 [1024], replicated
- dw_inner: float32 [1024, 4096], P('dp', 'tensor')
- db_inner: float32 [4096], P('tensor')
- dw_outer: float32 [4096, 1024], P('tensor', 'dp')
- db_outer: float32 [1024], replicated
- dgain_ffn: float32 [1024], replicated
- dshift_ffn: float32 [1024], replicated
Inputs may be any that keep to these rules, and one draw needn't show every extreme that they name: `seq_lengths`: in every data group the lengths sum to 512 or less; the rows after that sum are padding. In every group one sequence starts at row 96 or earlier and ends after row 3 * 512 // 4 (that row belongs to it); in some group it is the only one and fills all 512 rows.
All inputs are finite; a program needn't handle non-finite values. No bound on the sum of `key_mask` on one device may be relied on, other than what follows from the above.
Results may differ from a plain program's by a relative error of at most 0.015.
Values may be sent and summed in bfloat16 or wider, within the bound.
No kernel may reach another device: no remote copies, remote signals or barrier semaphores. Data moves between devices by JAX's collectives and lax.ppermute only.
A program may use at most 128 MiB of HBM per device.

v0:
```python
from functools import partial

import jax
import jax.numpy as jnp
from jax import lax
from jax.sharding import PartitionSpec as P

HEAD_DIM = 64


epsilon = 1e-12
masked_fill = -1e30


def layer_norm(values_in, norm_gain, norm_shift):
    centred = values_in - jnp.mean(values_in, axis=-1, keepdims=True)
    spread = jnp.mean(centred * centred, axis=-1, keepdims=True)
    return centred * lax.rsqrt(spread + epsilon) * norm_gain + norm_shift


def matmul(left_side, right_side):
    return jnp.dot(left_side, right_side, preferred_element_type=jnp.float32)


def matmul_nt(left_side, right_side):
    return lax.dot_general(
        left_side, right_side, (((1,), (1,)), ((), ())), preferred_element_type=jnp.float32
    )


def matmul_tn(left_side, right_side):
    return lax.dot_general(
        left_side, right_side, (((0,), (0,)), ((), ())), preferred_element_type=jnp.float32
    )


def fetch_attention(w_query, w_key, w_value, w_proj):
    return (
        lax.all_gather(w_query, "dp", axis=0, tiled=True),
        lax.all_gather(w_key, "dp", axis=0, tiled=True),
        lax.all_gather(w_value, "dp", axis=0, tiled=True),
        lax.all_gather(w_proj, "dp", axis=1, tiled=True),
    )


def fetch_inner(w_inner, w_outer):
    return (
        lax.all_gather(w_inner, "dp", axis=0, tiled=True),
        lax.all_gather(w_outer, "dp", axis=1, tiled=True),
    )


def masked_scores(query_heads, key_heads, allowed):
    scores = jnp.einsum("qhd,khd->hqk", query_heads, key_heads, preferred_element_type=jnp.float32)
    return jnp.where(allowed[None], scores, masked_fill)


def spread_into(shard_part, whole_width, offset):
    return lax.dynamic_update_slice_in_dim(
        jnp.zeros((whole_width,), jnp.float32), shard_part, offset, 0
    )


def on_device(
    tokens,
    key_mask,
    seq_lengths,
    w_query,
    b_query,
    w_key,
    w_value,
    b_value,
    w_proj,
    b_proj,
    gain_attn,
    shift_attn,
    w_inner,
    b_inner,
    w_outer,
    b_outer,
    gain_ffn,
    shift_ffn,
    out_grad,
):
    tensor_count = lax.axis_size("tensor")
    tensor_rank = lax.axis_index("tensor")
    piece_rows = tokens.shape[0]
    group_rows = piece_rows * tensor_count
    slot_count = seq_lengths.shape[1]
    model_width = tokens.shape[1]
    head_width = b_query.shape[0]
    local_heads = head_width // HEAD_DIM
    inner_width = b_inner.shape[0]
    head_scale = HEAD_DIM ** (-0.5)
    places = jnp.arange(group_rows, dtype=jnp.int32)
    slot_ends = jnp.cumsum(seq_lengths[0])
    segment = jnp.sum((places[:, None] >= slot_ends[None, :]).astype(jnp.int32), axis=1)
    allowed = (segment[:, None] == segment[None, :]) & (
        (key_mask[None, :] == 1) | (places[:, None] == places[None, :])
    )
    valid_all = (segment < slot_count).astype(jnp.float32)
    valid_piece = lax.dynamic_slice_in_dim(valid_all, tensor_rank * piece_rows, piece_rows, 0)[
        :, None
    ]
    query_full, key_full, value_full, proj_full = fetch_attention(w_query, w_key, w_value, w_proj)
    token_rows = lax.all_gather(tokens, "tensor", axis=0, tiled=True)
    query_low = ((matmul(token_rows, query_full) + b_query) * head_scale).astype(jnp.bfloat16)
    key_low = matmul(token_rows, key_full).astype(jnp.bfloat16)
    value_low = (matmul(token_rows, value_full) + b_value).astype(jnp.bfloat16)
    query_heads = query_low.reshape(group_rows, local_heads, HEAD_DIM)
    key_heads = key_low.reshape(group_rows, local_heads, HEAD_DIM)
    value_heads = value_low.reshape(group_rows, local_heads, HEAD_DIM)
    scores = masked_scores(query_heads, key_heads, allowed)
    row_top = jnp.max(scores, axis=2, keepdims=True)
    weights = jnp.exp(scores - row_top)
    row_total = jnp.sum(weights, axis=2, keepdims=True)
    probs_low = (weights / row_total).astype(jnp.bfloat16)
    context = jnp.einsum("hqk,khd->qhd", probs_low, value_heads, preferred_element_type=jnp.float32)
    context = context.reshape(group_rows, head_width).astype(jnp.bfloat16)
    attended = (
        lax.psum_scatter(matmul(context, proj_full), "tensor", scatter_dimension=0, tiled=True)
        + b_proj
    )
    first_in = tokens.astype(jnp.float32) + attended
    first_norm = layer_norm(first_in, gain_attn, shift_attn)
    first_low = first_norm.astype(jnp.bfloat16)
    inner_full, outer_full = fetch_inner(w_inner, w_outer)
    norm_rows = lax.all_gather(first_low, "tensor", axis=0, tiled=True)
    hidden = matmul(norm_rows, inner_full) + b_inner
    active_low = jax.nn.gelu(hidden, approximate=False).astype(jnp.bfloat16)
    branch = (
        lax.psum_scatter(matmul(active_low, outer_full), "tensor", scatter_dimension=0, tiled=True)
        + b_outer
    )
    second_in = first_norm + branch
    second, second_pull = jax.vjp(layer_norm, second_in, gain_ffn, shift_ffn)
    layer_out = (second * valid_piece).astype(jnp.bfloat16)
    out_cot = out_grad.astype(jnp.float32) * valid_piece
    second_grad, dgain_ffn, dshift_ffn = second_pull(out_cot)
    branch_grad = second_grad.astype(jnp.bfloat16)
    db_outer = jnp.sum(branch_grad.astype(jnp.float32), axis=0)
    branch_rows = lax.all_gather(branch_grad, "tensor", axis=0, tiled=True)
    active_grad = matmul_nt(branch_rows, outer_full)
    dw_outer = matmul_tn(active_low, branch_rows)
    gelu_pull = jax.vjp(partial(jax.nn.gelu, approximate=False), hidden)[1]
    hidden_grad = gelu_pull(active_grad)[0].astype(jnp.bfloat16)
    db_inner = jnp.sum(hidden_grad.astype(jnp.float32), axis=0)
    dw_inner = matmul_tn(norm_rows, hidden_grad)
    norm_back = lax.psum_scatter(
        matmul_nt(hidden_grad, inner_full), "tensor", scatter_dimension=0, tiled=True
    )
    first_pull = jax.vjp(layer_norm, first_in, gain_attn, shift_attn)[1]
    mix_grad, dgain_attn, dshift_attn = first_pull(second_grad + norm_back)
    proj_grad = mix_grad.astype(jnp.bfloat16)
    db_proj = jnp.sum(proj_grad.astype(jnp.float32), axis=0)
    proj_rows = lax.all_gather(proj_grad, "tensor", axis=0, tiled=True)
    dw_proj = matmul_tn(context, proj_rows)
    context_grad = matmul_nt(proj_rows, proj_full).astype(jnp.bfloat16)
    context_heads = context_grad.reshape(group_rows, local_heads, HEAD_DIM)
    scores = masked_scores(query_heads, key_heads, allowed)
    probs_exact = jnp.exp(scores - row_top) / row_total
    probs_again = probs_exact.astype(jnp.bfloat16)
    prob_grad = jnp.einsum(
        "qhd,khd->hqk", context_heads, value_heads, preferred_element_type=jnp.float32
    )
    row_delta = jnp.sum(prob_grad * probs_exact, axis=2, keepdims=True)
    score_grad = (probs_exact * (prob_grad - row_delta)).astype(jnp.bfloat16)
    query_grad = jnp.einsum(
        "hqk,khd->qhd", score_grad, key_heads, preferred_element_type=jnp.float32
    )
    query_grad = (query_grad.astype(jnp.bfloat16) * head_scale).reshape(group_rows, head_width)
    key_grad = jnp.einsum(
        "hqk,qhd->khd", score_grad, query_heads, preferred_element_type=jnp.float32
    )
    key_grad = key_grad.astype(jnp.bfloat16).reshape(group_rows, head_width)
    value_grad = jnp.einsum(
        "hqk,qhd->khd", probs_again, context_heads, preferred_element_type=jnp.float32
    )
    value_grad = value_grad.astype(jnp.bfloat16).reshape(group_rows, head_width)
    dw_query = matmul_tn(token_rows, query_grad)
    db_query = jnp.sum(query_grad.astype(jnp.float32), axis=0)
    dw_key = matmul_tn(token_rows, key_grad)
    dw_value = matmul_tn(token_rows, value_grad)
    db_value = jnp.sum(value_grad.astype(jnp.float32), axis=0)
    token_back = lax.psum_scatter(
        (
            matmul_nt(query_grad, query_full)
            + matmul_nt(key_grad, key_full)
            + matmul_nt(value_grad, value_full)
        ).astype(jnp.bfloat16),
        "tensor",
        scatter_dimension=0,
        tiled=True,
    ).astype(jnp.float32)
    tokens_grad = mix_grad + token_back
    dw_query_s, dw_key_s, dw_value_s, dw_proj_s, dw_inner_s, dw_outer_s = (
        lax.psum_scatter(dw_query, "dp", scatter_dimension=0, tiled=True),
        lax.psum_scatter(dw_key, "dp", scatter_dimension=0, tiled=True),
        lax.psum_scatter(dw_value, "dp", scatter_dimension=0, tiled=True),
        lax.psum_scatter(dw_proj, "dp", scatter_dimension=1, tiled=True),
        lax.psum_scatter(dw_inner, "dp", scatter_dimension=0, tiled=True),
        lax.psum_scatter(dw_outer, "dp", scatter_dimension=1, tiled=True),
    )
    head_offset = tensor_rank * head_width
    inner_offset = tensor_rank * inner_width
    inner_whole = inner_width * tensor_count
    summed = lax.psum(
        (
            spread_into(db_query, model_width, head_offset),
            spread_into(db_value, model_width, head_offset),
            spread_into(db_inner, inner_whole, inner_offset),
            db_proj,
            dgain_attn,
            dshift_attn,
            db_outer,
            dgain_ffn,
            dshift_ffn,
        ),
        ("dp", "tensor"),
    )
    db_query_s = lax.dynamic_slice_in_dim(summed[0], head_offset, head_width, 0)
    db_value_s = lax.dynamic_slice_in_dim(summed[1], head_offset, head_width, 0)
    db_inner_s = lax.dynamic_slice_in_dim(summed[2], inner_offset, inner_width, 0)
    return (
        layer_out,
        tokens_grad,
        dw_query_s,
        db_query_s,
        dw_key_s,
        dw_value_s,
        db_value_s,
        dw_proj_s,
        summed[3],
        summed[4],
        summed[5],
        dw_inner_s,
        db_inner_s,
        dw_outer_s,
        summed[6],
        summed[7],
        summed[8],
    )


def solution(mesh):
    in_specs = (
        P(("dp", "tensor"), None),
        P("dp"),
        P("dp", None),
        P("dp", "tensor"),
        P("tensor"),
        P("dp", "tensor"),
        P("dp", "tensor"),
        P("tensor"),
        P("tensor", "dp"),
        P(),
        P(),
        P(),
        P("dp", "tensor"),
        P("tensor"),
        P("tensor", "dp"),
        P(),
        P(),
        P(),
        P(("dp", "tensor"), None),
    )
    out_specs = (
        P(("dp", "tensor"), None),
        P(("dp", "tensor"), None),
        P("dp", "tensor"),
        P("tensor"),
        P("dp", "tensor"),
        P("dp", "tensor"),
        P("tensor"),
        P("tensor", "dp"),
        P(),
        P(),
        P(),
        P("dp", "tensor"),
        P("tensor"),
        P("tensor", "dp"),
        P(),
        P(),
        P(),
    )
    return jax.shard_map(
        on_device, mesh=mesh, in_specs=in_specs, out_specs=out_specs, check_vma=False
    )
```

profile of v0, /device:TPU:0, one launch (start us, length us, event | category | flops | bytes accessed | tf_op | source)
XLA Modules:
  0.0 873.4 jit_solution(14960254211893639935)
XLA Ops:
  10.4 33.4 %all_gather.31 = bf16[1024,256]{1,0:T(8,128)(2,1)S(1)} all-gather(bf16[128,256]{1,0:T(8,128)(2,1)} %param.25), channel_id=1, replica_groups=mesh['dp'=8,'tensor'=4] {'dp'}, dimensions={0}, use_global_device_ids=true | all-gather | bytes 589824 | tf_op jit(solution)/shard_map/all_gather | solution.py:41
  43.8 31.5 %all_gather.32 = bf16[1024,256]{1,0:T(8,128)(2,1)S(1)} all-gather(bf16[128,256]{1,0:T(8,128)(2,1)} %param.22), channel_id=1, replica_groups=mesh['dp'=8,'tensor'=4] {'dp'}, dimensions={0}, use_global_device_ids=true | all-gather | bytes 589824 | tf_op jit(solution)/shard_map/all_gather | solution.py:39
  75.3 31.9 %all_gather.33 = bf16[1024,256]{1,0:T(8,128)(2,1)S(1)} all-gather(bf16[128,256]{1,0:T(8,128)(2,1)} %param.24), channel_id=1, replica_groups=mesh['dp'=8,'tensor'=4] {'dp'}, dimensions={0}, use_global_device_ids=true | all-gather | bytes 589824 | tf_op jit(solution)/shard_map/all_gather | solution.py:40
  107.2 27.3 %all_gather.34 = bf16[256,1024]{1,0:T(8,128)(2,1)S(1)} all-gather(bf16[256,128]{1,0:T(8,128)(2,1)} %param.27), channel_id=1, replica_groups=mesh['dp'=8,'tensor'=4] {'dp'}, dimensions={1}, use_global_device_ids=true | all-gather | bytes 589824 | tf_op jit(solution)/shard_map/all_gather | solution.py:42
  136.5 1.8 fusion.14
  138.4 3.6 fusion.33
  142.5 2.8 convolution_convert_fusion.4
  145.3 1.8 fusion.34
  147.8 30.0 %reduce-scatter.11.cloned.1.call-done = f32[128,1024]{1,0:T(8,128)} async-done(((f32[512,1024]{1,0:T(8,128)}), f32[128,1024]{1,0:T(8,128)}) %reduce-scatter.11.cloned.1.call-update) | async-done | bytes 524304 | tf_op jit(solution)/shard_map/reduce_scatter | solution.py:121
  180.8 17.7 %all-gather.11.cloned.1.call-done = bf16[1024,1024]{1,0:T(8,128)(2,1)} async-done(((bf16[128,1024]{1,0:T(8,128)(2,1)}), bf16[1024,1024]{1,0:T(8,128)(2,1)}) %all-gather.11.cloned.1.call-update) | async-done | bytes 2097168 | tf_op jit(solution)/shard_map/all_gather | solution.py:48
  198.4 17.2 %all-gather.9.cloned.1.call-done = bf16[512,1024]{1,0:T(8,128)(2,1)} async-done(((bf16[128,1024]{1,0:T(8,128)(2,1)}), bf16[512,1024]{1,0:T(8,128)(2,1)}) %all-gather.9.cloned.1.call-update) | async-done | bytes 1048592 | tf_op jit(solution)/shard_map/all_gather | solution.py:128
  215.6 8.5 multiply_convert_fusion.1
  224.1 44.2 %all-gather.13.cloned.1.call-done = bf16[1024,1024]{1,0:T(8,128)(2,1)} async-done(((bf16[1024,128]{1,0:T(8,128)(2,1)}), bf16[1024,1024]{1,0:T(8,128)(2,1)}) %all-gather.13.cloned.1.call-update) | async-done | bytes 2097168 | tf_op jit(solution)/shard_map/all_gather | solution.py:49
  268.3 4.2 fusion.35
  272.7 29.6 %reduce-scatter.13.cloned.1.call-done = f32[128,1024]{1,0:T(8,128)} async-done(((f32[512,1024]{1,0:T(8,128)}), f32[128,1024]{1,0:T(8,128)}) %reduce-scatter.13.cloned.1.call-update) | async-done | bytes 524304 | tf_op jit(solution)/shard_map/reduce_scatter | solution.py:132
  306.2 16.5 %all-gather.15.cloned.1.call-done = bf16[512,1024]{1,0:T(8,128)(2,1)} async-done(((bf16[128,1024]{1,0:T(8,128)(2,1)}), bf16[512,1024]{1,0:T(8,128)(2,1)}) %all-gather.15.cloned.1.call-update) | async-done | bytes 1048592 | tf_op jit(solution)/shard_map/all_gather | solution.py:142
  322.7 5.2 convert_reduce_fusion
  328.9 2.6 fusion.36
  331.6 31.5 %reduce-scatter.15.cloned.1.call-done = f32[128,1024]{1,0:T(8,128)} async-done(((f32[512,1024]{1,0:T(8,128)}), f32[128,1024]{1,0:T(8,128)}) %reduce-scatter.15.cloned.1.call-update) | async-done | bytes 524304 | tf_op jit(solution)/shard_map/reduce_scatter | solution.py:149
  365.7 16.6 %all-gather.17.cloned.1.call-done = bf16[512,1024]{1,0:T(8,128)(2,1)} async-done(((bf16[128,1024]{1,0:T(8,128)(2,1)}), bf16[512,1024]{1,0:T(8,128)(2,1)}) %all-gather.17.cloned.1.call-update) | async-done | bytes 1048592 | tf_op jit(solution)/shard_map/all_gather | solution.py:156
  384.1 3.1 multiply_reduce_fusion
  394.9 3.0 convert_reduce_fusion.3
  404.6 4.5 fusion.40
  410.6 3.3 fusion.41
  414.8 40.8 %all-reduce = (f32[1024]{0:T(1024)S(1)}, f32[1024]{0:T(1024)S(1)}, f32[1024]{0:T(1024)}, f32[1024]{0:T(1024)}, f32[1024]{0:T(1024)}, /*index=5*/f32[4096]{0:T(10...) all-reduce(f32[1024]{0:T(1024)S(1)} %dynamic_update_slice.9, ...), channel_id=1, replica_groups=mesh['dp'=8,'tensor'=4] {'dp','tensor'}, use_global_device_ids=true, to_apply=%region_19.20 | all-reduce | flops 12288 | bytes 98304 | tf_op jit(solution)/shard_map/psum | solution.py:207
  459.1 62.2 %reduce-scatter.21.cloned.1.call-done = f32[128,256]{0,1:T(8,128)} async-done(((f32[1024,256]{0,1:T(8,128)}), f32[128,256]{0,1:T(8,128)}) %reduce-scatter.21.cloned.1.call-update) | async-done | bytes 131088 | tf_op jit(solution)/shard_map/reduce_scatter | solution.py:198
  523.0 65.1 %reduce-scatter.23.cloned.1.call-done = f32[128,256]{0,1:T(8,128)} async-done(((f32[1024,256]{0,1:T(8,128)}), f32[128,256]{0,1:T(8,128)}) %reduce-scatter.23.cloned.1.call-update) | async-done | bytes 131088 | tf_op jit(solution)/shard_map/reduce_scatter | solution.py:199
  589.7 24.6 %reduce-scatter.17.cloned.1.call-done = bf16[128,1024]{1,0:T(8,128)(2,1)} async-done(((bf16[512,1024]{1,0:T(8,128)(2,1)}), bf16[128,1024]{1,0:T(8,128)(2,1)}) %reduce-scatter.17.cloned.1.call-update) | async-done | bytes 262160 | tf_op jit(solution)/shard_map/reduce_scatter | solution.py:185
  614.3 1.9 convert_add_fusion
  616.2 66.6 %reduce-scatter.25.cloned.1.call-done = f32[256,128]{1,0:T(8,128)} async-done(((f32[256,1024]{1,0:T(8,128)}), f32[256,128]{1,0:T(8,128)}) %reduce-scatter.25.cloned.1.call-update) | async-done | bytes 131088 | tf_op jit(solution)/shard_map/reduce_scatter | solution.py:200
  682.7 91.0 %reduce-scatter.27.cloned.1.call-done = f32[128,1024]{1,0:T(8,128)} async-done(((f32[1024,1024]{1,0:T(8,128)}), f32[128,1024]{1,0:T(8,128)}) %reduce-scatter.27.cloned.1.call-update) | async-done | bytes 524304 | tf_op jit(solution)/shard_map/reduce_scatter | solution.py:201
  773.7 92.6 %reduce-scatter.29.cloned.1.call-done = f32[1024,128]{1,0:T(8,128)} async-done(((f32[1024,1024]{1,0:T(8,128)}), f32[1024,128]{1,0:T(8,128)}) %reduce-scatter.29.cloned.1.call-update) | async-done | bytes 524304 | tf_op jit(solution)/shard_map/reduce_scatter | solution.py:202
  (164 shorter events, 41.2 us)
Async XLA Ops:
  8.0 126.8 %all-gather.7.cloned.1.call-start = ((), (), s32[]{:S(2)}) async-start(), calls=%async_computation.10 | async-start | bytes 1310720 | tf_op jit(solution)/shard_map/all_gather | solution.py:106
  8.8 169.1 %reduce-scatter.11.cloned.1.call-start = ((), (), s32[]{:S(2)}) async-start(), calls=%async_computation.11 | async-start | bytes 2621440 | tf_op jit(solution)/shard_map/reduce_scatter | solution.py:121
  10.4 126.1 %copy-start.33 = (f32[256]{0:T(256)S(1)}, f32[256]{0:T(256)}, u32[]{:S(2)}) copy-start(f32[256]{0:T(256)} %param.23) | copy-start | bytes 3076
  43.8 98.2 %copy-start.8 = (bf16[1024,256]{1,0:T(8,128)(2,1)}, bf16[1024,256]{1,0:T(8,128)(2,1)S(1)}, u32[]{:S(2)}) copy-start(bf16[1024,256]{1,0:T(8,128)(2,1)S(1)} %all_gather.31) | copy-start | bytes 1572868
  75.3 63.0 %copy-start.10 = (bf16[1024,256]{1,0:T(8,128)(2,1)}, bf16[1024,256]{1,0:T(8,128)(2,1)S(1)}, u32[]{:S(2)}) copy-start(bf16[1024,256]{1,0:T(8,128)(2,1)S(1)} %all_gather.32) | copy-start | bytes 1572868
  107.2 31.1 %copy-start.3 = (bf16[1024,256]{1,0:T(8,128)(2,1)}, bf16[1024,256]{1,0:T(8,128)(2,1)S(1)}, u32[]{:S(2)}) copy-start(bf16[1024,256]{1,0:T(8,128)(2,1)S(1)} %all_gather.33) | copy-start | bytes 1572868
  145.3 32.5 %copy-start.17 = (bf16[128,1024]{1,0:T(8,128)(2,1)S(1)}, bf16[128,1024]{1,0:T(8,128)(2,1)}, u32[]{:S(2)}) copy-start(bf16[128,1024]{1,0:T(8,128)(2,1)} %param.19) | copy-start | bytes 786436
  145.3 32.5 %copy-start.28 = (f32[1024]{0:T(1024)S(1)}, f32[1024]{0:T(1024)}, u32[]{:S(2)}) copy-start(f32[1024]{0:T(1024)} %param.28) | copy-start | bytes 12292
  147.1 32.1 %copy-start.25 = (f32[1024]{0:T(1024)S(1)}, f32[1024]{0:T(1024)}, u32[]{:S(2)}) copy-start(f32[1024]{0:T(1024)} %param.29) | copy-start | bytes 12292
  147.1 32.1 %copy-start.26 = (f32[1024]{0:T(1024)S(1)}, f32[1024]{0:T(1024)}, u32[]{:S(2)}) copy-start(f32[1024]{0:T(1024)} %param.30) | copy-start | bytes 12292
  147.2 68.4 %copy-start.32 = (f32[1024]{0:T(1024)S(1)}, f32[1024]{0:T(1024)}, u32[]{:S(2)}) copy-start(f32[1024]{0:T(1024)} %param.32) | copy-start | bytes 12292
  147.2 51.3 %all-gather.11.cloned.1.call-start = ((), (), s32[]{:S(2)}) async-start(), calls=%async_computation.13 | async-start | bytes 2359296 | tf_op jit(solution)/shard_map/all_gather | solution.py:48
  147.8 67.8 %all-gather.9.cloned.1.call-start = ((), (), s32[]{:S(2)}) async-start(), calls=%async_computation.12 | async-start | bytes 1310720 | tf_op jit(solution)/shard_map/all_gather | solution.py:128
  180.2 88.1 %all-gather.13.cloned.1.call-start = ((), (), s32[]{:S(2)}) async-start(), calls=%async_computation.14 | async-start | bytes 2359296 | tf_op jit(solution)/shard_map/all_gather | solution.py:49
  180.7 121.5 %reduce-scatter.13.cloned.1.call-start = ((), (), s32[]{:S(2)}) async-start(), calls=%async_computation.15 | async-start | bytes 2621440 | tf_op jit(solution)/shard_map/reduce_scatter | solution.py:132
  224.1 48.3 %copy-start.13 = (bf16[512,1024]{1,0:T(8,128)(2,1)}, bf16[512,1024]{1,0:T(8,128)(2,1)S(1)}, u32[]{:S(2)}) copy-start(bf16[512,1024]{1,0:T(8,128)(2,1)S(1)} %get-tuple-element.79) | copy-start | bytes 3145732
  272.5 29.8 %copy-start.29 = (f32[1024]{0:T(1024)S(1)}, f32[1024]{0:T(1024)}, u32[]{:S(2)}) copy-start(f32[1024]{0:T(1024)} %param.34) | copy-start | bytes 12292
  272.5 31.3 %copy-start.19 = (bf16[128,1024]{1,0:T(8,128)(2,1)S(1)}, bf16[128,1024]{1,0:T(8,128)(2,1)}, u32[]{:S(2)}) copy-start(bf16[128,1024]{1,0:T(8,128)(2,1)} %param.37) | copy-start | bytes 786436
  272.5 31.3 %copy-start.27 = (f32[1024]{0:T(1024)S(1)}, f32[1024]{0:T(1024)}, u32[]{:S(2)}) copy-start(f32[1024]{0:T(1024)} %param.35) | copy-start | bytes 12292
  272.5 31.7 %copy-start.30 = (f32[1024]{0:T(1024)S(1)}, f32[1024]{0:T(1024)}, u32[]{:S(2)}) copy-start(f32[1024]{0:T(1024)} %param.36) | copy-start | bytes 12292
  272.5 50.2 %all-gather.15.cloned.1.call-start = ((), (), s32[]{:S(2)}) async-start(), calls=%async_computation.16 | async-start | bytes 1310720 | tf_op jit(solution)/shard_map/all_gather | solution.py:142
  306.0 57.1 %reduce-scatter.15.cloned.1.call-start = ((), (), s32[]{:S(2)}) async-start(), calls=%async_computation.17 | async-start | bytes 2621440 | tf_op jit(solution)/shard_map/reduce_scatter | solution.py:149
  331.6 50.8 %all-gather.17.cloned.1.call-start = ((), (), s32[]{:S(2)}) async-start(), calls=%async_computation.18 | async-start | bytes 1310720 | tf_op jit(solution)/shard_map/all_gather | solution.py:156
  364.8 22.4 %copy-start.1 = (f32[128,1024]{1,0:T(8,128)}, f32[128,1024]{1,0:T(8,128)S(1)}, u32[]{:S(2)}) copy-start(f32[128,1024]{1,0:T(8,128)S(1)} %get-tuple-element.73) | copy-start | bytes 1572868
  365.7 91.8 %reduce-scatter.19.cloned.1.call-start = ((), (), s32[]{:S(2)}) async-start(), calls=%async_computation.20 | async-start | bytes 1179648 | tf_op jit(solution)/shard_map/reduce_scatter | solution.py:197
  390.9 130.4 %reduce-scatter.21.cloned.1.call-start = ((), (), s32[]{:S(2)}) async-start(), calls=%async_computation.21 | async-start | bytes 1179648 | tf_op jit(solution)/shard_map/reduce_scatter | solution.py:198
  394.8 193.3 %reduce-scatter.23.cloned.1.call-start = ((), (), s32[]{:S(2)}) async-start(), calls=%async_computation.22 | async-start | bytes 1179648 | tf_op jit(solution)/shard_map/reduce_scatter | solution.py:199
  399.4 214.9 %reduce-scatter.17.cloned.1.call-start = ((), (), s32[]{:S(2)}) async-start(), calls=%async_computation.19 | async-start | bytes 1310720 | tf_op jit(solution)/shard_map/reduce_scatter | solution.py:185
  403.0 279.7 %reduce-scatter.25.cloned.1.call-start = ((), (), s32[]{:S(2)}) async-start(), calls=%async_computation.23 | async-start | bytes 1179648 | tf_op jit(solution)/shard_map/reduce_scatter | solution.py:200
  404.5 369.2 %reduce-scatter.27.cloned.1.call-start = ((), (), s32[]{:S(2)}) async-start(), calls=%async_computation.24 | async-start | bytes 4718592 | tf_op jit(solution)/shard_map/reduce_scatter | solution.py:201
  409.1 457.2 %reduce-scatter.29.cloned.1.call-start = ((), (), s32[]{:S(2)}) async-start(), calls=%async_computation.25 | async-start | bytes 4718592 | tf_op jit(solution)/shard_map/reduce_scatter | solution.py:202
  413.9 200.4 %copy-start.2 = (f32[128,1024]{1,0:T(8,128)S(1)}, f32[128,1024]{1,0:T(8,128)}, u32[]{:S(2)}) copy-start(f32[128,1024]{1,0:T(8,128)} %copy-done.1) | copy-start | bytes 1572868
  (23 other events, 70.8 us)
Sparse Core Ops, SparseCore 0:
  10.4 19.4 all-gather.6
  147.3 30.5 reduce-scatter.10
  272.6 29.5 reduce-scatter.12
  331.7 31.4 reduce-scatter.14
Sparse Core Ops, SparseCore 1:
  150.0 48.4 all-gather.10
  200.5 15.0 all-gather.8
  217.7 50.5 all-gather.12
  306.1 16.5 all-gather.14
  365.8 16.5 all-gather.16
  391.0 64.0 reduce-scatter.18
  458.3 63.0 reduce-scatter.20
  525.0 63.0 reduce-scatter.22
  590.4 23.8 reduce-scatter.16
  618.7 64.0 reduce-scatter.24
  686.8 86.8 reduce-scatter.26
  778.3 87.8 reduce-scatter.28
where the time goes:
time: 874 us; the launch traced here: 873 us
  waiting for transfers between devices  607 us (69%)
  blocking collectives  165 us (19%)
  matrix products  58.7 us (7%)
  between operations  15.9 us (2%)
  other arithmetic  13.4 us (2%)
  local copies, waits for them, and re-layouts  12.3 us (1%)
    reduce_scatter x1, waiting for transfers between devices, on_device(): lax.psum_scatter(dw_outer, 'dp', scatter_dimension=1, tiled=True)  92.6 us
    reduce_scatter x1, waiting for transfers between devices, on_device(): lax.psum_scatter(dw_inner, 'dp', scatter_dimension=0, tiled=True)  91 us
    reduce_scatter x1, waiting for transfers between devices, on_device(): lax.psum_scatter(dw_proj, 'dp', scatter_dimension=1, tiled=True)  66.6 us
    reduce_scatter x1, waiting for transfers between devices, on_device(): lax.psum_scatter(dw_value, 'dp', scatter_dimension=0, tiled=True)  65.1 us
    reduce_scatter x1, waiting for transfers between devices, on_device(): lax.psum_scatter(dw_key, 'dp', scatter_dimension=0, tiled=True)  62.2 us
    all_gather x1, waiting for transfers between devices, fetch_inner(): lax.all_gather(w_outer, 'dp', axis=1, tiled=True)  44.2 us
    psum x1, blocking collectives, on_device(): lax.psum((spread_into(db_query, model_width, head_offset), spread_into(db...  40.8 us
    all_gather x1, blocking collectives, fetch_attention(): lax.all_gather(w_value, 'dp', axis=0, tiled=True)  33.4 us
  transfers between devices with their start and end apart: 16, of which 14 were waited for; matrix products, arithmetic and copies ran while one was open for 5% of the time, Pallas kernels for 0%

commit v1 on v0

v1 whole, which is shorter than its diff:
```python
from functools import partial

import jax
import jax.numpy as jnp
from jax import lax
from jax.sharding import PartitionSpec as P

HEAD_DIM = 64


epsilon = 1e-12
masked_fill = -1e30


def layer_norm(values_in, norm_gain, norm_shift):
    centred = values_in - jnp.mean(values_in, axis=-1, keepdims=True)
    spread = jnp.mean(centred * centred, axis=-1, keepdims=True)
    return centred * lax.rsqrt(spread + epsilon) * norm_gain + norm_shift


def matmul(left_side, right_side):
    return jnp.dot(left_side, right_side, preferred_element_type=jnp.float32)


def matmul_nt(left_side, right_side):
    return lax.dot_general(
        left_side, right_side, (((1,), (1,)), ((), ())), preferred_element_type=jnp.float32
    )


def matmul_tn(left_side, right_side):
    return lax.dot_general(
        left_side, right_side, (((0,), (0,)), ((), ())), preferred_element_type=jnp.float32
    )


def swap(block, axis_name, offset):
    count = lax.axis_size(axis_name)
    return lax.ppermute(block, axis_name, [(i, i ^ offset) for i in range(count)])


def after(blocks, marks):
    return lax.optimization_barrier((blocks, marks))[0]


def gather_rows(piece):
    across = swap(piece, "tensor", 2)
    beside = swap(piece, "tensor", 1)
    corner = swap(across, "tensor", 1)
    return jnp.concatenate([piece, beside, across, corner], axis=0)


def scatter_rows(partial_sums):
    rows = partial_sums.shape[0] // 4
    own, beside, across, corner = (partial_sums[k * rows : (k + 1) * rows] for k in range(4))
    far = across + swap(corner.astype(jnp.bfloat16), "tensor", 1).astype(jnp.float32)
    near = own + swap(beside.astype(jnp.bfloat16), "tensor", 1).astype(jnp.float32)
    return near + swap(far.astype(jnp.bfloat16), "tensor", 2).astype(jnp.float32)


def sum_rows_ranks(vector):
    vector = vector + swap(vector, "tensor", 1)
    return vector + swap(vector, "tensor", 2)


def stage_offsets(count):
    bits = count.bit_length() - 1
    stages, bit = [], 1
    while bit < bits:
        width = min(2, bits - bit)
        stages.append([k << bit for k in range(1, 1 << width)])
        bit += width
    return stages


def slot_order(count):
    return list(range(0, count, 2)) + list(range(1, count, 2))


def gather_even(shard):
    held = [([0], shard)]
    for stage in stage_offsets(lax.axis_size("dp")):
        offsets = [o for some, _ in held for o in some]
        block = held[0][1] if len(held) == 1 else jnp.concatenate([b for _, b in held], axis=0)
        for offset in stage:
            held.append(([o ^ offset for o in offsets], swap(block, "dp", offset)))
    return held


def gather_odd(held):
    return [([o ^ 1 for o in offsets], swap(block, "dp", 1)) for offsets, block in held]


def whole_of(even, odd):
    return jnp.concatenate([block for _, block in even + odd], axis=0)


def scatter_shards(partial_sums):
    half = partial_sums.shape[0] // 2
    sums = partial_sums[:half] + swap(
        partial_sums[half:].astype(jnp.bfloat16), "dp", 1
    ).astype(jnp.float32)
    for stage in reversed(stage_offsets(lax.axis_size("dp"))):
        rows = sums.shape[0] // (len(stage) + 1)
        kept = sums[:rows]
        for place, offset in enumerate(stage, 1):
            piece = sums[place * rows : (place + 1) * rows].astype(jnp.bfloat16)
            kept = kept + swap(piece, "dp", offset).astype(jnp.float32)
        sums = kept
    return sums


def sum_dp_ranks(vector):
    offset = 1
    while offset < lax.axis_size("dp"):
        vector = vector + swap(vector, "dp", offset)
        offset *= 2
    return vector


def to_slots(array):
    count, rank = lax.axis_size("dp"), lax.axis_index("dp")
    width = array.shape[-1] // count
    return jnp.concatenate(
        [
            lax.dynamic_slice_in_dim(array, (rank ^ o) * width, width, array.ndim - 1)
            for o in slot_order(count)
        ],
        axis=-1,
    )


def from_slots(array):
    count, rank = lax.axis_size("dp"), lax.axis_index("dp")
    width = array.shape[-1] // count
    pieces = []
    for block in range(count):
        offset = rank ^ block
        place = offset // 2 + (count // 2) * (offset % 2)
        pieces.append(lax.dynamic_slice_in_dim(array, place * width, width, array.ndim - 1))
    return jnp.concatenate(pieces, axis=-1)


def masked_scores(query_heads, key_heads, allowed):
    scores = jnp.einsum("qhd,khd->hqk", query_heads, key_heads, preferred_element_type=jnp.float32)
    return jnp.where(allowed[None], scores, masked_fill)


def on_device(
    tokens,
    key_mask,
    seq_lengths,
    w_query,
    b_query,
    w_key,
    w_value,
    b_value,
    w_proj,
    b_proj,
    gain_attn,
    shift_attn,
    w_inner,
    b_inner,
    w_outer,
    b_outer,
    gain_ffn,
    shift_ffn,
    out_grad,
):
    tensor_count = lax.axis_size("tensor")
    tensor_rank = lax.axis_index("tensor")
    piece_rows = tokens.shape[0]
    group_rows = piece_rows * tensor_count
    slot_count = seq_lengths.shape[1]
    head_width = b_query.shape[0]
    local_heads = head_width // HEAD_DIM
    inner_width = b_inner.shape[0]
    head_scale = HEAD_DIM ** (-0.5)

    qkv_even = gather_even(jnp.concatenate([w_query, w_key, w_value], axis=1))
    tokens = to_slots(tokens)
    token_rows = gather_rows(tokens)
    qkv_odd = gather_odd(qkv_even)
    qkv_full = whole_of(qkv_even, qkv_odd)
    ffn_shards = jnp.concatenate([w_proj.T, w_inner, w_outer.T], axis=1)
    ffn_even = gather_even(after(ffn_shards, [block for _, block in qkv_even]))
    ffn_odd = gather_odd(ffn_even)
    ffn_full = whole_of(ffn_even, ffn_odd)
    proj_full_t = ffn_full[:, :head_width]
    inner_full = ffn_full[:, head_width : head_width + inner_width]
    outer_full_t = ffn_full[:, head_width + inner_width :]

    out_grad = to_slots(out_grad)
    small = to_slots(jnp.stack([b_proj, gain_attn, shift_attn, b_outer, gain_ffn, shift_ffn]))
    b_proj, gain_attn, shift_attn, b_outer, gain_ffn, shift_ffn = (small[k] for k in range(6))

    steps = jnp.arange(piece_rows, dtype=jnp.int32)
    places = jnp.concatenate([(tensor_rank ^ k) * piece_rows + steps for k in range(tensor_count)])
    key_rows = jnp.concatenate(
        [
            lax.dynamic_slice_in_dim(key_mask, (tensor_rank ^ k) * piece_rows, piece_rows, 0)
            for k in range(tensor_count)
        ]
    )
    slot_ends = jnp.cumsum(seq_lengths[0])
    segment = jnp.sum((places[:, None] >= slot_ends[None, :]).astype(jnp.int32), axis=1)
    allowed = (segment[:, None] == segment[None, :]) & (
        (key_rows[None, :] == 1) | (places[:, None] == places[None, :])
    )
    valid_piece = (segment[:piece_rows] < slot_count).astype(jnp.float32)[:, None]

    qkv = matmul(token_rows, qkv_full)
    query_low = ((qkv[:, :head_width] + b_query) * head_scale).astype(jnp.bfloat16)
    key_low = qkv[:, head_width : 2 * head_width].astype(jnp.bfloat16)
    value_low = (qkv[:, 2 * head_width :] + b_value).astype(jnp.bfloat16)
    query_heads = query_low.reshape(group_rows, local_heads, HEAD_DIM)
    key_heads = key_low.reshape(group_rows, local_heads, HEAD_DIM)
    value_heads = value_low.reshape(group_rows, local_heads, HEAD_DIM)
    scores = masked_scores(query_heads, key_heads, allowed)
    row_top = jnp.max(scores, axis=2, keepdims=True)
    weights = jnp.exp(scores - row_top)
    row_total = jnp.sum(weights, axis=2, keepdims=True)
    probs_low = (weights / row_total).astype(jnp.bfloat16)
    context = jnp.einsum("hqk,khd->qhd", probs_low, value_heads, preferred_element_type=jnp.float32)
    context = context.reshape(group_rows, head_width).astype(jnp.bfloat16)
    attended = scatter_rows(matmul_nt(context, proj_full_t)) + b_proj
    first_in = tokens.astype(jnp.float32) + attended
    first_norm = layer_norm(first_in, gain_attn, shift_attn)
    first_low = first_norm.astype(jnp.bfloat16)
    norm_rows = gather_rows(first_low)
    hidden = matmul(norm_rows, inner_full) + b_inner
    active_low = jax.nn.gelu(hidden, approximate=False).astype(jnp.bfloat16)
    branch = scatter_rows(matmul_nt(active_low, outer_full_t)) + b_outer
    second_in = first_norm + branch
    second, second_pull = jax.vjp(layer_norm, second_in, gain_ffn, shift_ffn)
    layer_out = from_slots((second * valid_piece).astype(jnp.bfloat16))
    out_cot = out_grad.astype(jnp.float32) * valid_piece
    second_grad, dgain_ffn, dshift_ffn = second_pull(out_cot)
    branch_grad = second_grad.astype(jnp.bfloat16)
    db_outer = jnp.sum(branch_grad.astype(jnp.float32), axis=0)
    branch_rows = gather_rows(branch_grad)
    active_grad = matmul(branch_rows, outer_full_t)
    gelu_pull = jax.vjp(partial(jax.nn.gelu, approximate=False), hidden)[1]
    hidden_grad = gelu_pull(active_grad)[0].astype(jnp.bfloat16)
    norm_back = scatter_rows(matmul_nt(hidden_grad, inner_full))
    dw_outer_t = scatter_shards(matmul_tn(branch_rows, active_low))
    dw_inner = scatter_shards(matmul_tn(norm_rows, hidden_grad))
    db_inner = jnp.sum(hidden_grad.astype(jnp.float32), axis=0)
    first_pull = jax.vjp(layer_norm, first_in, gain_attn, shift_attn)[1]
    mix_grad, dgain_attn, dshift_attn = first_pull(second_grad + norm_back)
    proj_grad = mix_grad.astype(jnp.bfloat16)
    db_proj = jnp.sum(proj_grad.astype(jnp.float32), axis=0)
    proj_rows = gather_rows(proj_grad)
    whole_sums = sum_rows_ranks(
        from_slots(jnp.stack([db_proj, dgain_attn, dshift_attn, db_outer, dgain_ffn, dshift_ffn]))
    )
    context_grad = matmul(proj_rows, proj_full_t).astype(jnp.bfloat16)
    dw_proj_t = scatter_shards(matmul_tn(proj_rows, context))
    context_heads = context_grad.reshape(group_rows, local_heads, HEAD_DIM)
    scores = masked_scores(query_heads, key_heads, allowed)
    probs_exact = jnp.exp(scores - row_top) / row_total
    probs_again = probs_exact.astype(jnp.bfloat16)
    prob_grad = jnp.einsum(
        "qhd,khd->hqk", context_heads, value_heads, preferred_element_type=jnp.float32
    )
    row_delta = jnp.sum(prob_grad * probs_exact, axis=2, keepdims=True)
    score_grad = (probs_exact * (prob_grad - row_delta)).astype(jnp.bfloat16)
    query_grad = jnp.einsum(
        "hqk,khd->qhd", score_grad, key_heads, preferred_element_type=jnp.float32
    )
    query_grad = (query_grad.astype(jnp.bfloat16) * head_scale).reshape(group_rows, head_width)
    key_grad = jnp.einsum(
        "hqk,qhd->khd", score_grad, query_heads, preferred_element_type=jnp.float32
    )
    key_grad = key_grad.astype(jnp.bfloat16).reshape(group_rows, head_width)
    value_grad = jnp.einsum(
        "hqk,qhd->khd", probs_again, context_heads, preferred_element_type=jnp.float32
    )
    value_grad = value_grad.astype(jnp.bfloat16).reshape(group_rows, head_width)
    qkv_grad = jnp.concatenate([query_grad, key_grad, value_grad], axis=1)
    dw_qkv = scatter_shards(matmul_tn(token_rows, qkv_grad))
    tokens_grad = from_slots(mix_grad + scatter_rows(matmul_nt(qkv_grad, qkv_full)))
    db_query = jnp.sum(query_grad.astype(jnp.float32), axis=0)
    db_value = jnp.sum(value_grad.astype(jnp.float32), axis=0)
    sums = sum_dp_ranks(jnp.concatenate([whole_sums.reshape(-1), db_inner, db_query, db_value]))
    whole_width = whole_sums.size
    shared = sums[:whole_width].reshape(whole_sums.shape)
    db_inner = sums[whole_width : whole_width + inner_width]
    db_query = sums[whole_width + inner_width : whole_width + inner_width + head_width]
    db_value = sums[whole_width + inner_width + head_width :]
    return (
        layer_out,
        tokens_grad,
        dw_qkv[:, :head_width],
        db_query,
        dw_qkv[:, head_width : 2 * head_width],
        dw_qkv[:, 2 * head_width :],
        db_value,
        dw_proj_t.T,
        shared[0],
        shared[1],
        shared[2],
        dw_inner,
        db_inner,
        dw_outer_t.T,
        shared[3],
        shared[4],
        shared[5],
    )


def solution(mesh):
    in_specs = (
        P(("dp", "tensor"), None),
        P("dp"),
        P("dp", None),
        P("dp", "tensor"),
        P("tensor"),
        P("dp", "tensor"),
        P("dp", "tensor"),
        P("tensor"),
        P("tensor", "dp"),
        P(),
        P(),
        P(),
        P("dp", "tensor"),
        P("tensor"),
        P("tensor", "dp"),
        P(),
        P(),
        P(),
        P(("dp", "tensor"), None),
    )
    out_specs = (
        P(("dp", "tensor"), None),
        P(("dp", "tensor"), None),
        P("dp", "tensor"),
        P("tensor"),
        P("dp", "tensor"),
        P("dp", "tensor"),
        P("tensor"),
        P("tensor", "dp"),
        P(),
        P(),
        P(),
        P("dp", "tensor"),
        P("tensor"),
        P("tensor", "dp"),
        P(),
        P(),
        P(),
    )
    return jax.shard_map(
        on_device, mesh=mesh, in_specs=in_specs, out_specs=out_specs, check_vma=False
    )
```

time: 874 us -> 308 us (0.35)
  waiting for transfers between devices: 607 us -> 142 us
  blocking collectives: 165 us -> 0 us
  starting transfers between devices: 1.08 us -> 58.8 us
  local copies, waits for them, and re-layouts: 12.3 us -> 36.8 us
  matrix products: 58.7 us -> 43.1 us
  between operations: 15.9 us -> 2.13 us
  other arithmetic: 13.4 us -> 23.3 us
    reduce_scatter x10 -> x0, waiting for transfers between devices: 493 us -> none  [the longest x1 92.6 us: on_device(): lax.psum_scatter(dw_outer, 'dp', scatter_dimension=1, tiled=True)]
    ppermute x0 -> x59, waiting for transfers between devices: none -> 142 us  [swap(): lax.ppermute(block, axis_name, [(i, i ^ offset) for i in range(count)])]
    all_gather x4 -> x0, blocking collectives: 124 us -> none  [the longest x1 33.4 us: fetch_attention(): lax.all_gather(w_value, 'dp', axis=0, tiled=True)]
    all_gather x6 -> x0, waiting for transfers between devices: 112 us -> none  [the longest x1 44.2 us: fetch_inner(): lax.all_gather(w_outer, 'dp', axis=1, tiled=True)]
    ppermute x0 -> x59, starting transfers between devices: none -> 58.8 us  [swap(): lax.ppermute(block, axis_name, [(i, i ^ offset) for i in range(count)])]
    psum x1 -> x0, blocking collectives: 40.8 us -> none  [on_device(): lax.psum((spread_into(db_query, model_width, head_offset), spread_into(db...]
    unnamed x81 -> x166, local copies, waits for them, and re-layouts: 9.51 us -> 24.1 us
    dot_general x6 -> x4, matrix products: 18.5 us -> 15.4 us  [matmul(): return jnp.dot(left_side, right_side, preferred_element_type=jnp.float32)]
  transfers between devices with their start and end apart: 16 -> 59, of which waited for: 14 -> 25; matrix products, arithmetic and copies ran while one was open for 5% -> 24% of each run, Pallas kernels for 0% -> 0%
where the time goes in v1:
time: 308 us; the launch traced here: 306 us
  waiting for transfers between devices  142 us (46%)
  starting transfers between devices  58.8 us (19%)
  matrix products  43.1 us (14%)
  local copies, waits for them, and re-layouts  36.8 us (12%)
  other arithmetic  23.3 us (8%)
    ppermute x59, waiting for transfers between devices, swap(): lax.ppermute(block, axis_name, [(i, i ^ offset) for i in range(count)])  142 us
    ppermute x59, starting transfers between devices, swap(): lax.ppermute(block, axis_name, [(i, i ^ offset) for i in range(count)])  58.8 us
    unnamed x166, local copies, waits for them, and re-layouts  24.1 us
    dot_general x4, matrix products, matmul(): return jnp.dot(left_side, right_side, preferred_element_type=jnp.float32)  15.4 us
    another operation x5, other arithmetic  8.85 us
    dot_general x4, matrix products, matmul_nt(): lax.dot_general(left_side, right_side, (((1,), (1,)), ((), ())), preferre...  8.47 us
    dot_general x4, matrix products, matmul_tn(): lax.dot_general(left_side, right_side, (((0,), (0,)), ((), ())), preferre...  6.75 us
  transfers between devices with their start and end apart: 59, of which 25 were waited for; matrix products, arithmetic and copies ran while one was open for 24% of the time, Pallas kernels for 0%

profile of v1, /device:TPU:0, one launch (start us, length us, event | category | flops | bytes accessed | tf_op | source)
XLA Modules:
  0.0 306.2 jit_solution(12681056054595143386)
XLA Ops:
  5.1 3.0 collective-permute-start.3
  8.2 2.6 collective-permute-start.4
  26.3 3.3 %collective-permute-start.10 = (bf16[128,2304]{0,1:T(8,128)(2,1)S(1)}, bf16[128,2304]{0,1:T(8,128)(2,1)S(1)}, u32[]{:S(2)}, u32[]{:S(2)}) collective-permute-start(bf16[128,2304]{0,1:T(8,128)(2,1)S(1)} %pad_maximum_fusion.5), channel_id=1, source_target_pairs={{0,8},{4,12},{8,0},{12,4},{16,24},{20,28},{24,16},{28,20},{1,9},{5... | collective-permute-start | bytes 1769480 | tf_op jit(solution)/shard_map/ppermute | solution.py:39
  33.4 4.1 %collective-permute-done.7 = bf16[128,768]{1,0:T(8,128)(2,1)S(1)} collective-permute-done((bf16[128,768]{1,0:T(8,128)(2,1)S(1)}, bf16[128,768]{1,0:T(8,128)(2,1)S(1)}, u32[]{:S(2)}, u32[]{:S(2)}) %collective-permute-start.7) | collective-permute-done | bytes 196640 | tf_op jit(solution)/shard_map/ppermute | solution.py:39
  37.5 3.7 %collective-permute-done.8 = bf16[128,768]{1,0:T(8,128)(2,1)S(1)} collective-permute-done((bf16[128,768]{1,0:T(8,128)(2,1)S(1)}, bf16[128,768]{1,0:T(8,128)(2,1)S(1)}, u32[]{:S(2)}, u32[]{:S(2)}) %collective-permute-start.8) | collective-permute-done | bytes 196640 | tf_op jit(solution)/shard_map/ppermute | solution.py:39
  50.8 4.6 %fusion.104 = (f32[4,512]{1,0:T(4,128)S(1)}, f32[4,512,512]{1,2,0:T(8,128)}) fusion(pred[512,512]{0,1:T(8,128)(4,1)} %or_and_fusion, bf16[512,4,64]{0,2,1:T(8,128)(2,1)S(1)} %bitcast.66, bf16[512,4,64]{0,2,1:T(8,128)(2,1)S(1)} %bitcast.64), kind=kOutput, calls=%fused_computation.266 | convolution fusion | flops 137363968 | bytes 4988928 | tf_op jit(solution)/shard_map/sub | solution.py:221
  55.4 2.7 convolution_convert_fusion.4
  58.7 22.9 %collective-permute-done.11 = bf16[128,2304]{0,1:T(8,128)(2,1)S(1)} collective-permute-done((bf16[128,2304]{0,1:T(8,128)(2,1)S(1)}, bf16[128,2304]{0,1:T(8,128)(2,1)S(1)}, u32[]{:S(2)}, u32[]{:S(2)}) %collective-permute-start.11) | collective-permute-done | bytes 589856 | tf_op jit(solution)/shard_map/ppermute | solution.py:39
  90.3 7.5 %collective-permute-done.15 = bf16[128,2304]{0,1:T(8,128)(2,1)S(1)} collective-permute-done((bf16[128,2304]{0,1:T(8,128)(2,1)S(1)}, bf16[128,2304]{0,1:T(8,128)(2,1)S(1)}, u32[]{:S(2)}, u32[]{:S(2)}) %collective-permute-start.15) | collective-permute-done | bytes 589856 | tf_op jit(solution)/shard_map/ppermute | solution.py:39
  98.8 6.9 %collective-permute-done.16 = bf16[128,2304]{0,1:T(8,128)(2,1)S(1)} collective-permute-done((bf16[128,2304]{0,1:T(8,128)(2,1)}, bf16[128,2304]{0,1:T(8,128)(2,1)S(1)}, u32[]{:S(2)}, u32[]{:S(2)}) %collective-permute-start.16) | collective-permute-done | bytes 589856 | tf_op jit(solution)/shard_map/ppermute | solution.py:39
  111.0 7.2 %collective-permute-done.19 = bf16[128,1024]{1,0:T(8,128)(2,1)S(1)} collective-permute-done((bf16[128,1024]{1,0:T(8,128)(2,1)S(1)}, bf16[128,1024]{1,0:T(8,128)(2,1)S(1)}, u32[]{:S(2)}, u32[]{:S(2)}) %collective-permute-start.19) | collective-permute-done | bytes 262176 | tf_op jit(solution)/shard_map/ppermute | solution.py:39
  120.0 6.4 %collective-permute-done.21 = bf16[128,1024]{1,0:T(8,128)(2,1)S(1)} collective-permute-done((bf16[128,1024]{1,0:T(8,128)(2,1)S(1)}, bf16[128,1024]{1,0:T(8,128)(2,1)S(1)}, u32[]{:S(2)}, u32[]{:S(2)}) %collective-permute-start.21) | collective-permute-done | bytes 262176 | tf_op jit(solution)/shard_map/ppermute | solution.py:39
  128.0 8.0 %multiply_convert_fusion.1 = (bf16[512,1024]{1,0:T(8,128)(2,1)S(1)}, f32[512,1024]{1,0:T(8,128)}, f32[512,1024]{1,0:T(8,128)}) fusion(f32[1024]{0:T(1024)S(1)} %copy-done.47, bf16[1024,2304]{0,1:T(8,128)(2,1)S(1)} %copy-done.11, bf16[128,1024]{1,0:T(8,128)(2,1)S(1)} %collective-permute-done.22, bf16[128,1024]{1,0:T(8,128)(2,1)S(1)} %collective-permute-done.21, ...), kind=kOutput, calls=%fused_computation.14 | convolution fusion | flops 1112539136 | bytes 8392704 | tf_op jit(solution)/shard_map/dot_general | solution.py:22
  141.8 7.3 %collective-permute-done.25 = bf16[128,1024]{1,0:T(8,128)(2,1)} collective-permute-done((bf16[128,1024]{1,0:T(8,128)(2,1)}, bf16[128,1024]{1,0:T(8,128)(2,1)}, u32[]{:S(2)}, u32[]{:S(2)}) %collective-permute-start.25) | collective-permute-done | bytes 262176 | tf_op jit(solution)/shard_map/ppermute | solution.py:39
  152.9 6.4 %collective-permute-done.27 = bf16[128,1024]{1,0:T(8,128)(2,1)S(1)} collective-permute-done((bf16[128,1024]{1,0:T(8,128)(2,1)S(1)}, bf16[128,1024]{1,0:T(8,128)(2,1)S(1)}, u32[]{:S(2)}, u32[]{:S(2)}) %collective-permute-start.27) | collective-permute-done | bytes 262176 | tf_op jit(solution)/shard_map/ppermute | solution.py:39
  160.8 3.6 %convert_reduce_fusion = (f32[1024]{0:T(1024)S(1)}, bf16[512,1024]{1,0:T(8,128)(2,1)S(1)}) fusion(f32[512,1024]{1,0:T(8,128)S(1)} %copy-done.51, bf16[1024,2304]{0,1:T(8,128)(2,1)} %constant_dynamic-update-slice_fusion.21, bf16[128,1024]{1,0:T(8,128)(2,1)S(1)} %collective-permute-done.28, bf16[128,1024]{1,0:T(8,128)(2,1)S(1)} %collective-permute-done.27, ...), kind=kOutput, calls=%fused_computation.12 | convolution fusion | flops 1086848000 | bytes 8396800 | tf_op jit(solution)/shard_map/dot_general | solution.py:22
  164.4 2.9 fusion.107
  175.4 4.2 %collective-permute-done.31 = bf16[128,1024]{1,0:T(8,128)(2,1)S(1)} collective-permute-done((bf16[128,1024]{1,0:T(8,128)(2,1)S(1)}, bf16[128,1024]{1,0:T(8,128)(2,1)S(1)}, u32[]{:S(2)}, u32[]{:S(2)}) %collective-permute-start.31) | collective-permute-done | bytes 262176 | tf_op jit(solution)/shard_map/ppermute | solution.py:39
  185.8 3.0 collective-permute-done.43
  188.9 6.8 %collective-permute-done.51 = bf16[512,1024]{1,0:T(8,128)(2,1)} collective-permute-done((bf16[512,1024]{1,0:T(8,128)(2,1)S(1)}, bf16[512,1024]{1,0:T(8,128)(2,1)}, u32[]{:S(2)}, u32[]{:S(2)}) %collective-permute-start.51) | collective-permute-done | bytes 1048608 | tf_op jit(solution)/shard_map/ppermute | solution.py:39
  195.7 3.9 %fusion.80 = (bf16[512,1024]{1,0:T(8,128)(2,1)S(1)}, f32[512,1024]{1,0:T(8,128)}) fusion(bf16[512,1024]{1,0:T(8,128)(2,1)} %collective-permute-done.51, f32[1024,1024]{1,0:T(8,128)} %copy-done.3), kind=kLoop, calls=%fused_computation.246 | loop fusion | flops 1572864 | bytes 6291456 | tf_op jit(solution)/shard_map/convert.6
  200.5 2.8 collective-permute-start.54
  203.2 14.1 %collective-permute-done.55 = bf16[512,1024]{1,0:T(8,128)(2,1)} collective-permute-done((bf16[512,1024]{1,0:T(8,128)(2,1)S(1)}, bf16[512,1024]{1,0:T(8,128)(2,1)}, u32[]{:S(2)}, u32[]{:S(2)}) %collective-permute-start.55) | collective-permute-done | bytes 1048608 | tf_op jit(solution)/shard_map/ppermute | solution.py:39
  220.8 2.8 collective-permute-start.58
  232.9 2.7 fusion.108
  239.0 2.9 collective-permute-done.45
  254.4 4.6 %collective-permute-done.47 = bf16[512,256]{1,0:T(8,128)(2,1)S(1)} collective-permute-done((bf16[512,256]{1,0:T(8,128)(2,1)S(1)}, bf16[512,256]{1,0:T(8,128)(2,1)S(1)}, u32[]{:S(2)}, u32[]{:S(2)}) %collective-permute-start.47) | collective-permute-done | bytes 262176 | tf_op jit(solution)/shard_map/ppermute | solution.py:39
  262.1 2.5 collective-permute-start.50
  274.0 12.7 %collective-permute-done.38 = bf16[512,768]{1,0:T(8,128)(2,1)S(1)} collective-permute-done((bf16[512,768]{1,0:T(8,128)(2,1)}, bf16[512,768]{1,0:T(8,128)(2,1)S(1)}, u32[]{:S(2)}, u32[]{:S(2)}) %collective-permute-start.38) | collective-permute-done | bytes 786464 | tf_op jit(solution)/shard_map/ppermute | solution.py:39
  288.4 2.6 collective-permute-start.41
  292.9 5.2 %collective-permute-done.41 = bf16[128,768]{1,0:T(8,128)(2,1)S(1)} collective-permute-done((bf16[128,768]{1,0:T(8,128)(2,1)S(1)}, bf16[128,768]{1,0:T(8,128)(2,1)S(1)}, u32[]{:S(2)}, u32[]{:S(2)}) %collective-permute-start.41) | collective-permute-done | bytes 196640 | tf_op jit(solution)/shard_map/ppermute | solution.py:39
  298.1 7.3 %collective-permute-done.40 = bf16[128,768]{1,0:T(8,128)(2,1)S(1)} collective-permute-done((bf16[128,768]{1,0:T(8,128)(2,1)S(1)}, bf16[128,768]{1,0:T(8,128)(2,1)S(1)}, u32[]{:S(2)}, u32[]{:S(2)}) %collective-permute-start.40) | collective-permute-done | bytes 196640 | tf_op jit(solution)/shard_map/ppermute | solution.py:39
  (353 shorter events, 123.0 us)
Async XLA Ops:
  5.1 20.2 %collective-permute-start.3 = (bf16[128,768]{1,0:T(8,128)(2,1)S(1)}, bf16[128,768]{1,0:T(8,128)(2,1)S(1)}, u32[]{:S(2)}, u32[]{:S(2)}) collective-permute-start(bf16[128,768]{1,0:T(8,128)(2,1)S(1)} %get-tuple-element.126), channel_id=1, source_target_pairs={{0,8},{4,12},{8,0},{12,4},{16,24},{20,28},{24,16},{28,20},{1,9},{5... | collective-permute-start | bytes 589832 | tf_op jit(solution)/shard_map/ppermute | solution.py:39
  8.2 17.2 %collective-permute-start.4 = (bf16[128,768]{1,0:T(8,128)(2,1)S(1)}, bf16[128,768]{1,0:T(8,128)(2,1)S(1)}, u32[]{:S(2)}, u32[]{:S(2)}) collective-permute-start(bf16[128,768]{1,0:T(8,128)(2,1)S(1)} %get-tuple-element.126), channel_id=1, source_target_pairs={{0,16},{4,20},{8,24},{12,28},{16,0},{20,4},{24,8},{28,12},{1,17},{... | collective-permute-start | bytes 589832 | tf_op jit(solution)/shard_map/ppermute | solution.py:39
  10.8 14.6 %collective-permute-start.5 = (bf16[128,768]{1,0:T(8,128)(2,1)S(1)}, bf16[128,768]{1,0:T(8,128)(2,1)S(1)}, u32[]{:S(2)}, u32[]{:S(2)}) collective-permute-start(bf16[128,768]{1,0:T(8,128)(2,1)S(1)} %get-tuple-element.126), channel_id=1, source_target_pairs={{0,24},{4,28},{8,16},{12,20},{16,8},{20,12},{24,0},{28,4},{1,25},{... | collective-permute-start | bytes 589832 | tf_op jit(solution)/shard_map/ppermute | solution.py:39
  10.8 20.4 %collective-permute-start.6 = (bf16[128,768]{1,0:T(8,128)(2,1)S(1)}, bf16[128,768]{1,0:T(8,128)(2,1)S(1)}, u32[]{:S(2)}, u32[]{:S(2)}) collective-permute-start(bf16[128,768]{1,0:T(8,128)(2,1)S(1)} %get-tuple-element.126), channel_id=1, source_target_pairs={{0,4},{4,0},{8,12},{12,8},{16,20},{20,16},{24,28},{28,24},{1,5},{5... | collective-permute-start | bytes 589832 | tf_op jit(solution)/shard_map/ppermute | solution.py:39
  18.7 13.1 %collective-permute-start.1 = (bf16[128,1024]{1,0:T(8,128)(2,1)S(1)}, bf16[128,1024]{1,0:T(8,128)(2,1)}, u32[]{:S(2)}, u32[]{:S(2)}) collective-permute-start(bf16[128,1024]{1,0:T(8,128)(2,1)S(1)} %constant_dynamic-update-slice_fusion), channel_id=1, source_target_pairs={{0,2},{1,3},{2,0},{3,1},{4,6},{5,7},{6,4},{7,5},{8,10},{9,11},{10,... | collective-permute-start | bytes 786440 | tf_op jit(solution)/shard_map/ppermute | solution.py:39
  25.4 20.4 %collective-permute-start = (bf16[128,1024]{1,0:T(8,128)(2,1)S(1)}, bf16[128,1024]{1,0:T(8,128)(2,1)S(1)}, u32[]{:S(2)}, u32[]{:S(2)}) collective-permute-start(bf16[128,1024]{1,0:T(8,128)(2,1)S(1)} %constant_dynamic-update-slice_fusion), channel_id=1, source_target_pairs={{0,1},{1,0},{2,3},{3,2},{4,5},{5,4},{6,7},{7,6},{8,9},{9,8},{10,11... | collective-permute-start | bytes 786440 | tf_op jit(solution)/shard_map/ppermute | solution.py:39
  26.3 31.8 %collective-permute-start.10 = (bf16[128,2304]{0,1:T(8,128)(2,1)S(1)}, bf16[128,2304]{0,1:T(8,128)(2,1)S(1)}, u32[]{:S(2)}, u32[]{:S(2)}) collective-permute-start(bf16[128,2304]{0,1:T(8,128)(2,1)S(1)} %pad_maximum_fusion.5), channel_id=1, source_target_pairs={{0,8},{4,12},{8,0},{12,4},{16,24},{20,28},{24,16},{28,20},{1,9},{5... | collective-permute-start | bytes 1769480 | tf_op jit(solution)/shard_map/ppermute | solution.py:39
  31.2 9.9 %collective-permute-start.8 = (bf16[128,768]{1,0:T(8,128)(2,1)S(1)}, bf16[128,768]{1,0:T(8,128)(2,1)S(1)}, u32[]{:S(2)}, u32[]{:S(2)}) collective-permute-start(bf16[128,768]{1,0:T(8,128)(2,1)S(1)} %collective-permute-done.4), channel_id=1, source_target_pairs={{0,4},{4,0},{8,12},{12,8},{16,20},{20,16},{24,28},{28,24},{1,5},{5... | collective-permute-start | bytes 589832 | tf_op jit(solution)/shard_map/ppermute | solution.py:39
  31.8 11.4 %collective-permute-start.9 = (bf16[128,768]{1,0:T(8,128)(2,1)S(1)}, bf16[128,768]{1,0:T(8,128)(2,1)S(1)}, u32[]{:S(2)}, u32[]{:S(2)}) collective-permute-start(bf16[128,768]{1,0:T(8,128)(2,1)S(1)} %collective-permute-done.5), channel_id=1, source_target_pairs={{0,4},{4,0},{8,12},{12,8},{16,20},{20,16},{24,28},{28,24},{1,5},{5... | collective-permute-start | bytes 589832 | tf_op jit(solution)/shard_map/ppermute | solution.py:39
  37.4 9.9 %collective-permute-start.2 = (bf16[128,1024]{1,0:T(8,128)(2,1)}, bf16[128,1024]{1,0:T(8,128)(2,1)S(1)}, u32[]{:S(2)}, u32[]{:S(2)}) collective-permute-start(bf16[128,1024]{1,0:T(8,128)(2,1)} %collective-permute-done.1), channel_id=1, source_target_pairs={{0,1},{1,0},{2,3},{3,2},{4,5},{5,4},{6,7},{7,6},{8,9},{9,8},{10,11... | collective-permute-start | bytes 786440 | tf_op jit(solution)/shard_map/ppermute | solution.py:39
  41.1 40.5 %collective-permute-start.11 = (bf16[128,2304]{0,1:T(8,128)(2,1)S(1)}, bf16[128,2304]{0,1:T(8,128)(2,1)S(1)}, u32[]{:S(2)}, u32[]{:S(2)}) collective-permute-start(bf16[128,2304]{0,1:T(8,128)(2,1)S(1)} %pad_maximum_fusion.5), channel_id=1, source_target_pairs={{0,16},{4,20},{8,24},{12,28},{16,0},{20,4},{24,8},{28,12},{1,17},{... | collective-permute-start | bytes 1769480 | tf_op jit(solution)/shard_map/ppermute | solution.py:39
  43.2 40.8 %collective-permute-start.12 = (bf16[128,2304]{0,1:T(8,128)(2,1)S(1)}, bf16[128,2304]{0,1:T(8,128)(2,1)}, u32[]{:S(2)}, u32[]{:S(2)}) collective-permute-start(bf16[128,2304]{0,1:T(8,128)(2,1)S(1)} %pad_maximum_fusion.5), channel_id=1, source_target_pairs={{0,24},{4,28},{8,16},{12,20},{16,8},{20,12},{24,0},{28,4},{1,25},{... | collective-permute-start | bytes 1769480 | tf_op jit(solution)/shard_map/ppermute | solution.py:39
  45.8 41.7 %collective-permute-start.13 = (bf16[128,2304]{0,1:T(8,128)(2,1)S(1)}, bf16[128,2304]{0,1:T(8,128)(2,1)}, u32[]{:S(2)}, u32[]{:S(2)}) collective-permute-start(bf16[128,2304]{0,1:T(8,128)(2,1)S(1)} %pad_maximum_fusion.5), channel_id=1, source_target_pairs={{0,4},{4,0},{8,12},{12,8},{16,20},{20,16},{24,28},{28,24},{1,5},{5... | collective-permute-start | bytes 1769480 | tf_op jit(solution)/shard_map/ppermute | solution.py:39
  58.1 31.3 %collective-permute-start.14 = (bf16[128,2304]{0,1:T(8,128)(2,1)S(1)}, bf16[128,2304]{0,1:T(8,128)(2,1)S(1)}, u32[]{:S(2)}, u32[]{:S(2)}) collective-permute-start(bf16[128,2304]{0,1:T(8,128)(2,1)S(1)} %collective-permute-done.10), channel_id=1, source_target_pairs={{0,4},{4,0},{8,12},{12,8},{16,20},{20,16},{24,28},{28,24},{1,5},{5... | collective-permute-start | bytes 1769480 | tf_op jit(solution)/shard_map/ppermute | solution.py:39
  81.6 16.3 %collective-permute-start.15 = (bf16[128,2304]{0,1:T(8,128)(2,1)S(1)}, bf16[128,2304]{0,1:T(8,128)(2,1)S(1)}, u32[]{:S(2)}, u32[]{:S(2)}) collective-permute-start(bf16[128,2304]{0,1:T(8,128)(2,1)S(1)} %collective-permute-done.11), channel_id=1, source_target_pairs={{0,4},{4,0},{8,12},{12,8},{16,20},{20,16},{24,28},{28,24},{1,5},{5... | collective-permute-start | bytes 1769480 | tf_op jit(solution)/shard_map/ppermute | solution.py:39
  84.0 21.7 %collective-permute-start.16 = (bf16[128,2304]{0,1:T(8,128)(2,1)}, bf16[128,2304]{0,1:T(8,128)(2,1)S(1)}, u32[]{:S(2)}, u32[]{:S(2)}) collective-permute-start(bf16[128,2304]{0,1:T(8,128)(2,1)} %collective-permute-done.12), channel_id=1, source_target_pairs={{0,4},{4,0},{8,12},{12,8},{16,20},{20,16},{24,28},{28,24},{1,5},{5... | collective-permute-start | bytes 1769480 | tf_op jit(solution)/shard_map/ppermute | solution.py:39
  169.5 26.2 %collective-permute-start.51 = (bf16[512,1024]{1,0:T(8,128)(2,1)S(1)}, bf16[512,1024]{1,0:T(8,128)(2,1)}, u32[]{:S(2)}, u32[]{:S(2)}) collective-permute-start(bf16[512,1024]{1,0:T(8,128)(2,1)S(1)} %slice.455), channel_id=1, source_target_pairs={{0,4},{4,0},{8,12},{12,8},{16,20},{20,16},{24,28},{28,24},{1,5},{5... | collective-permute-start | bytes 3145736 | tf_op jit(solution)/shard_map/ppermute | solution.py:39
  173.8 43.5 %collective-permute-start.55 = (bf16[512,1024]{1,0:T(8,128)(2,1)S(1)}, bf16[512,1024]{1,0:T(8,128)(2,1)}, u32[]{:S(2)}, u32[]{:S(2)}) collective-permute-start(bf16[512,1024]{1,0:T(8,128)(2,1)S(1)} %slice.454), channel_id=1, source_target_pairs={{0,4},{4,0},{8,12},{12,8},{16,20},{20,16},{24,28},{28,24},{1,5},{5... | collective-permute-start | bytes 3145736 | tf_op jit(solution)/shard_map/ppermute | solution.py:39
  185.6 35.2 %collective-permute-start.32 = (bf16[128,1024]{1,0:T(8,128)(2,1)S(1)}, bf16[128,1024]{1,0:T(8,128)(2,1)}, u32[]{:S(2)}, u32[]{:S(2)}) collective-permute-start(bf16[128,1024]{1,0:T(8,128)(2,1)S(1)} %get-tuple-element.85), channel_id=1, source_target_pairs={{0,1},{1,0},{2,3},{3,2},{4,5},{5,4},{6,7},{7,6},{8,9},{9,8},{10,11... | collective-permute-start | bytes 786440 | tf_op jit(solution)/shard_map/ppermute | solution.py:39
  188.8 34.7 %collective-permute-start.34 = (bf16[128,1024]{1,0:T(8,128)(2,1)}, bf16[128,1024]{1,0:T(8,128)(2,1)S(1)}, u32[]{:S(2)}, u32[]{:S(2)}) collective-permute-start(bf16[128,1024]{1,0:T(8,128)(2,1)} %collective-permute-done.33), channel_id=1, source_target_pairs={{0,1},{1,0},{2,3},{3,2},{4,5},{5,4},{6,7},{7,6},{8,9},{9,8},{10,11... | collective-permute-start | bytes 786440 | tf_op jit(solution)/shard_map/ppermute | solution.py:39
  200.5 48.8 %collective-permute-start.54 = (bf16[128,1024]{1,0:T(8,128)(2,1)}, bf16[128,1024]{1,0:T(8,128)(2,1)S(1)}, u32[]{:S(2)}, u32[]{:S(2)}) collective-permute-start(bf16[128,1024]{1,0:T(8,128)(2,1)} %get-tuple-element.105), channel_id=1, source_target_pairs={{0,24},{4,28},{8,16},{12,20},{16,8},{20,12},{24,0},{28,4},{1,25},{... | collective-permute-start | bytes 786440 | tf_op jit(solution)/shard_map/ppermute | solution.py:39
  203.2 47.0 %collective-permute-start.53 = (bf16[128,1024]{1,0:T(8,128)(2,1)}, bf16[128,1024]{1,0:T(8,128)(2,1)}, u32[]{:S(2)}, u32[]{:S(2)}) collective-permute-start(bf16[128,1024]{1,0:T(8,128)(2,1)} %get-tuple-element.106), channel_id=1, source_target_pairs={{0,16},{4,20},{8,24},{12,28},{16,0},{20,4},{24,8},{28,12},{1,17},{... | collective-permute-start | bytes 786440 | tf_op jit(solution)/shard_map/ppermute | solution.py:39
  217.3 32.9 %collective-permute-start.52 = (bf16[128,1024]{1,0:T(8,128)(2,1)}, bf16[128,1024]{1,0:T(8,128)(2,1)}, u32[]{:S(2)}, u32[]{:S(2)}) collective-permute-start(bf16[128,1024]{1,0:T(8,128)(2,1)} %get-tuple-element.104), channel_id=1, source_target_pairs={{0,8},{4,12},{8,0},{12,4},{16,24},{20,28},{24,16},{28,20},{1,9},{5... | collective-permute-start | bytes 786440 | tf_op jit(solution)/shard_map/ppermute | solution.py:39
  220.8 41.2 %collective-permute-start.58 = (bf16[128,1024]{1,0:T(8,128)(2,1)}, bf16[128,1024]{1,0:T(8,128)(2,1)S(1)}, u32[]{:S(2)}, u32[]{:S(2)}) collective-permute-start(bf16[128,1024]{1,0:T(8,128)(2,1)} %get-tuple-element.102), channel_id=1, source_target_pairs={{0,24},{4,28},{8,16},{12,20},{16,8},{20,12},{24,0},{28,4},{1,25},{... | collective-permute-start | bytes 786440 | tf_op jit(solution)/shard_map/ppermute | solution.py:39
  247.1 17.5 %collective-permute-start.57 = (bf16[128,1024]{1,0:T(8,128)(2,1)S(1)}, bf16[128,1024]{1,0:T(8,128)(2,1)S(1)}, u32[]{:S(2)}, u32[]{:S(2)}) collective-permute-start(bf16[128,1024]{1,0:T(8,128)(2,1)S(1)} %copy-done.22), channel_id=1, source_target_pairs={{0,16},{4,20},{8,24},{12,28},{16,0},{20,4},{24,8},{28,12},{1,17},{... | collective-permute-start | bytes 786440 | tf_op jit(solution)/shard_map/ppermute | solution.py:39
  249.3 15.4 %collective-permute-start.56 = (bf16[128,1024]{1,0:T(8,128)(2,1)S(1)}, bf16[128,1024]{1,0:T(8,128)(2,1)S(1)}, u32[]{:S(2)}, u32[]{:S(2)}) collective-permute-start(bf16[128,1024]{1,0:T(8,128)(2,1)S(1)} %copy-done.21), channel_id=1, source_target_pairs={{0,8},{4,12},{8,0},{12,4},{16,24},{20,28},{24,16},{28,20},{1,9},{5... | collective-permute-start | bytes 786440 | tf_op jit(solution)/shard_map/ppermute | solution.py:39
  253.5 19.2 %collective-permute-start.35 = (bf16[128,1024]{1,0:T(8,128)(2,1)}, bf16[128,1024]{1,0:T(8,128)(2,1)S(1)}, u32[]{:S(2)}, u32[]{:S(2)}) collective-permute-start(bf16[128,1024]{1,0:T(8,128)(2,1)} %get-tuple-element.107), channel_id=1, source_target_pairs={{0,1},{1,0},{2,3},{3,2},{4,5},{5,4},{6,7},{7,6},{8,9},{9,8},{10,11... | collective-permute-start | bytes 786440 | tf_op jit(solution)/shard_map/ppermute | solution.py:39
  259.0 13.7 %collective-permute-start.37 = (bf16[128,1024]{1,0:T(8,128)(2,1)}, bf16[128,1024]{1,0:T(8,128)(2,1)}, u32[]{:S(2)}, u32[]{:S(2)}) collective-permute-start(bf16[128,1024]{1,0:T(8,128)(2,1)} %fusion.30), channel_id=1, source_target_pairs={{0,2},{1,3},{2,0},{3,1},{4,6},{5,7},{6,4},{7,5},{8,10},{9,11},{10,... | collective-permute-start | bytes 786440 | tf_op jit(solution)/shard_map/ppermute | solution.py:39
  268.5 18.2 %collective-permute-start.38 = (bf16[512,768]{1,0:T(8,128)(2,1)}, bf16[512,768]{1,0:T(8,128)(2,1)S(1)}, u32[]{:S(2)}, u32[]{:S(2)}) collective-permute-start(bf16[512,768]{1,0:T(8,128)(2,1)} %slice.456), channel_id=1, source_target_pairs={{0,4},{4,0},{8,12},{12,8},{16,20},{20,16},{24,28},{28,24},{1,5},{5... | collective-permute-start | bytes 2359304 | tf_op jit(solution)/shard_map/ppermute | solution.py:39
  288.4 9.7 %collective-permute-start.41 = (bf16[128,768]{1,0:T(8,128)(2,1)S(1)}, bf16[128,768]{1,0:T(8,128)(2,1)S(1)}, u32[]{:S(2)}, u32[]{:S(2)}) collective-permute-start(bf16[128,768]{1,0:T(8,128)(2,1)S(1)} %get-tuple-element.116), channel_id=1, source_target_pairs={{0,24},{4,28},{8,16},{12,20},{16,8},{20,12},{24,0},{28,4},{1,25},{... | collective-permute-start | bytes 589832 | tf_op jit(solution)/shard_map/ppermute | solution.py:39
  291.0 14.4 %collective-permute-start.40 = (bf16[128,768]{1,0:T(8,128)(2,1)S(1)}, bf16[128,768]{1,0:T(8,128)(2,1)S(1)}, u32[]{:S(2)}, u32[]{:S(2)}) collective-permute-start(bf16[128,768]{1,0:T(8,128)(2,1)S(1)} %get-tuple-element.117), channel_id=1, source_target_pairs={{0,16},{4,20},{8,24},{12,28},{16,0},{20,4},{24,8},{28,12},{1,17},{... | collective-permute-start | bytes 589832 | tf_op jit(solution)/shard_map/ppermute | solution.py:39
  291.0 14.4 %collective-permute-start.39 = (bf16[128,768]{1,0:T(8,128)(2,1)S(1)}, bf16[128,768]{1,0:T(8,128)(2,1)S(1)}, u32[]{:S(2)}, u32[]{:S(2)}) collective-permute-start(bf16[128,768]{1,0:T(8,128)(2,1)S(1)} %get-tuple-element.115), channel_id=1, source_target_pairs={{0,8},{4,12},{8,0},{12,4},{16,24},{20,28},{24,16},{28,20},{1,9},{5... | collective-permute-start | bytes 589832 | tf_op jit(solution)/shard_map/ppermute | solution.py:39
  (80 other events, 700.1 us)

commit v2 on v0

v2 whole, which is shorter than its diff:
```python
from functools import partial

import jax
import jax.numpy as jnp
from jax import lax
from jax.experimental import pallas as pl
from jax.experimental.pallas import tpu as pltpu
from jax.sharding import PartitionSpec as P

HEAD_DIM = 64


epsilon = 1e-12
masked_fill = -1e30

row_slots = (0, 2, 1, 3)
slot_offsets = (0, 4, 6, 5, 7, 3, 2, 1)


def matmul(left_side, right_side):
    return jnp.dot(left_side, right_side, preferred_element_type=jnp.float32)


def matmul_nt(left_side, right_side):
    return lax.dot_general(
        left_side, right_side, (((1,), (1,)), ((), ())), preferred_element_type=jnp.float32
    )


def matmul_tn(left_side, right_side):
    return lax.dot_general(
        left_side, right_side, (((0,), (0,)), ((), ())), preferred_element_type=jnp.float32
    )


def low(value):
    return value.astype(jnp.bfloat16)


def wide(value):
    return value.astype(jnp.float32)


def shaped(shape, dtype=jnp.bfloat16):
    return jax.ShapeDtypeStruct(shape, dtype)


def paired():
    return lax.axis_size("dp") == len(slot_offsets)


def swap(block, axis_name, offset):
    count = lax.axis_size(axis_name)
    return lax.ppermute(block, axis_name, [(i, i ^ offset) for i in range(count)])


def part(array, start, rows):
    return array, start, rows


def kernel_call(body, out_shape, whole=(), pieces=(), scalars=(), marks=(), scratch=()):
    pieces = [
        [p if isinstance(p, tuple) else (p, 0, p.shape[0]) for p in some] for some in pieces
    ]
    buffers = [
        pltpu.VMEM((sum(p[2] for p in some), *some[0][0].shape[1:]), some[0][0].dtype)
        for some in pieces
    ]
    flat = [p for some in pieces for p in some]
    flat_out, tree = jax.tree.flatten(list(out_shape))
    counts = (len(scalars), len(whole), len(flat), len(marks), len(flat_out), len(buffers))

    def run(*refs):
        groups, start = [], 0
        for count in counts:
            groups.append(refs[start : start + count])
            start += count
        scalar_refs, whole_refs, piece_refs, _, out_refs, buffer_refs = groups
        rest = refs[start:]
        copies = []
        if flat:
            done, rest = rest[0], rest[1:]
            k = 0
            for some, buffer in zip(pieces, buffer_refs):
                row, mine = 0, []
                for _, first, rows in some:
                    mine.append(
                        pltpu.make_async_copy(
                            piece_refs[k].at[pl.ds(first, rows)],
                            buffer.at[pl.ds(row, rows)],
                            done.at[k],
                        )
                    )
                    row += rows
                    k += 1
                copies.append(mine)
            for copy in (c for mine in copies for c in mine):
                copy.start()

        def need(number):
            for copy in copies[number]:
                copy.wait()

        outs = jax.tree.unflatten(tree, out_refs)
        body(need, *scalar_refs, *whole_refs, *buffer_refs, *outs, *rest)

    anywhere = pl.BlockSpec(memory_space=pl.ANY)
    inside = pl.BlockSpec(memory_space=pltpu.VMEM)
    semaphores = [pltpu.SemaphoreType.DMA((len(flat),))] if flat else []
    results = pl.pallas_call(
        run,
        out_shape=flat_out,
        in_specs=[pl.BlockSpec(memory_space=pltpu.SMEM)] * len(scalars)
        + [inside] * len(whole)
        + [anywhere] * (len(flat) + len(marks)),
        out_specs=[inside] * len(flat_out),
        scratch_shapes=buffers + semaphores + list(scratch),
        compiler_params=pltpu.CompilerParams(vmem_limit_bytes=VMEM_LIMIT),
        cost_estimate=pl.CostEstimate(
            flops=int(QUICK * 1.1e9), bytes_accessed=int(QUICK * 3.5e6), transcendentals=0
        ),
    )(*scalars, *whole, *[p[0] for p in flat], *marks)
    return jax.tree.unflatten(tree, results)


VMEM_LIMIT = 63 << 20
QUICK = 0.01
PARTS = 1


def part_shapes(rows, columns):
    return [shaped((rows // PARTS, columns))] * PARTS


def write_parts(refs, value, columns=slice(None)):
    rows = refs[0].shape[0]
    for k, ref in enumerate(refs):
        ref[:, columns] = low(value[k * rows : (k + 1) * rows])


def region(flag, body, *operands):
    def nothing(*some):
        return jax.tree.map(lambda x: jnp.zeros(x.shape, x.dtype), jax.eval_shape(body, *operands))

    return lax.cond(flag, body, nothing, *operands)


def swap_parts(parts, offset):
    return [swap(p, "tensor", offset) for p in parts]


def gather_rows(parts):
    across = swap_parts(parts, 2)
    beside = swap_parts(parts, 1)
    corner = swap_parts(across, 1)
    return [*parts, *across, *beside, *corner]


def turn_kernel(need, near_ref, arrived_ref, out_refs):
    need(0)
    need(1)
    write_parts(out_refs, near_ref[...] + wide(arrived_ref[...]))


def scatter_rows(near, far, marks=()):
    rows, columns = near.shape
    half = rows // 2
    arrived = swap_parts(far, 1)
    turned = kernel_call(
        turn_kernel,
        [part_shapes(half, columns)],
        pieces=[[part(near, half, half)], arrived[PARTS:]],
        marks=marks,
    )[0]
    return [[part(near, 0, half)], arrived[:PARTS], swap_parts(turned, 2)]


def own_sum(need, near_ref, arrived_ref, across_ref):
    for number in range(3):
        need(number)
    return near_ref[...] + wide(arrived_ref[...]) + wide(across_ref[...])


def gather_first(shard):
    if not paired():
        return [lax.all_gather(shard, "dp", axis=0, tiled=True)]
    beside = swap(shard, "dp", 1)
    farther, far = swap(shard, "dp", 6), swap(shard, "dp", 4)
    above = swap(shard, "dp", 2)
    return [shard, far, farther, swap(beside, "dp", 2), above, beside]


def gather_rest(pieces):
    if not paired():
        return pieces
    shard, far, farther, corner, above, beside = pieces
    return [shard, far, farther, swap(far, "dp", 1), swap(farther, "dp", 1), corner, above, beside]


def far_pieces(pieces):
    return pieces[1:3] if paired() else pieces


def weight_cuts(width, columns):
    if not paired():
        return [shaped((width, columns), jnp.float32)]
    block = width // len(slot_offsets)
    return [shaped((block, columns), jnp.float32)] + [
        shaped((block * n, columns)) for n in (2, 2, 2, 1)
    ]


def weight_grad_into(pairs, out_refs):
    column = 0
    for left_ref, right_ref in pairs:
        right = right_ref[...]
        columns = slice(column, column + right.shape[1])
        column += right.shape[1]
        start = 0
        for out_ref in out_refs:
            for place in range(0, out_ref.shape[0], 128):
                block = left_ref[:, start : start + 128]
                out_ref[place : place + 128, columns] = matmul_tn(block, right).astype(
                    out_ref.dtype
                )
                start += 128


def scatter_first(cuts):
    if not paired():
        return cuts
    kept, far, far_beside, above, beside = cuts
    return kept, far, beside, swap(far_beside, "dp", 1), swap(above, "dp", 2)


def combine_kernel(
    need, far_ref, far_in_ref, beside_ref, above_ref, far_out, farther_out, beside_out
):
    block = far_out.shape[0]
    need(0)
    need(1)
    farther_out[...] = low(wide(far_ref[block:]) + wide(far_in_ref[block:]))
    far_out[...] = low(wide(far_ref[:block]) + wide(far_in_ref[:block]))
    need(2)
    need(3)
    beside_out[...] = low(wide(beside_ref[...]) + wide(above_ref[...]))


def scatter_second(state, marks=()):
    if not paired():
        return state, marks
    kept, far, beside, far_in, above = state
    block = kept.shape[0]
    far_out, farther_out, beside_out = kernel_call(
        combine_kernel,
        [shaped(kept.shape)] * 3,
        pieces=[[far], [far_in], [beside], [part(above, 0, block)]],
        marks=marks,
    )
    state = [
        kept,
        part(above, block, block),
        swap(farther_out, "dp", 6),
        swap(far_out, "dp", 4),
        swap(beside_out, "dp", 1),
    ]
    return state, [beside_out]


def last_kernel(write, count, need, *refs):
    total = None
    for number, ref in enumerate(refs[:count]):
        need(number)
        total = wide(ref[...]) if total is None else total + wide(ref[...])
    write(total, *refs[count:])


def scatter_last(state, write, out_shape, marks=()):
    if not paired():
        state = [lax.psum_scatter(state[0], "dp", scatter_dimension=0, tiled=True)]
    return kernel_call(
        partial(last_kernel, write, len(state)),
        out_shape,
        pieces=[[term] for term in state],
        marks=marks,
    )


def sum_dp_ranks(value):
    if paired():
        value = value + swap(value, "dp", 1)
        farther, far = swap(value, "dp", 6), swap(value, "dp", 4)
        return (value + swap(value, "dp", 2)) + (far + farther)
    offset = 1
    while offset < lax.axis_size("dp"):
        value = value + swap(value, "dp", offset)
        offset *= 2
    return value


def to_slots(array_ref, rank, in_slots):
    if not in_slots:
        return array_ref[...]
    width = array_ref.shape[-1] // len(slot_offsets)
    return jnp.concatenate(
        [
            array_ref[:, pl.ds(pl.multiple_of((rank ^ o) * width, width), width)]
            for o in slot_offsets
        ],
        axis=1,
    )


def from_slots(value, rank, in_slots, out_ref):
    if not in_slots:
        out_ref[...] = value.astype(out_ref.dtype)
        return
    width = out_ref.shape[-1] // len(slot_offsets)
    for place, o in enumerate(slot_offsets):
        out_ref[:, pl.ds(pl.multiple_of((rank ^ o) * width, width), width)] = value[
            :, place * width : (place + 1) * width
        ].astype(out_ref.dtype)


def segments(lengths_ref, places):
    total = jnp.int32(0)
    found = jnp.zeros(places.shape, jnp.int32)
    for k in range(lengths_ref.shape[1]):
        total = total + lengths_ref[0, k]
        found = found + jnp.where(places >= total, 1, 0)
    return found


def prepare_kernel(need, query_ref, key_ref, value_ref, proj_ref, out_ref):
    width = query_ref.shape[1]
    for place, ref in enumerate((query_ref, key_ref, value_ref)):
        out_ref[:, place * width : (place + 1) * width] = ref[...]
    out_ref[:, 3 * width :] = proj_ref[...].T


def place_kernel(in_slots, need, ranks_ref, tokens_ref, grad_ref, small_ref, *out_refs):
    write_parts(out_refs[0], to_slots(tokens_ref, ranks_ref[0], in_slots))
    for ref, out_ref in zip((grad_ref, small_ref), out_refs[1:]):
        out_ref[...] = to_slots(ref, ranks_ref[0], in_slots)


def pass_kernel(need, in_ref, out_ref):
    need(0)
    out_ref[...] = in_ref[...]


def turn_over_kernel(need, in_ref, out_ref):
    need(0)
    out_ref[...] = in_ref[...].T


def back_into(left_ref, right_ref, inner, near_ref, far_ref):
    half = near_ref.shape[0]
    for start in range(0, near_ref.shape[1], 256):
        columns = slice(start, start + 256)
        total = matmul_nt(left_ref[...], right_ref[columns, inner])
        near_ref[:, columns] = total[:half]
        write_parts(far_ref, total[half:], columns)


def attention_kernel(
    scale,
    need,
    ranks_ref,
    lengths_ref,
    key_ref,
    bias_ref,
    tokens_ref,
    weights_ref,
    qkv_ref,
    probs_ref,
    context_ref,
    fill_ref,
):
    rows = tokens_ref.shape[0]
    piece = rows // len(row_slots)
    head_width = context_ref.shape[1]
    rank = ranks_ref[1]
    down = lax.broadcasted_iota(jnp.int32, (rows, 1), 0)
    along = lax.broadcasted_iota(jnp.int32, (1, rows), 1)

    def places(index):
        slot, step = index // piece, index % piece
        owner = jnp.where(slot == 0, row_slots[0], 0)
        for k in range(1, len(row_slots)):
            owner = jnp.where(slot == k, row_slots[k], owner)
        return (owner ^ rank) * piece + step

    segment_down = segments(lengths_ref, places(down))
    segment_along = segments(lengths_ref, places(along))
    keys = jnp.concatenate([key_ref[pl.ds(rank ^ o, 1), :] for o in row_slots], axis=1)
    allowed = (segment_down == segment_along) & ((keys == 1) | (down == along))
    fill_ref[...] = jnp.where(allowed, 0.0, masked_fill)

    need(0)
    need(1)
    qkv = matmul(tokens_ref[...], weights_ref[:, : 3 * head_width]) + bias_ref[...]
    qkv_ref[:, :head_width] = low(qkv[:, :head_width] * scale)
    qkv_ref[:, head_width:] = low(qkv[:, head_width:])
    for head in range(head_width // HEAD_DIM):
        columns = [
            slice(part * head_width + head * HEAD_DIM, part * head_width + (head + 1) * HEAD_DIM)
            for part in range(3)
        ]
        query, key, value = (qkv_ref[:, c] for c in columns)
        scores = matmul_nt(query, key) + fill_ref[...]
        weights = jnp.exp(scores - jnp.max(scores, axis=1, keepdims=True))
        probs = low(weights * (1.0 / jnp.sum(weights, axis=1, keepdims=True)))
        probs_ref[head] = probs
        context_ref[:, columns[0]] = low(matmul(probs, value))


def project_kernel(need, context_ref, weights_ref, shard_ref, near_ref, far_ref, out_ref):
    need(2)
    out_ref[...] = shard_ref[...]
    need(0)
    need(1)
    width = context_ref.shape[1]
    back_into(context_ref, weights_ref, slice(3 * width, None), near_ref, far_ref)


def first_norm_kernel(
    need,
    small_ref,
    near_ref,
    arrived_ref,
    across_ref,
    tokens_ref,
    first_ref,
    unit_ref,
    scale_ref,
    low_ref,
):
    need(3)
    total = (
        wide(tokens_ref[...])
        + own_sum(need, near_ref, arrived_ref, across_ref)
        + small_ref[0:1]
    )
    centred = total - jnp.mean(total, axis=1, keepdims=True)
    scale = lax.rsqrt(jnp.mean(centred * centred, axis=1, keepdims=True) + epsilon)
    unit = centred * scale
    first = unit * small_ref[1:2] + small_ref[2:3]
    unit_ref[...] = unit
    scale_ref[...] = scale
    first_ref[...] = first
    write_parts(low_ref, first)


def inner_kernel(need, bias_ref, rows_ref, weights_ref, active_ref, slope_ref):
    need(0)
    need(1)
    for start in range(0, active_ref.shape[1], 256):
        columns = slice(start, start + 256)
        hidden = matmul(rows_ref[...], weights_ref[:, columns]) + bias_ref[:, columns]
        share = 0.5 + 0.5 * lax.erf(hidden * (0.5**0.5))
        active_ref[:, columns] = low(hidden * share)
        slope_ref[:, columns] = share + hidden * jnp.exp(-0.5 * hidden * hidden) * (
            0.3989422804014327
        )


def outer_kernel(need, active_ref, weights_ref, near_ref, far_ref):
    need(0)
    need(1)
    back_into(active_ref, weights_ref, slice(None), near_ref, far_ref)


def second_norm_kernel(
    in_slots,
    need,
    ranks_ref,
    lengths_ref,
    small_ref,
    near_ref,
    arrived_ref,
    across_ref,
    first_ref,
    grad_ref,
    out_ref,
    second_grad_ref,
    low_ref,
    sums_ref,
):
    rows, _ = first_ref.shape
    need(3)
    need(4)
    total = first_ref[...] + own_sum(need, near_ref, arrived_ref, across_ref) + small_ref[3:4]
    centred = total - jnp.mean(total, axis=1, keepdims=True)
    scale = lax.rsqrt(jnp.mean(centred * centred, axis=1, keepdims=True) + epsilon)
    unit = centred * scale
    place = ranks_ref[1] * rows + lax.broadcasted_iota(jnp.int32, (rows, 1), 0)
    valid = jnp.where(segments(lengths_ref, place) < lengths_ref.shape[1], 1.0, 0.0)
    gain = small_ref[4:5]
    second = (unit * gain + small_ref[5:6]) * valid
    from_slots(second, ranks_ref[0], in_slots, out_ref)
    cot = wide(grad_ref[...]) * valid
    pulled = cot * gain
    second_grad = scale * (
        pulled
        - jnp.mean(pulled, axis=1, keepdims=True)
        - unit * jnp.mean(pulled * unit, axis=1, keepdims=True)
    )
    second_grad_ref[...] = second_grad
    rounded = low(second_grad)
    write_parts(low_ref, rounded)
    sums_ref[0:1] = jnp.sum(wide(rounded), axis=0, keepdims=True)
    sums_ref[1:2] = jnp.sum(cot * unit, axis=0, keepdims=True)
    sums_ref[2:3] = jnp.sum(cot, axis=0, keepdims=True)
    sums_ref[3:8] = jnp.zeros_like(sums_ref[3:8])


def hidden_grad_kernel(
    need, rows_ref, outer_ref, slope_ref, inner_ref, hidden_grad_ref, near_ref, far_ref, sums_ref
):
    for number in range(3):
        need(number)
    for start in range(0, hidden_grad_ref.shape[1], 256):
        columns = slice(start, start + 256)
        grad = low(matmul(rows_ref[...], outer_ref[:, columns]) * slope_ref[:, columns])
        hidden_grad_ref[:, columns] = grad
        sums_ref[0:1, columns] = jnp.sum(wide(grad), axis=0, keepdims=True)
    need(3)
    back_into(hidden_grad_ref, inner_ref, slice(None), near_ref, far_ref)


def single_grad_kernel(need, left_ref, right_ref, *out_refs):
    need(0)
    need(1)
    weight_grad_into([(left_ref, right_ref)], out_refs)


def first_back_kernel(
    in_slots,
    need,
    ranks_ref,
    scale_ref,
    small_ref,
    second_sums_ref,
    near_ref,
    arrived_ref,
    across_ref,
    second_grad_ref,
    unit_ref,
    mix_ref,
    low_ref,
    sums_ref,
):
    need(3)
    need(4)
    cot = second_grad_ref[...] + own_sum(need, near_ref, arrived_ref, across_ref)
    unit = unit_ref[...]
    pulled = cot * small_ref[1:2]
    mix = scale_ref[...] * (
        pulled
        - jnp.mean(pulled, axis=1, keepdims=True)
        - unit * jnp.mean(pulled * unit, axis=1, keepdims=True)
    )
    mix_ref[...] = mix
    rounded = low(mix)
    write_parts(low_ref, rounded)
    sums = jnp.concatenate(
        [
            jnp.sum(wide(rounded), axis=0, keepdims=True),
            jnp.sum(cot * unit, axis=0, keepdims=True),
            jnp.sum(cot, axis=0, keepdims=True),
            second_sums_ref[0:3],
            jnp.zeros((2, mix.shape[1]), jnp.float32),
        ],
        axis=0,
    )
    from_slots(sums, ranks_ref[0], in_slots, sums_ref)


def attention_back_kernel(
    scale,
    need,
    rows_ref,
    weights_ref,
    qkv_ref,
    probs_ref,
    grads_ref,
    near_ref,
    far_ref,
    sums_ref,
    context_grad_ref,
):
    head_width = context_grad_ref.shape[1]
    need(0)
    need(1)
    context_grad_ref[...] = low(matmul(rows_ref[...], weights_ref[:, 3 * head_width :]))
    need(2)
    need(3)
    for head in range(head_width // HEAD_DIM):
        columns = [
            slice(part * head_width + head * HEAD_DIM, part * head_width + (head + 1) * HEAD_DIM)
            for part in range(3)
        ]
        query, key, value = (qkv_ref[:, c] for c in columns)
        probs = probs_ref[head]
        context_grad = context_grad_ref[:, columns[0]]
        prob_grad = matmul_nt(context_grad, value)
        exact = wide(probs)
        product = prob_grad * exact
        score_grad = low(product - exact * jnp.sum(product, axis=1, keepdims=True))
        query_grad = low(matmul(score_grad, key)) * jnp.asarray(scale, jnp.bfloat16)
        key_grad = low(matmul_tn(score_grad, query))
        value_grad = low(matmul_tn(probs, context_grad))
        for place, grad in zip(columns, (query_grad, key_grad, value_grad)):
            grads_ref[:, place] = grad
    sums_ref[...] = jnp.zeros_like(sums_ref)
    sums_ref[0:1, : 3 * head_width] = jnp.sum(wide(grads_ref[...]), axis=0, keepdims=True)
    back_into(grads_ref, weights_ref, slice(0, 3 * head_width), near_ref, far_ref)


def attention_grad_kernel(need, tokens_ref, qkv_grad_ref, rows_ref, context_ref, *out_refs):
    for number in range(4):
        need(number)
    weight_grad_into([(tokens_ref, qkv_grad_ref), (rows_ref, context_ref)], out_refs)


def tokens_grad_kernel(
    in_slots, need, ranks_ref, near_ref, arrived_ref, across_ref, mix_ref, out_ref
):
    need(3)
    total = mix_ref[...] + own_sum(need, near_ref, arrived_ref, across_ref)
    from_slots(total, ranks_ref[0], in_slots, out_ref)


def write_turned(total, out_ref):
    out_ref[...] = total.T


def write_plain(total, out_ref):
    out_ref[...] = total


def write_attention(total, query_ref, key_ref, value_ref, proj_ref):
    width = query_ref.shape[1]
    for place, ref in enumerate((query_ref, key_ref, value_ref)):
        ref[...] = total[:, place * width : (place + 1) * width]
    proj_ref[...] = total[:, 3 * width :].T


def on_device(
    tokens,
    key_mask,
    seq_lengths,
    w_query,
    b_query,
    w_key,
    w_value,
    b_value,
    w_proj,
    b_proj,
    gain_attn,
    shift_attn,
    w_inner,
    b_inner,
    w_outer,
    b_outer,
    gain_ffn,
    shift_ffn,
    out_grad,
):
    in_slots = paired()
    flag = seq_lengths[0, 0] >= 0
    ranks = jnp.stack([lax.axis_index("dp"), lax.axis_index("tensor")]).astype(jnp.int32)
    piece_rows, model_width = tokens.shape
    group_rows = piece_rows * lax.axis_size("tensor")
    half_rows = group_rows // 2
    shard_rows = w_query.shape[0]
    head_width = b_query.shape[0]
    heads = head_width // HEAD_DIM
    inner_width = b_inner.shape[0]
    scale = HEAD_DIM ** (-0.5)
    own = (piece_rows, model_width)
    own_parts = part_shapes(*own)
    partial_sums = [shaped((half_rows, model_width), jnp.float32), own_parts + own_parts]

    attn_shard = kernel_call(
        prepare_kernel,
        [shaped((shard_rows, 4 * head_width))],
        whole=[w_query, w_key, w_value, w_proj],
    )[0]
    attn_pieces = gather_first(attn_shard)
    small = jnp.stack(
        [b_proj, gain_attn, shift_attn, b_outer, gain_ffn, shift_ffn, b_proj, b_proj]
    )
    tokens, out_grad, small = kernel_call(
        partial(place_kernel, in_slots),
        [own_parts, shaped(own), shaped(small.shape, jnp.float32)],
        whole=[tokens, out_grad, small],
        scalars=[ranks],
    )
    token_rows = gather_rows(tokens)
    outer_shard = kernel_call(
        turn_over_kernel, [shaped(w_outer.shape[::-1])], pieces=[[w_outer]], marks=tokens[:1]
    )[0]
    inner_shard = kernel_call(
        pass_kernel, [shaped(w_inner.shape)], pieces=[[w_inner]], marks=far_pieces(attn_pieces)
    )[0]
    inner_pieces = gather_first(inner_shard)
    attn_weights = gather_rest(attn_pieces)
    qkv_bias = jnp.concatenate([b_query, jnp.zeros_like(b_query), b_value])[None, :]
    qkv, probs, context = kernel_call(
        partial(attention_kernel, scale),
        [
            shaped((group_rows, 3 * head_width)),
            shaped((heads, group_rows, group_rows)),
            shaped((group_rows, head_width)),
        ],
        scalars=[ranks, seq_lengths],
        whole=[key_mask.reshape(lax.axis_size("tensor"), piece_rows), qkv_bias],
        pieces=[token_rows, attn_weights],
        marks=[inner_shard],
        scratch=[pltpu.VMEM((group_rows, group_rows), jnp.float32)],
    )
    near, far, outer_shard = kernel_call(
        project_kernel,
        [*partial_sums, shaped(outer_shard.shape)],
        pieces=[[context], attn_weights, [outer_shard]],
        marks=far_pieces(inner_pieces),
    )
    outer_pieces = gather_first(outer_shard)
    inner_weights = gather_rest(inner_pieces)
    def first_part(near, far, tokens, small):
        terms = scatter_rows(near, far)
        return kernel_call(
            first_norm_kernel,
            [
                shaped(own, jnp.float32),
                shaped(own, jnp.float32),
                shaped((piece_rows, 1), jnp.float32),
                own_parts,
            ],
            whole=[small],
            pieces=[*terms, tokens],
        )

    first, unit, unit_scale, first_low = region(flag, first_part, near, far, tokens, small)
    outer_weights = gather_rest(outer_pieces)
    norm_rows = gather_rows(first_low)
    active, slope = kernel_call(
        inner_kernel,
        [shaped((group_rows, inner_width)), shaped((group_rows, inner_width), jnp.float32)],
        whole=[b_inner[None, :]],
        pieces=[norm_rows, inner_weights],
    )
    near, far = kernel_call(
        outer_kernel, partial_sums, pieces=[[active], outer_weights]
    )
    terms = scatter_rows(near, far)
    layer_out, second_grad, branch_grad, second_sums = kernel_call(
        partial(second_norm_kernel, in_slots),
        [
            shaped(own),
            shaped(own, jnp.float32),
            own_parts,
            shaped((8, model_width), jnp.float32),
        ],
        scalars=[ranks, seq_lengths],
        whole=[small],
        pieces=[*terms, [first], [out_grad]],
    )

    branch_rows = gather_rows(branch_grad)
    outer_cuts = kernel_call(
        single_grad_kernel,
        weight_cuts(model_width, inner_width),
        pieces=[branch_rows, [active]],
    )
    outer_state = scatter_first(outer_cuts)
    hidden_grad, near, far, inner_sums = kernel_call(
        hidden_grad_kernel,
        [
            shaped((group_rows, inner_width)),
            *partial_sums,
            shaped((1, inner_width), jnp.float32),
        ],
        pieces=[branch_rows, outer_weights, [slope], inner_weights],
        marks=[outer_cuts[0]],
    )
    terms = scatter_rows(near, far)
    inner_state = scatter_first(
        kernel_call(
            single_grad_kernel,
            weight_cuts(model_width, inner_width),
            pieces=[norm_rows, [hidden_grad]],
            marks=[outer_state[0], terms[1][0]],
        )
    )
    mix_grad, proj_grad, sums = kernel_call(
        partial(first_back_kernel, in_slots),
        [shaped(own, jnp.float32), own_parts, shaped((8, model_width), jnp.float32)],
        scalars=[ranks],
        whole=[unit_scale, small, second_sums],
        pieces=[*terms, [second_grad], [unit]],
    )
    proj_rows = gather_rows(proj_grad)
    outer_state, outer_mark = scatter_second(outer_state, proj_grad[:1])
    sums = sums + swap(sums, "tensor", 1)
    sums = sums + swap(sums, "tensor", 2)
    qkv_grad, near, far, attn_sums = kernel_call(
        partial(attention_back_kernel, scale),
        [
            shaped((group_rows, 3 * head_width)),
            *partial_sums,
            shaped((1, model_width), jnp.float32),
        ],
        pieces=[proj_rows, attn_weights, [qkv], [probs]],
        marks=[*outer_mark, sums],
        scratch=[pltpu.VMEM((group_rows, head_width), jnp.bfloat16)],
    )
    attn_state = scatter_first(
        kernel_call(
            attention_grad_kernel,
            weight_cuts(model_width, 4 * head_width),
            pieces=[token_rows, [qkv_grad], proj_rows, [context]],
        )
    )
    inner_state, inner_mark = scatter_second(inner_state, [attn_state[0], *outer_state[2:]])
    terms = scatter_rows(near, far, inner_mark)
    dw_outer = scatter_last(
        outer_state, write_turned, [shaped(w_outer.shape, jnp.float32)], inner_mark
    )[0]
    attn_state, attn_mark = scatter_second(attn_state, inner_mark)
    tokens_grad = kernel_call(
        partial(tokens_grad_kernel, in_slots),
        [shaped(own, jnp.float32)],
        scalars=[ranks],
        pieces=[*terms, [mix_grad]],
        marks=attn_mark,
    )[0]
    dw_inner = scatter_last(
        inner_state, write_plain, [shaped(w_inner.shape, jnp.float32)], [tokens_grad]
    )[0]
    dw_query, dw_key, dw_value, dw_proj = scatter_last(
        attn_state,
        write_attention,
        [shaped(w.shape, jnp.float32) for w in (w_query, w_key, w_value, w_proj)],
    )

    sums = sum_dp_ranks(jnp.concatenate([sums[:6], inner_sums, attn_sums], axis=0))
    return (
        layer_out,
        tokens_grad,
        dw_query,
        sums[7, :head_width],
        dw_key,
        dw_value,
        sums[7, 2 * head_width : 3 * head_width],
        dw_proj,
        sums[0],
        sums[1],
        sums[2],
        dw_inner,
        sums[6],
        dw_outer,
        sums[3],
        sums[4],
        sums[5],
    )


def solution(mesh):
    in_specs = (
        P(("dp", "tensor"), None),
        P("dp"),
        P("dp", None),
        P("dp", "tensor"),
        P("tensor"),
        P("dp", "tensor"),
        P("dp", "tensor"),
        P("tensor"),
        P("tensor", "dp"),
        P(),
        P(),
        P(),
        P("dp", "tensor"),
        P("tensor"),
        P("tensor", "dp"),
        P(),
        P(),
        P(),
        P(("dp", "tensor"), None),
    )
    out_specs = (
        P(("dp", "tensor"), None),
        P(("dp", "tensor"), None),
        P("dp", "tensor"),
        P("tensor"),
        P("dp", "tensor"),
        P("dp", "tensor"),
        P("tensor"),
        P("tensor", "dp"),
        P(),
        P(),
        P(),
        P("dp", "tensor"),
        P("tensor"),
        P("tensor", "dp"),
        P(),
        P(),
        P(),
    )
    return jax.shard_map(
        on_device, mesh=mesh, in_specs=in_specs, out_specs=out_specs, check_vma=False
    )
```

time: 874 us -> 280 us (0.32)
  waiting for transfers between devices: 607 us -> 102 us
  blocking collectives: 165 us -> 0 us
  Pallas kernels: 0 us -> 88.5 us
  starting transfers between devices: 1.08 us -> 77 us
  matrix products: 58.7 us -> 0 us
  between operations: 15.9 us -> 1.48 us
  other arithmetic: 13.4 us -> 1.99 us
    reduce_scatter x10 -> x0, waiting for transfers between devices: 493 us -> none  [the longest x1 92.6 us: on_device(): lax.psum_scatter(dw_outer, 'dp', scatter_dimension=1, tiled=True)]
    all_gather x4 -> x0, blocking collectives: 124 us -> none  [the longest x1 33.4 us: fetch_attention(): lax.all_gather(w_value, 'dp', axis=0, tiled=True)]
    all_gather x6 -> x0, waiting for transfers between devices: 112 us -> none  [the longest x1 44.2 us: fetch_inner(): lax.all_gather(w_outer, 'dp', axis=1, tiled=True)]
    ppermute x0 -> x66, waiting for transfers between devices: none -> 102 us  [swap(): lax.ppermute(block, axis_name, [(i, i ^ offset) for i in range(count)])]
    pallas_call x0 -> x27, Pallas kernels: none -> 88.5 us  [kernel_call(): pl.pallas_call(run, out_shape=flat_out, in_specs=[pl.BlockSpec(memory_spa...]
    ppermute x0 -> x66, starting transfers between devices: none -> 77 us  [swap(): lax.ppermute(block, axis_name, [(i, i ^ offset) for i in range(count)])]
    dot_general x23 -> x0, matrix products: 55.2 us -> none  [the longest x6 18.5 us: matmul(): return jnp.dot(left_side, right_side, preferred_element_type=jnp.float32)]
    psum x1 -> x0, blocking collectives: 40.8 us -> none  [on_device(): lax.psum((spread_into(db_query, model_width, head_offset), spread_into(db...]
  transfers between devices with their start and end apart: 16 -> 66, of which waited for: 14 -> 26; matrix products, arithmetic and copies ran while one was open for 5% -> 2% of each run, Pallas kernels for 0% -> 24%
where the time goes in v2:
time: 280 us; the launch traced here: 279 us
  waiting for transfers between devices  102 us (36%)
  Pallas kernels  88.5 us (32%)
  starting transfers between devices  77 us (28%)
  local copies, waits for them, and re-layouts  7.63 us (3%)
    ppermute x66, waiting for transfers between devices, swap(): lax.ppermute(block, axis_name, [(i, i ^ offset) for i in range(count)])  102 us
    pallas_call x27, Pallas kernels, kernel_call(): pl.pallas_call(run, out_shape=flat_out, in_specs=[pl.BlockSpec(memory_spa...  88.5 us
    ppermute x66, starting transfers between devices, swap(): lax.ppermute(block, axis_name, [(i, i ^ offset) for i in range(count)])  77 us
  transfers between devices with their start and end apart: 66, of which 26 were waited for; matrix products, arithmetic and copies ran while one was open for 2% of the time, Pallas kernels for 24%

profile of v2, /device:TPU:0, one launch (start us, length us, event | category | flops | bytes accessed | tf_op | source)
XLA Modules:
  0.0 278.9 jit_solution(13053634834879907532)
XLA Ops:
  2.4 3.0 %collective-permute-start.10 = (bf16[128,1024]{1,0:T(8,128)(2,1)}, bf16[128,1024]{1,0:T(8,128)(2,1)}, u32[]{:S(2)}, u32[]{:S(2)}) collective-permute-start(bf16[128,1024]{1,0:T(8,128)(2,1)} %shard_map.315.refs_8_.refs_1_.refs_4_), channel_id=1, source_target_pairs={{0,4},{4,0},{8,12},{12,8},{16,20},{20,16},{24,28},{28,24},{1,5},{5... | collective-permute-start | bytes 786440 | tf_op jit(solution)/shard_map/ppermute | solution.py:54
  5.4 3.6 %collective-permute-start.7 = (bf16[128,1024]{1,0:T(8,128)(2,1)}, bf16[128,1024]{1,0:T(8,128)(2,1)S(1)}, u32[]{:S(2)}, u32[]{:S(2)}) collective-permute-start(bf16[128,1024]{1,0:T(8,128)(2,1)} %shard_map.315.refs_8_.refs_1_.refs_4_), channel_id=1, source_target_pairs={{0,24},{4,28},{8,16},{12,20},{16,8},{20,12},{24,0},{28,4},{1,25},{... | collective-permute-start | bytes 786440 | tf_op jit(solution)/shard_map/ppermute | solution.py:54
  16.7 10.5 %collective-permute-start.11 = (bf16[128,1024]{1,0:T(8,128)(2,1)}, bf16[128,1024]{1,0:T(8,128)(2,1)}, u32[]{:S(2)}, u32[]{:S(2)}) collective-permute-start(bf16[128,1024]{1,0:T(8,128)(2,1)} %collective-permute-done.10.refs_15_.refs_8_.refs_11_), channel_id=1, source_target_pairs={{0,8},{4,12},{8,0},{12,4},{16,24},{20,28},{24,16},{28,20},{1,9},{5... | collective-permute-start | bytes 786440 | tf_op jit(solution)/shard_map/ppermute | solution.py:54
  27.2 4.1 %collective-permute-done.6.refs_1_.refs_9_.refs_2_.refs_5_ = bf16[128,1024]{1,0:T(8,128)(2,1)S(1)} collective-permute-done((bf16[128,1024]{1,0:T(8,128)(2,1)}, bf16[128,1024]{1,0:T(8,128)(2,1)S(1)}, u32[]{:S(2)}, u32[]{:S(2)}) %collective-permute-start.6) | collective-permute-done | bytes 262176 | tf_op jit(solution)/shard_map/ppermute | solution.py:54
  43.2 3.2 %collective-permute-done.20.refs_12_.refs_20_ = bf16[128,1024]{1,0:T(8,128)(2,1)} collective-permute-done((bf16[128,1024]{1,0:T(8,128)(2,1)}, bf16[128,1024]{1,0:T(8,128)(2,1)}, u32[]{:S(2)}, u32[]{:S(2)}) %collective-permute-start.20) | collective-permute-done | bytes 262176 | tf_op jit(solution)/shard_map/ppermute | solution.py:54
  46.3 3.5 %collective-permute-done.8.refs_11_.refs_4_.refs_7_ = bf16[128,1024]{1,0:T(8,128)(2,1)S(1)} collective-permute-done((bf16[128,1024]{1,0:T(8,128)(2,1)}, bf16[128,1024]{1,0:T(8,128)(2,1)S(1)}, u32[]{:S(2)}, u32[]{:S(2)}) %collective-permute-start.8) | collective-permute-done | bytes 262176 | tf_op jit(solution)/shard_map/ppermute | solution.py:54
  50.5 6.9 %shard_map.317 = (bf16[512,768]{1,0:T(8,128)(2,1)}, bf16[4,512,512]{2,1,0:T(8,128)(2,1)}, bf16[512,256]{1,0:T(8,128)(2,1)}) custom-call(s32[2]{0:T(128)} %pad_add_fusion.refs_0_, s32[1,4]{1,0:T(1,128)} %refs_1_.7, s32[4,128]{1,0:T(4,128)} %bitcast.40, f32[1,768]{1,0:T(1,128)} %broadcast_in_dim.11.refs_3_, ...), custom_call_target="tpu_custom_call" | custom-call | flops 11000000 | bytes 35000 | tf_op jit(solution)/shard_map/pallas_call | solution.py:110
  57.5 3.6 %collective-permute-done.13.refs_10_.refs_6_.refs_14_ = bf16[128,1024]{1,0:T(8,128)(2,1)S(1)} collective-permute-done((bf16[128,1024]{1,0:T(8,128)(2,1)}, bf16[128,1024]{1,0:T(8,128)(2,1)S(1)}, u32[]{:S(2)}, u32[]{:S(2)}) %collective-permute-start.13) | collective-permute-done | bytes 262176 | tf_op jit(solution)/shard_map/ppermute | solution.py:54
  61.8 3.3 %shard_map.319 = (f32[256,1024]{1,0:T(8,128)}, bf16[128,1024]{1,0:T(8,128)(2,1)}, bf16[128,1024]{1,0:T(8,128)(2,1)}, bf16[128,1024]{1,0:T(8,128)(2,1)}) custom-call(bf16[512,256]{1,0:T(8,128)(2,1)} %get-tuple-element.98.refs_0_.refs_9_, bf16[128,1024]{1,0:T(8,128)(2,1)} %shard_map.315.refs_8_.refs_1_.refs_4_, bf16[128,1024]{1,0:T(8,128)(2,1)} %copy-done.1, ...), custom_call_target="tpu_custom_call" | custom-call | flops 11000000 | bytes 35000 | tf_op jit(solution)/shard_map/pallas_call | solution.py:110
  66.3 16.1 %conditional.1 = ((f32[128,1024]{1,0:T(8,128)}, f32[128,1024]{1,0:T(8,128)}, f32[128,1]{1,0:T(8,128)S(1)}, bf16[128,1024]{1,0:T(8,128)(2,1)S(1)})) conditional(s32[]{:T(128)} %bitcast.9, () %tuple.15, (bf16[128,1024]{1,0:T(8,128)(2,1)}, bf16[128,1024]{1,0:T(8,128)(2,1)}, f32[256,1024]{1,0:T(8,128)}, f32[8,1024]{1,0:T(8,128)S(1)}, ...), branch_computations={%region_0.0_spmd, %region_1.0_spmd} | conditional | flops 22000000 | bytes 5313064 | solution.py:145
  72.0 7.1 %collective-permute-done.2.refs_3_ = bf16[128,1024]{1,0:T(8,128)(2,1)S(1)} collective-permute-done((bf16[128,1024]{1,0:T(8,128)(2,1)}, bf16[128,1024]{1,0:T(8,128)(2,1)S(1)}, u32[]{:S(2)}, u32[]{:S(2)}) %collective-permute-start.2) | collective-permute-done | bytes 262176 | tf_op jit(solution)/shard_map/cond/branch_1_fun/ppermute | solution.py:54
  87.5 4.3 %collective-permute-done.18.refs_8_.refs_16_ = bf16[128,1024]{1,0:T(8,128)(2,1)S(1)} collective-permute-done((bf16[128,1024]{1,0:T(8,128)(2,1)S(1)}, bf16[128,1024]{1,0:T(8,128)(2,1)S(1)}, u32[]{:S(2)}, u32[]{:S(2)}) %collective-permute-start.18) | collective-permute-done | bytes 262176 | tf_op jit(solution)/shard_map/ppermute | solution.py:54
  98.4 11.2 %collective-permute-done.23.refs_2_.refs_5_ = bf16[128,1024]{1,0:T(8,128)(2,1)S(1)} collective-permute-done((bf16[128,1024]{1,0:T(8,128)(2,1)}, bf16[128,1024]{1,0:T(8,128)(2,1)S(1)}, u32[]{:S(2)}, u32[]{:S(2)}) %collective-permute-start.23) | collective-permute-done | bytes 262176 | tf_op jit(solution)/shard_map/ppermute | solution.py:54
  111.5 6.2 %shard_map.320 = (bf16[512,1024]{1,0:T(8,128)(2,1)}, f32[512,1024]{1,0:T(8,128)}) custom-call(f32[1,1024]{1,0:T(1,128)} %bitcast.27, bf16[128,1024]{1,0:T(8,128)(2,1)S(1)} %get-tuple-element.102.refs_1_.refs_0_, bf16[128,1024]{1,0:T(8,128)(2,1)} %copy-done.11, bf16[128,1024]{1,0:T(8,128)(2,1)} %copy-done.12, bf16[128,1024]{1,0:T(8,128)(2,1)} %copy-done.13, ...), custom_call_target="tpu_custom_call" | custom-call | flops 11000000 | bytes 35000 | tf_op jit(solution)/shard_map/pallas_call | solution.py:110
  117.8 4.2 %shard_map.321 = (f32[256,1024]{1,0:T(8,128)}, bf16[128,1024]{1,0:T(8,128)(2,1)}, bf16[128,1024]{1,0:T(8,128)(2,1)}) custom-call(bf16[512,1024]{1,0:T(8,128)(2,1)} %get-tuple-element.103.refs_0_.refs_4_, bf16[128,1024]{1,0:T(8,128)(2,1)} %get-tuple-element.104.refs_1_.refs_4_, bf16[128,1024]{1,0:T(8,128)(2,1)} %copy-done.10, ...), custom_call_target="tpu_custom_call" | custom-call | flops 11000000 | bytes 35000 | tf_op jit(solution)/shard_map/pallas_call | solution.py:110
  126.5 8.1 %collective-permute-done.32.refs_5_ = bf16[128,1024]{1,0:T(8,128)(2,1)} collective-permute-done((bf16[128,1024]{1,0:T(8,128)(2,1)}, bf16[128,1024]{1,0:T(8,128)(2,1)}, u32[]{:S(2)}, u32[]{:S(2)}) %collective-permute-start.32) | collective-permute-done | bytes 262176 | tf_op jit(solution)/shard_map/ppermute | solution.py:54
  134.6 3.7 %shard_map.323 = (bf16[128,1024]{1,0:T(8,128)(2,1)}, f32[128,1024]{1,0:T(8,128)}, bf16[128,1024]{1,0:T(8,128)(2,1)}, f32[8,1024]{1,0:T(8,128)}) custom-call(s32[2]{0:T(128)} %pad_add_fusion.refs_0_, s32[1,4]{1,0:T(1,128)} %refs_1_.7, f32[8,1024]{1,0:T(8,128)S(1)} %get-tuple-element.96.refs_2_, f32[256,1024]{1,0:T(8,128)} %get-tuple-element.105.refs_0_.refs_3_, ...), custom_call_target="tpu_custom_call" | custom-call | flops 11000000 | bytes 35000 | tf_op jit(solution)/shard_map/pallas_call | solution.py:110
  138.9 7.2 %collective-permute-done.33.refs_1_ = bf16[128,1024]{1,0:T(8,128)(2,1)S(1)} collective-permute-done((bf16[128,1024]{1,0:T(8,128)(2,1)}, bf16[128,1024]{1,0:T(8,128)(2,1)S(1)}, u32[]{:S(2)}, u32[]{:S(2)}) %collective-permute-start.33) | collective-permute-done | bytes 262176 | tf_op jit(solution)/shard_map/ppermute | solution.py:54
  147.8 3.6 %shard_map.324 = (f32[128,1024]{1,0:T(8,128)}, bf16[256,1024]{1,0:T(8,128)(2,1)}, bf16[256,1024]{1,0:T(8,128)(2,1)}, bf16[256,1024]{1,0:T(8,128)(2,1)}, bf16[128,1024]{1,0:T(8,128)(2,1)}) custom-call(bf16[128,1024]{1,0:T(8,128)(2,1)} %get-tuple-element.113.refs_0_, bf16[128,1024]{1,0:T(8,128)(2,1)} %copy-done.14, ...), custom_call_target="tpu_custom_call" | custom-call | flops 11000000 | bytes 35000 | tf_op jit(solution)/shard_map/pallas_call | solution.py:110
  151.4 6.4 %shard_map.325 = (bf16[512,1024]{1,0:T(8,128)(2,1)}, f32[256,1024]{1,0:T(8,128)}, bf16[128,1024]{1,0:T(8,128)(2,1)}, bf16[128,1024]{1,0:T(8,128)(2,1)}, f32[1,1024]{1,0:T(1,128)}) custom-call(bf16[128,1024]{1,0:T(8,128)(2,1)} %get-tuple-element.113.refs_0_, bf16[128,1024]{1,0:T(8,128)(2,1)} %copy-done.14, bf16[128,1024]{1,0:T(8,128)(2,1)} %collective-permute-done.34.refs_2_, ...), custom_call_target="tpu_custom_call" | custom-call | flops 11000000 | bytes 35000 | tf_op jit(solution)/shard_map/pallas_call | solution.py:110
  162.6 7.8 %collective-permute-done.38.refs_6_ = bf16[128,1024]{1,0:T(8,128)(2,1)} collective-permute-done((bf16[128,1024]{1,0:T(8,128)(2,1)}, bf16[128,1024]{1,0:T(8,128)(2,1)}, u32[]{:S(2)}, u32[]{:S(2)}) %collective-permute-start.38) | collective-permute-done | bytes 262176 | tf_op jit(solution)/shard_map/ppermute | solution.py:54
  170.4 3.7 %shard_map.327 = (f32[128,1024]{1,0:T(8,128)}, bf16[128,1024]{1,0:T(8,128)(2,1)}, f32[8,1024]{1,0:T(8,128)}) custom-call(s32[2]{0:T(128)} %pad_add_fusion.refs_0_, f32[128,1]{1,0:T(8,128)S(1)} %get-tuple-element.111.refs_1_, f32[8,1024]{1,0:T(8,128)S(1)} %get-tuple-element.96.refs_2_, f32[8,1024]{1,0:T(8,128)} %get-tuple-element.112.refs_3_, ...), custom_call_target="tpu_custom_call" | custom-call | flops 11000000 | bytes 35000 | tf_op jit(solution)/shard_map/pallas_call | solution.py:110
  174.7 3.8 %shard_map.330 = (f32[128,1024]{1,0:T(8,128)}, bf16[256,1024]{1,0:T(8,128)(2,1)}, bf16[256,1024]{1,0:T(8,128)(2,1)}, bf16[256,1024]{1,0:T(8,128)(2,1)}, bf16[128,1024]{1,0:T(8,128)(2,1)}) custom-call(bf16[128,1024]{1,0:T(8,128)(2,1)S(1)} %get-tuple-element.102.refs_1_.refs_0_, bf16[128,1024]{1,0:T(8,128)(2,1)} %copy-done.11, bf16[128,1024]{1,0:T(8,128)(2,1)} %copy-done.12, ...), custom_call_target="tpu_custom_call" | custom-call | flops 11000000 | bytes 35000 | tf_op jit(solution)/shard_map/pallas_call | solution.py:110
  189.3 8.4 %shard_map.329 = (bf16[512,768]{1,0:T(8,128)(2,1)}, f32[256,1024]{1,0:T(8,128)}, bf16[128,1024]{1,0:T(8,128)(2,1)}, bf16[128,1024]{1,0:T(8,128)(2,1)}, f32[1,1024]{1,0:T(1,128)}) custom-call(bf16[128,1024]{1,0:T(8,128)(2,1)} %get-tuple-element.121.refs_4_.refs_0_.refs_5_, bf16[128,1024]{1,0:T(8,128)(2,1)} %collective-permute-done.39.refs_1_.refs_6_, ...), custom_call_target="tpu_custom_call" | custom-call | flops 11000000 | bytes 35000 | tf_op jit(solution)/shard_map/pallas_call | solution.py:110
  200.6 4.3 %shard_map.331 = (f32[128,1024]{1,0:T(8,128)}, bf16[256,1024]{1,0:T(8,128)(2,1)}, bf16[256,1024]{1,0:T(8,128)(2,1)}, bf16[256,1024]{1,0:T(8,128)(2,1)}, bf16[128,1024]{1,0:T(8,128)(2,1)}) custom-call(bf16[128,1024]{1,0:T(8,128)(2,1)S(1)} %get-tuple-element.97.refs_4_.refs_1_.refs_0_, bf16[128,1024]{1,0:T(8,128)(2,1)} %collective-permute-done.3.refs_5_.refs_1_, ...), custom_call_target="tpu_custom_call" | custom-call | flops 11000000 | bytes 35000 | tf_op jit(solution)/shard_map/pallas_call | solution.py:110
  209.0 2.9 %collective-permute-done.51.refs_6_.refs_3_ = bf16[128,1024]{1,0:T(8,128)(2,1)} collective-permute-done((bf16[128,1024]{1,0:T(8,128)(2,1)}, bf16[128,1024]{1,0:T(8,128)(2,1)}, u32[]{:S(2)}, u32[]{:S(2)}) %collective-permute-start.51) | collective-permute-done | bytes 262176 | tf_op jit(solution)/shard_map/ppermute | solution.py:54
  212.0 2.8 collective-permute-start.62
  214.7 8.9 %collective-permute-done.62 = f32[8,1024]{1,0:T(8,128)S(1)} collective-permute-done((f32[8,1024]{1,0:T(8,128)S(1)}, f32[8,1024]{1,0:T(8,128)S(1)}, u32[]{:S(2)}, u32[]{:S(2)}) %collective-permute-start.62) | collective-permute-done | bytes 32800 | tf_op jit(solution)/shard_map/ppermute | solution.py:54
  240.3 13.8 %collective-permute-start.57 = (bf16[128,1024]{1,0:T(8,128)(2,1)}, bf16[128,1024]{1,0:T(8,128)(2,1)S(1)}, u32[]{:S(2)}, u32[]{:S(2)}) collective-permute-start(bf16[128,1024]{1,0:T(8,128)(2,1)} %get-tuple-element.150), channel_id=1, source_target_pairs={{0,16},{4,20},{8,24},{12,28},{16,0},{20,4},{24,8},{28,12},{1,17},{... | collective-permute-start | bytes 786440 | tf_op jit(solution)/shard_map/ppermute | solution.py:54
  256.4 3.0 %shard_map.335.refs_5_ = f32[128,1024]{1,0:T(8,128)} custom-call(s32[2]{0:T(128)} %pad_add_fusion.refs_0_, f32[256,1024]{1,0:T(8,128)} %get-tuple-element.130.refs_0_.refs_1_, bf16[128,1024]{1,0:T(8,128)(2,1)} %collective-permute-done.46.refs_2_, bf16[128,1024]{1,0:T(8,128)(2,1)} %collective-permute-done.53.refs_3_, f32[128,1024]{1,0:T(8,128)} %get-tuple-element.143.refs_4_, ...), custom_call_target="tpu_custom_call" | custom-call | flops 11000000 | bytes 35000 | tf_op jit(solution)/shard_map/pallas_call | solution.py:110
  259.4 5.6 %collective-permute-done.64.refs_3_ = bf16[128,1024]{1,0:T(8,128)(2,1)} collective-permute-done((bf16[128,1024]{1,0:T(8,128)(2,1)}, bf16[128,1024]{1,0:T(8,128)(2,1)}, u32[]{:S(2)}, u32[]{:S(2)}) %collective-permute-start.64) | collective-permute-done | bytes 262176 | tf_op jit(solution)/shard_map/ppermute | solution.py:54
  267.3 8.5 %collective-permute-done.57.refs_3_ = bf16[128,1024]{1,0:T(8,128)(2,1)S(1)} collective-permute-done((bf16[128,1024]{1,0:T(8,128)(2,1)}, bf16[128,1024]{1,0:T(8,128)(2,1)S(1)}, u32[]{:S(2)}, u32[]{:S(2)}) %collective-permute-start.57) | collective-permute-done | bytes 262176 | tf_op jit(solution)/shard_map/ppermute | solution.py:54
  (198 shorter events, 99.8 us)
Async XLA Ops:
  9.0 22.3 %collective-permute-start.6 = (bf16[128,1024]{1,0:T(8,128)(2,1)}, bf16[128,1024]{1,0:T(8,128)(2,1)S(1)}, u32[]{:S(2)}, u32[]{:S(2)}) collective-permute-start(bf16[128,1024]{1,0:T(8,128)(2,1)} %shard_map.315.refs_8_.refs_1_.refs_4_), channel_id=1, source_target_pairs={{0,16},{4,20},{8,24},{12,28},{16,0},{20,4},{24,8},{28,12},{1,17},{... | collective-permute-start | bytes 786440 | tf_op jit(solution)/shard_map/ppermute | solution.py:54
  9.0 24.7 %collective-permute-start.12 = (bf16[128,1024]{1,0:T(8,128)(2,1)}, bf16[128,1024]{1,0:T(8,128)(2,1)}, u32[]{:S(2)}, u32[]{:S(2)}) collective-permute-start(bf16[128,1024]{1,0:T(8,128)(2,1)} %shard_map.315.refs_8_.refs_1_.refs_4_), channel_id=1, source_target_pairs={{0,8},{4,12},{8,0},{12,4},{16,24},{20,28},{24,16},{28,20},{1,9},{5... | collective-permute-start | bytes 786440 | tf_op jit(solution)/shard_map/ppermute | solution.py:54
  13.7 21.4 %collective-permute-start.4 = (bf16[128,1024]{1,0:T(8,128)(2,1)S(1)}, bf16[128,1024]{1,0:T(8,128)(2,1)}, u32[]{:S(2)}, u32[]{:S(2)}) collective-permute-start(bf16[128,1024]{1,0:T(8,128)(2,1)S(1)} %get-tuple-element.97.refs_4_.refs_1_.refs_0_), channel_id=1, source_target_pairs={{0,1},{1,0},{2,3},{3,2},{4,5},{5,4},{6,7},{7,6},{8,9},{9,8},{10,11... | collective-permute-start | bytes 786440 | tf_op jit(solution)/shard_map/ppermute | solution.py:54
  13.7 22.1 %collective-permute-start.3 = (bf16[128,1024]{1,0:T(8,128)(2,1)S(1)}, bf16[128,1024]{1,0:T(8,128)(2,1)}, u32[]{:S(2)}, u32[]{:S(2)}) collective-permute-start(bf16[128,1024]{1,0:T(8,128)(2,1)S(1)} %get-tuple-element.97.refs_4_.refs_1_.refs_0_), channel_id=1, source_target_pairs={{0,2},{1,3},{2,0},{3,1},{4,6},{5,7},{6,4},{7,5},{8,10},{9,11},{10,... | collective-permute-start | bytes 786440 | tf_op jit(solution)/shard_map/ppermute | solution.py:54
  16.7 20.1 %collective-permute-start.11 = (bf16[128,1024]{1,0:T(8,128)(2,1)}, bf16[128,1024]{1,0:T(8,128)(2,1)}, u32[]{:S(2)}, u32[]{:S(2)}) collective-permute-start(bf16[128,1024]{1,0:T(8,128)(2,1)} %collective-permute-done.10.refs_15_.refs_8_.refs_11_), channel_id=1, source_target_pairs={{0,8},{4,12},{8,0},{12,4},{16,24},{20,28},{24,16},{28,20},{1,9},{5... | collective-permute-start | bytes 786440 | tf_op jit(solution)/shard_map/ppermute | solution.py:54
  35.1 14.7 %collective-permute-start.8 = (bf16[128,1024]{1,0:T(8,128)(2,1)}, bf16[128,1024]{1,0:T(8,128)(2,1)S(1)}, u32[]{:S(2)}, u32[]{:S(2)}) collective-permute-start(bf16[128,1024]{1,0:T(8,128)(2,1)} %copy-done.1), channel_id=1, source_target_pairs={{0,4},{4,0},{8,12},{12,8},{16,20},{20,16},{24,28},{28,24},{1,5},{5... | collective-permute-start | bytes 786440 | tf_op jit(solution)/shard_map/ppermute | solution.py:54
  36.9 20.6 %collective-permute-start.14 = (bf16[128,1024]{1,0:T(8,128)(2,1)}, bf16[128,1024]{1,0:T(8,128)(2,1)}, u32[]{:S(2)}, u32[]{:S(2)}) collective-permute-start(bf16[128,1024]{1,0:T(8,128)(2,1)} %shard_map.316.refs_16_.refs_5_.refs_13_), channel_id=1, source_target_pairs={{0,24},{4,28},{8,16},{12,20},{16,8},{20,12},{24,0},{28,4},{1,25},{... | collective-permute-start | bytes 786440 | tf_op jit(solution)/shard_map/ppermute | solution.py:54
  40.7 20.4 %collective-permute-start.13 = (bf16[128,1024]{1,0:T(8,128)(2,1)}, bf16[128,1024]{1,0:T(8,128)(2,1)S(1)}, u32[]{:S(2)}, u32[]{:S(2)}) collective-permute-start(bf16[128,1024]{1,0:T(8,128)(2,1)} %shard_map.316.refs_16_.refs_5_.refs_13_), channel_id=1, source_target_pairs={{0,16},{4,20},{8,24},{12,28},{16,0},{20,4},{24,8},{28,12},{1,17},{... | collective-permute-start | bytes 786440 | tf_op jit(solution)/shard_map/ppermute | solution.py:54
  46.3 38.6 %collective-permute-start.22 = (bf16[128,1024]{1,0:T(8,128)(2,1)}, bf16[128,1024]{1,0:T(8,128)(2,1)}, u32[]{:S(2)}, u32[]{:S(2)}) collective-permute-start(bf16[128,1024]{1,0:T(8,128)(2,1)} %shard_map.316.refs_16_.refs_5_.refs_13_), channel_id=1, source_target_pairs={{0,8},{4,12},{8,0},{12,4},{16,24},{20,28},{24,16},{28,20},{1,9},{5... | collective-permute-start | bytes 786440 | tf_op jit(solution)/shard_map/ppermute | solution.py:54
  49.8 35.1 %collective-permute-start.21 = (bf16[128,1024]{1,0:T(8,128)(2,1)}, bf16[128,1024]{1,0:T(8,128)(2,1)}, u32[]{:S(2)}, u32[]{:S(2)}) collective-permute-start(bf16[128,1024]{1,0:T(8,128)(2,1)} %collective-permute-done.20.refs_12_.refs_20_), channel_id=1, source_target_pairs={{0,8},{4,12},{8,0},{12,4},{16,24},{20,28},{24,16},{28,20},{1,9},{5... | collective-permute-start | bytes 786440 | tf_op jit(solution)/shard_map/ppermute | solution.py:54
  65.2 20.9 %collective-permute-start.19 = (bf16[128,1024]{1,0:T(8,128)(2,1)}, bf16[128,1024]{1,0:T(8,128)(2,1)}, u32[]{:S(2)}, u32[]{:S(2)}) collective-permute-start(bf16[128,1024]{1,0:T(8,128)(2,1)} %collective-permute-done.14.refs_11_.refs_7_.refs_15_), channel_id=1, source_target_pairs={{0,4},{4,0},{8,12},{12,8},{16,20},{20,16},{24,28},{28,24},{1,5},{5... | collective-permute-start | bytes 786440 | tf_op jit(solution)/shard_map/ppermute | solution.py:54
  91.8 17.9 %collective-permute-start.23 = (bf16[128,1024]{1,0:T(8,128)(2,1)}, bf16[128,1024]{1,0:T(8,128)(2,1)S(1)}, u32[]{:S(2)}, u32[]{:S(2)}) collective-permute-start(bf16[128,1024]{1,0:T(8,128)(2,1)} %get-tuple-element.104.refs_1_.refs_4_), channel_id=1, source_target_pairs={{0,16},{4,20},{8,24},{12,28},{16,0},{20,4},{24,8},{28,12},{1,17},{... | collective-permute-start | bytes 786440 | tf_op jit(solution)/shard_map/ppermute | solution.py:54
  91.8 19.0 %collective-permute-start.17 = (bf16[128,1024]{1,0:T(8,128)(2,1)S(1)}, bf16[128,1024]{1,0:T(8,128)(2,1)S(1)}, u32[]{:S(2)}, u32[]{:S(2)}) collective-permute-start(bf16[128,1024]{1,0:T(8,128)(2,1)S(1)} %collective-permute-done.15.refs_2_.refs_1_), channel_id=1, source_target_pairs={{0,1},{1,0},{2,3},{3,2},{4,5},{5,4},{6,7},{7,6},{8,9},{9,8},{10,11... | collective-permute-start | bytes 786440 | tf_op jit(solution)/shard_map/ppermute | solution.py:54
  92.5 25.3 %collective-permute-start.29 = (bf16[128,1024]{1,0:T(8,128)(2,1)}, bf16[128,1024]{1,0:T(8,128)(2,1)}, u32[]{:S(2)}, u32[]{:S(2)}) collective-permute-start(bf16[128,1024]{1,0:T(8,128)(2,1)} %get-tuple-element.104.refs_1_.refs_4_), channel_id=1, source_target_pairs={{0,8},{4,12},{8,0},{12,4},{16,24},{20,28},{24,16},{28,20},{1,9},{5... | collective-permute-start | bytes 786440 | tf_op jit(solution)/shard_map/ppermute | solution.py:54
  95.8 22.0 %collective-permute-start.28 = (bf16[128,1024]{1,0:T(8,128)(2,1)}, bf16[128,1024]{1,0:T(8,128)(2,1)}, u32[]{:S(2)}, u32[]{:S(2)}) collective-permute-start(bf16[128,1024]{1,0:T(8,128)(2,1)} %collective-permute-done.27.refs_8_.refs_11_), channel_id=1, source_target_pairs={{0,8},{4,12},{8,0},{12,4},{16,24},{20,28},{24,16},{28,20},{1,9},{5... | collective-permute-start | bytes 786440 | tf_op jit(solution)/shard_map/ppermute | solution.py:54
  97.5 20.3 %collective-permute-start.26 = (bf16[128,1024]{1,0:T(8,128)(2,1)}, bf16[128,1024]{1,0:T(8,128)(2,1)}, u32[]{:S(2)}, u32[]{:S(2)}) collective-permute-start(bf16[128,1024]{1,0:T(8,128)(2,1)} %collective-permute-done.24.refs_3_.refs_6_), channel_id=1, source_target_pairs={{0,4},{4,0},{8,12},{12,8},{16,20},{20,16},{24,28},{28,24},{1,5},{5... | collective-permute-start | bytes 786440 | tf_op jit(solution)/shard_map/ppermute | solution.py:54
  158.1 21.9 %collective-permute-start.42 = (bf16[256,1024]{1,0:T(8,128)(2,1)}, bf16[256,1024]{1,0:T(8,128)(2,1)}, u32[]{:S(2)}, u32[]{:S(2)}) collective-permute-start(bf16[256,1024]{1,0:T(8,128)(2,1)} %get-tuple-element.125), channel_id=1, source_target_pairs={{0,4},{4,0},{8,12},{12,8},{16,20},{20,16},{24,28},{28,24},{1,5},{5... | collective-permute-start | bytes 1572872 | tf_op jit(solution)/shard_map/ppermute | solution.py:54
  162.3 19.7 %collective-permute-start.43 = (bf16[256,1024]{1,0:T(8,128)(2,1)}, bf16[256,1024]{1,0:T(8,128)(2,1)}, u32[]{:S(2)}, u32[]{:S(2)}) collective-permute-start(bf16[256,1024]{1,0:T(8,128)(2,1)} %get-tuple-element.127), channel_id=1, source_target_pairs={{0,8},{4,12},{8,0},{12,4},{16,24},{20,28},{24,16},{28,20},{1,9},{5... | collective-permute-start | bytes 1572872 | tf_op jit(solution)/shard_map/ppermute | solution.py:54
  178.5 21.2 %collective-permute-start.48 = (bf16[256,1024]{1,0:T(8,128)(2,1)}, bf16[256,1024]{1,0:T(8,128)(2,1)}, u32[]{:S(2)}, u32[]{:S(2)}) collective-permute-start(bf16[256,1024]{1,0:T(8,128)(2,1)} %get-tuple-element.135), channel_id=1, source_target_pairs={{0,4},{4,0},{8,12},{12,8},{16,20},{20,16},{24,28},{28,24},{1,5},{5... | collective-permute-start | bytes 1572872 | tf_op jit(solution)/shard_map/ppermute | solution.py:54
  179.5 25.5 %collective-permute-start.49 = (bf16[256,1024]{1,0:T(8,128)(2,1)}, bf16[256,1024]{1,0:T(8,128)(2,1)}, u32[]{:S(2)}, u32[]{:S(2)}) collective-permute-start(bf16[256,1024]{1,0:T(8,128)(2,1)} %get-tuple-element.137), channel_id=1, source_target_pairs={{0,8},{4,12},{8,0},{12,4},{16,24},{20,28},{24,16},{28,20},{1,9},{5... | collective-permute-start | bytes 1572872 | tf_op jit(solution)/shard_map/ppermute | solution.py:54
  186.0 19.0 %collective-permute-start.50 = (bf16[128,1024]{1,0:T(8,128)(2,1)}, bf16[128,1024]{1,0:T(8,128)(2,1)S(1)}, u32[]{:S(2)}, u32[]{:S(2)}) collective-permute-start(bf16[128,1024]{1,0:T(8,128)(2,1)} %get-tuple-element.140), channel_id=1, source_target_pairs={{0,24},{4,28},{8,16},{12,20},{16,8},{20,12},{24,0},{28,4},{1,25},{... | collective-permute-start | bytes 786440 | tf_op jit(solution)/shard_map/ppermute | solution.py:54
  188.9 23.0 %collective-permute-start.51 = (bf16[128,1024]{1,0:T(8,128)(2,1)}, bf16[128,1024]{1,0:T(8,128)(2,1)}, u32[]{:S(2)}, u32[]{:S(2)}) collective-permute-start(bf16[128,1024]{1,0:T(8,128)(2,1)} %get-tuple-element.141), channel_id=1, source_target_pairs={{0,16},{4,20},{8,24},{12,28},{16,0},{20,4},{24,8},{28,12},{1,17},{... | collective-permute-start | bytes 786440 | tf_op jit(solution)/shard_map/ppermute | solution.py:54
  199.7 15.0 %collective-permute-start.52 = (bf16[128,1024]{1,0:T(8,128)(2,1)}, bf16[128,1024]{1,0:T(8,128)(2,1)}, u32[]{:S(2)}, u32[]{:S(2)}) collective-permute-start(bf16[128,1024]{1,0:T(8,128)(2,1)} %get-tuple-element.128.refs_14_), channel_id=1, source_target_pairs={{0,4},{4,0},{8,12},{12,8},{16,20},{20,16},{24,28},{28,24},{1,5},{5... | collective-permute-start | bytes 786440 | tf_op jit(solution)/shard_map/ppermute | solution.py:54
  204.9 21.2 %collective-permute-start.47 = (bf16[128,1024]{1,0:T(8,128)(2,1)}, bf16[128,1024]{1,0:T(8,128)(2,1)S(1)}, u32[]{:S(2)}, u32[]{:S(2)}) collective-permute-start(bf16[128,1024]{1,0:T(8,128)(2,1)} %get-tuple-element.132), channel_id=1, source_target_pairs={{0,1},{1,0},{2,3},{3,2},{4,5},{5,4},{6,7},{7,6},{8,9},{9,8},{10,11... | collective-permute-start | bytes 786440 | tf_op jit(solution)/shard_map/ppermute | solution.py:54
  205.0 28.1 %collective-permute-start.54 = (bf16[256,1024]{1,0:T(8,128)(2,1)}, bf16[256,1024]{1,0:T(8,128)(2,1)}, u32[]{:S(2)}, u32[]{:S(2)}) collective-permute-start(bf16[256,1024]{1,0:T(8,128)(2,1)} %get-tuple-element.145), channel_id=1, source_target_pairs={{0,4},{4,0},{8,12},{12,8},{16,20},{20,16},{24,28},{28,24},{1,5},{5... | collective-permute-start | bytes 1572872 | tf_op jit(solution)/shard_map/ppermute | solution.py:54
  206.2 28.0 %collective-permute-start.55 = (bf16[256,1024]{1,0:T(8,128)(2,1)}, bf16[256,1024]{1,0:T(8,128)(2,1)S(1)}, u32[]{:S(2)}, u32[]{:S(2)}) collective-permute-start(bf16[256,1024]{1,0:T(8,128)(2,1)} %get-tuple-element.147), channel_id=1, source_target_pairs={{0,8},{4,12},{8,0},{12,4},{16,24},{20,28},{24,16},{28,20},{1,9},{5... | collective-permute-start | bytes 1572872 | tf_op jit(solution)/shard_map/ppermute | solution.py:54
  229.4 24.8 %collective-permute-start.53 = (bf16[128,1024]{1,0:T(8,128)(2,1)}, bf16[128,1024]{1,0:T(8,128)(2,1)}, u32[]{:S(2)}, u32[]{:S(2)}) collective-permute-start(bf16[128,1024]{1,0:T(8,128)(2,1)} %shard_map.333), channel_id=1, source_target_pairs={{0,2},{1,3},{2,0},{3,1},{4,6},{5,7},{6,4},{7,5},{8,10},{9,11},{10,... | collective-permute-start | bytes 786440 | tf_op jit(solution)/shard_map/ppermute | solution.py:54
  233.1 32.0 %collective-permute-start.65 = (bf16[128,1024]{1,0:T(8,128)(2,1)S(1)}, bf16[128,1024]{1,0:T(8,128)(2,1)}, u32[]{:S(2)}, u32[]{:S(2)}) collective-permute-start(bf16[128,1024]{1,0:T(8,128)(2,1)S(1)} %copy-done.6), channel_id=1, source_target_pairs={{0,4},{4,0},{8,12},{12,8},{16,20},{20,16},{24,28},{28,24},{1,5},{5... | collective-permute-start | bytes 786440 | tf_op jit(solution)/shard_map/ppermute | solution.py:54
  234.2 30.8 %collective-permute-start.64 = (bf16[128,1024]{1,0:T(8,128)(2,1)}, bf16[128,1024]{1,0:T(8,128)(2,1)}, u32[]{:S(2)}, u32[]{:S(2)}) collective-permute-start(bf16[128,1024]{1,0:T(8,128)(2,1)} %get-tuple-element.159), channel_id=1, source_target_pairs={{0,16},{4,20},{8,24},{12,28},{16,0},{20,4},{24,8},{28,12},{1,17},{... | collective-permute-start | bytes 786440 | tf_op jit(solution)/shard_map/ppermute | solution.py:54
  238.7 28.5 %collective-permute-start.56 = (bf16[128,1024]{1,0:T(8,128)(2,1)}, bf16[128,1024]{1,0:T(8,128)(2,1)S(1)}, u32[]{:S(2)}, u32[]{:S(2)}) collective-permute-start(bf16[128,1024]{1,0:T(8,128)(2,1)} %get-tuple-element.149), channel_id=1, source_target_pairs={{0,24},{4,28},{8,16},{12,20},{16,8},{20,12},{24,0},{28,4},{1,25},{... | collective-permute-start | bytes 786440 | tf_op jit(solution)/shard_map/ppermute | solution.py:54
  240.3 35.5 %collective-permute-start.57 = (bf16[128,1024]{1,0:T(8,128)(2,1)}, bf16[128,1024]{1,0:T(8,128)(2,1)S(1)}, u32[]{:S(2)}, u32[]{:S(2)}) collective-permute-start(bf16[128,1024]{1,0:T(8,128)(2,1)} %get-tuple-element.150), channel_id=1, source_target_pairs={{0,16},{4,20},{8,24},{12,28},{16,0},{20,4},{24,8},{28,12},{1,17},{... | collective-permute-start | bytes 786440 | tf_op jit(solution)/shard_map/ppermute | solution.py:54
  254.2 21.6 %collective-permute-start.58 = (bf16[128,1024]{1,0:T(8,128)(2,1)}, bf16[128,1024]{1,0:T(8,128)(2,1)}, u32[]{:S(2)}, u32[]{:S(2)}) collective-permute-start(bf16[128,1024]{1,0:T(8,128)(2,1)} %get-tuple-element.148.refs_5_), channel_id=1, source_target_pairs={{0,4},{4,0},{8,12},{12,8},{16,20},{20,16},{24,28},{28,24},{1,5},{5... | collective-permute-start | bytes 786440 | tf_op jit(solution)/shard_map/ppermute | solution.py:54
  (63 other events, 552.9 us)

commit v3 on v2

--- a/solution.py
+++ b/solution.py
@@ -125,17 +125,6 @@
 
 VMEM_LIMIT = 63 << 20
 QUICK = 0.01
-PARTS = 1
-
-
-def part_shapes(rows, columns):
-    return [shaped((rows // PARTS, columns))] * PARTS
-
-
-def write_parts(refs, value, columns=slice(None)):
-    rows = refs[0].shape[0]
-    for k, ref in enumerate(refs):
-        ref[:, columns] = low(value[k * rows : (k + 1) * rows])
 
 
 def region(flag, body, *operands):
@@ -145,34 +134,28 @@
     return lax.cond(flag, body, nothing, *operands)
 
 
-def swap_parts(parts, offset):
-    return [swap(p, "tensor", offset) for p in parts]
-
-
-def gather_rows(parts):
-    across = swap_parts(parts, 2)
-    beside = swap_parts(parts, 1)
-    corner = swap_parts(across, 1)
-    return [*parts, *across, *beside, *corner]
-
-
-def turn_kernel(need, near_ref, arrived_ref, out_refs):
+def join_kernel(need, own_ref, across_ref, out_ref):
+    rows = own_ref.shape[0]
     need(0)
+    out_ref[:rows] = own_ref[...]
     need(1)
-    write_parts(out_refs, near_ref[...] + wide(arrived_ref[...]))
-
-
-def scatter_rows(near, far, marks=()):
-    rows, columns = near.shape
-    half = rows // 2
-    arrived = swap_parts(far, 1)
-    turned = kernel_call(
-        turn_kernel,
-        [part_shapes(half, columns)],
-        pieces=[[part(near, half, half)], arrived[PARTS:]],
-        marks=marks,
-    )[0]
-    return [[part(near, 0, half)], arrived[:PARTS], swap_parts(turned, 2)]
+    out_ref[rows:] = across_ref[...]
+
+
+def gather_rows(piece, joined=True):
+    across = swap(piece, "tensor", 2)
+    if not joined:
+        return [piece, across, swap(piece, "tensor", 1), swap(across, "tensor", 1)]
+    rows, columns = piece.shape
+    pair = kernel_call(join_kernel, [shaped((2 * rows, columns))], pieces=[[piece], [across]])[0]
+    return [pair, swap(pair, "tensor", 1)]
+
+
+def scatter_rows(near, far):
+    half = near.shape[0] // 2
+    arrived = swap(far, "tensor", 1)
+    turned = low(near[half:] + wide(arrived[half:]))
+    return [[part(near, 0, half)], [part(arrived, 0, half)], [swap(turned, "tensor", 2)]]
 
 
 def own_sum(need, near_ref, arrived_ref, across_ref):
@@ -181,24 +164,22 @@
     return near_ref[...] + wide(arrived_ref[...]) + wide(across_ref[...])
 
 
-def gather_first(shard):
+def far_of(shard):
+    return [swap(shard, "dp", 4), swap(shard, "dp", 6)] if paired() else []
+
+
+def above_of(shard):
+    return [swap(shard, "dp", 2)] if paired() else []
+
+
+def rest_of(pieces):
+    return [swap(p, "dp", 1) for p in pieces]
+
+
+def weight_pieces(shard, far, rest, above, beside):
     if not paired():
         return [lax.all_gather(shard, "dp", axis=0, tiled=True)]
-    beside = swap(shard, "dp", 1)
-    farther, far = swap(shard, "dp", 6), swap(shard, "dp", 4)
-    above = swap(shard, "dp", 2)
-    return [shard, far, farther, swap(beside, "dp", 2), above, beside]
-
-
-def gather_rest(pieces):
-    if not paired():
-        return pieces
-    shard, far, farther, corner, above, beside = pieces
-    return [shard, far, farther, swap(far, "dp", 1), swap(farther, "dp", 1), corner, above, beside]
-
-
-def far_pieces(pieces):
-    return pieces[1:3] if paired() else pieces
+    return [shard, *far, *rest, *above, *beside]
 
 
 def weight_cuts(width, columns):
@@ -234,8 +215,9 @@
 
 
 def combine_kernel(
-    need, far_ref, far_in_ref, beside_ref, above_ref, far_out, farther_out, beside_out
+    need, far_ref, far_in_ref, beside_ref, above_ref, *rest
 ):
+    *waiting, far_out, farther_out, beside_out = rest
     block = far_out.shape[0]
     need(0)
     need(1)
@@ -243,28 +225,30 @@
     far_out[...] = low(wide(far_ref[:block]) + wide(far_in_ref[:block]))
     need(2)
     need(3)
-    beside_out[...] = low(wide(beside_ref[...]) + wide(above_ref[...]))
-
-
-def scatter_second(state, marks=()):
+    beside_out[:block] = low(wide(beside_ref[...]) + wide(above_ref[...]))
+    for number, ref in enumerate(waiting):
+        need(4 + number)
+        beside_out[(number + 1) * block : (number + 2) * block] = ref[...]
+
+
+def scatter_second(state, marks, waiting=()):
     if not paired():
-        return state, marks
+        return state, None, list(marks)
     kept, far, beside, far_in, above = state
-    block = kept.shape[0]
+    block, columns = kept.shape
     far_out, farther_out, beside_out = kernel_call(
         combine_kernel,
-        [shaped(kept.shape)] * 3,
-        pieces=[[far], [far_in], [beside], [part(above, 0, block)]],
+        [shaped(kept.shape)] * 2 + [shaped((block * (1 + len(waiting)), columns))],
+        pieces=[[far], [far_in], [beside], [part(above, 0, block)], *[[w] for w in waiting]],
         marks=marks,
     )
-    state = [
+    terms = [
         kept,
         part(above, block, block),
         swap(farther_out, "dp", 6),
         swap(far_out, "dp", 4),
-        swap(beside_out, "dp", 1),
     ]
-    return state, [beside_out]
+    return terms, beside_out, [beside_out]
 
 
 def last_kernel(write, count, need, *refs):
@@ -284,18 +268,6 @@
         pieces=[[term] for term in state],
         marks=marks,
     )
-
-
-def sum_dp_ranks(value):
-    if paired():
-        value = value + swap(value, "dp", 1)
-        farther, far = swap(value, "dp", 6), swap(value, "dp", 4)
-        return (value + swap(value, "dp", 2)) + (far + farther)
-    offset = 1
-    while offset < lax.axis_size("dp"):
-        value = value + swap(value, "dp", offset)
-        offset *= 2
-    return value
 
 
 def to_slots(array_ref, rank, in_slots):
@@ -338,20 +310,23 @@
     out_ref[:, 3 * width :] = proj_ref[...].T
 
 
+def shards_kernel(need, attn_ref, inner_ref, outer_ref, out_ref):
+    rows = attn_ref.shape[0]
+    out_ref[:rows] = attn_ref[...]
+    out_ref[rows : 2 * rows] = inner_ref[...]
+    out_ref[2 * rows :] = outer_ref[...].T
+
+
 def place_kernel(in_slots, need, ranks_ref, tokens_ref, grad_ref, small_ref, *out_refs):
-    write_parts(out_refs[0], to_slots(tokens_ref, ranks_ref[0], in_slots))
-    for ref, out_ref in zip((grad_ref, small_ref), out_refs[1:]):
+    for ref, out_ref in zip((tokens_ref, grad_ref, small_ref), out_refs):
         out_ref[...] = to_slots(ref, ranks_ref[0], in_slots)
 
 
-def pass_kernel(need, in_ref, out_ref):
-    need(0)
-    out_ref[...] = in_ref[...]
-
-
-def turn_over_kernel(need, in_ref, out_ref):
-    need(0)
-    out_ref[...] = in_ref[...].T
+def pass_kernel(need, *refs):
+    half = len(refs) // 2
+    for number, (in_ref, out_ref) in enumerate(zip(refs[:half], refs[half:])):
+        need(number)
+        out_ref[...] = in_ref[...]
 
 
 def back_into(left_ref, right_ref, inner, near_ref, far_ref):
@@ -360,7 +335,7 @@
         columns = slice(start, start + 256)
         total = matmul_nt(left_ref[...], right_ref[columns, inner])
         near_ref[:, columns] = total[:half]
-        write_parts(far_ref, total[half:], columns)
+        far_ref[:, columns] = low(total[half:])
 
 
 def attention_kernel(
@@ -415,9 +390,12 @@
         context_ref[:, columns[0]] = low(matmul(probs, value))
 
 
-def project_kernel(need, context_ref, weights_ref, shard_ref, near_ref, far_ref, out_ref):
-    need(2)
-    out_ref[...] = shard_ref[...]
+def project_kernel(need, context_ref, weights_ref, *refs):
+    passed = len(refs) // 2 - 1
+    near_ref, far_ref = refs[passed : passed + 2]
+    for number, (in_ref, out_ref) in enumerate(zip(refs[:passed], refs[passed + 2 :])):
+        need(2 + number)
+        out_ref[...] = in_ref[...]
     need(0)
     need(1)
     width = context_ref.shape[1]
@@ -449,7 +427,7 @@
     unit_ref[...] = unit
     scale_ref[...] = scale
     first_ref[...] = first
-    write_parts(low_ref, first)
+    low_ref[...] = low(first)
 
 
 def inner_kernel(need, bias_ref, rows_ref, weights_ref, active_ref, slope_ref):
@@ -508,7 +486,7 @@
     )
     second_grad_ref[...] = second_grad
     rounded = low(second_grad)
-    write_parts(low_ref, rounded)
+    low_ref[...] = rounded
     sums_ref[0:1] = jnp.sum(wide(rounded), axis=0, keepdims=True)
     sums_ref[1:2] = jnp.sum(cot * unit, axis=0, keepdims=True)
     sums_ref[2:3] = jnp.sum(cot, axis=0, keepdims=True)
@@ -563,7 +541,7 @@
     )
     mix_ref[...] = mix
     rounded = low(mix)
-    write_parts(low_ref, rounded)
+    low_ref[...] = rounded
     sums = jnp.concatenate(
         [
             jnp.sum(wide(rounded), axis=0, keepdims=True),
@@ -632,6 +610,16 @@
     from_slots(total, ranks_ref[0], in_slots, out_ref)
 
 
+def finish_kernel(need, sums_ref, arrived_ref, *out_refs):
+    *row_refs, query_ref, value_ref = out_refs
+    for k, ref in enumerate(row_refs):
+        ref[...] = sums_ref[k, :] + arrived_ref[k, :]
+    width = query_ref.shape[0]
+    k = len(row_refs)
+    query_ref[...] = sums_ref[k, :width] + arrived_ref[k, :width]
+    value_ref[...] = sums_ref[k, 2 * width : 3 * width] + arrived_ref[k, 2 * width : 3 * width]
+
+
 def write_turned(total, out_ref):
     out_ref[...] = total.T
 
@@ -680,33 +668,52 @@
     inner_width = b_inner.shape[0]
     scale = HEAD_DIM ** (-0.5)
     own = (piece_rows, model_width)
-    own_parts = part_shapes(*own)
-    partial_sums = [shaped((half_rows, model_width), jnp.float32), own_parts + own_parts]
+    partial_sums = [shaped((half_rows, model_width), jnp.float32), shaped((half_rows, model_width))]
 
     attn_shard = kernel_call(
         prepare_kernel,
         [shaped((shard_rows, 4 * head_width))],
         whole=[w_query, w_key, w_value, w_proj],
     )[0]
-    attn_pieces = gather_first(attn_shard)
+    shards = kernel_call(
+        shards_kernel,
+        [shaped((3 * shard_rows, 4 * head_width))],
+        whole=[attn_shard, w_inner, w_outer],
+    )[0]
+    attn_beside, inner_beside, outer_beside = [], [], []
+    if in_slots:
+        beside = swap(shards, "dp", 1)
+        attn_beside, inner_beside, outer_beside = (
+            [part(beside, k * shard_rows, shard_rows)] for k in range(3)
+        )
+    attn_far = far_of(attn_shard)
+    attn_above = above_of(attn_shard)
     small = jnp.stack(
         [b_proj, gain_attn, shift_attn, b_outer, gain_ffn, shift_ffn, b_proj, b_proj]
     )
-    tokens, out_grad, small = kernel_call(
-        partial(place_kernel, in_slots),
-        [own_parts, shaped(own), shaped(small.shape, jnp.float32)],
-        whole=[tokens, out_grad, small],
-        scalars=[ranks],
-    )
-    token_rows = gather_rows(tokens)
-    outer_shard = kernel_call(
-        turn_over_kernel, [shaped(w_outer.shape[::-1])], pieces=[[w_outer]], marks=tokens[:1]
-    )[0]
-    inner_shard = kernel_call(
-        pass_kernel, [shaped(w_inner.shape)], pieces=[[w_inner]], marks=far_pieces(attn_pieces)
-    )[0]
-    inner_pieces = gather_first(inner_shard)
-    attn_weights = gather_rest(attn_pieces)
+
+    def tokens_in_part(tokens, out_grad, small):
+        tokens, out_grad, small = kernel_call(
+            partial(place_kernel, in_slots),
+            [shaped(own), shaped(own), shaped(small.shape, jnp.float32)],
+            whole=[tokens, out_grad, small],
+            scalars=[ranks],
+        )
+        return tokens, out_grad, small, gather_rows(tokens)
+
+    tokens, out_grad, small, token_rows = region(flag, tokens_in_part, tokens, out_grad, small)
+    joined = [shaped((3 * shard_rows, model_width))] if in_slots else []
+    inner_shard, *attn_joined = kernel_call(
+        pass_kernel,
+        [shaped(w_inner.shape), *joined],
+        pieces=[[part(shards, shard_rows, shard_rows)]] + [attn_far + attn_above] * in_slots,
+        marks=[tokens],
+    )
+    attn_weights = weight_pieces(
+        attn_shard, attn_far, rest_of(attn_joined), attn_above, attn_beside
+    )
+    inner_far = far_of(inner_shard)
+    inner_above = above_of(inner_shard)
     qkv_bias = jnp.concatenate([b_query, jnp.zeros_like(b_query), b_value])[None, :]
     qkv, probs, context = kernel_call(
         partial(attention_kernel, scale),
@@ -721,14 +728,17 @@
         marks=[inner_shard],
         scratch=[pltpu.VMEM((group_rows, group_rows), jnp.float32)],
     )
-    near, far, outer_shard = kernel_call(
+    near, far, outer_shard, *inner_joined = kernel_call(
         project_kernel,
-        [*partial_sums, shaped(outer_shard.shape)],
-        pieces=[[context], attn_weights, [outer_shard]],
-        marks=far_pieces(inner_pieces),
-    )
-    outer_pieces = gather_first(outer_shard)
-    inner_weights = gather_rest(inner_pieces)
+        [*partial_sums, shaped(inner_shard.shape), *joined],
+        pieces=[[context], attn_weights, [part(shards, 2 * shard_rows, shard_rows)]]
+        + [inner_far + inner_above] * in_slots,
+    )
+    inner_weights = weight_pieces(
+        inner_shard, inner_far, rest_of(inner_joined), inner_above, inner_beside
+    )
+    outer_far = far_of(outer_shard)
+    outer_corner = above_of(beside[2 * shard_rows :]) if in_slots else []
     def first_part(near, far, tokens, small):
         terms = scatter_rows(near, far)
         return kernel_call(
@@ -737,20 +747,37 @@
                 shaped(own, jnp.float32),
                 shaped(own, jnp.float32),
                 shaped((piece_rows, 1), jnp.float32),
-                own_parts,
+                shaped(own),
             ],
             whole=[small],
-            pieces=[*terms, tokens],
+            pieces=[*terms, [tokens]],
         )
 
     first, unit, unit_scale, first_low = region(flag, first_part, near, far, tokens, small)
-    outer_weights = gather_rest(outer_pieces)
-    norm_rows = gather_rows(first_low)
-    active, slope = kernel_call(
-        inner_kernel,
-        [shaped((group_rows, inner_width)), shaped((group_rows, inner_width), jnp.float32)],
-        whole=[b_inner[None, :]],
-        pieces=[norm_rows, inner_weights],
+    outer_weights = weight_pieces(
+        outer_shard,
+        outer_far,
+        rest_of(outer_far),
+        outer_corner + above_of(outer_shard),
+        outer_beside,
+    )
+
+    def inner_part(first_low, arrived, marks):
+        norm_rows = gather_rows(first_low)
+        return norm_rows, kernel_call(
+            inner_kernel,
+            [shaped((group_rows, inner_width)), shaped((group_rows, inner_width), jnp.float32)],
+            whole=[b_inner[None, :]],
+            pieces=[norm_rows, arrived + inner_beside],
+            marks=marks,
+        )
+
+    norm_rows, (active, slope) = region(
+        flag,
+        inner_part,
+        first_low,
+        inner_weights[: len(inner_weights) - len(inner_beside)],
+        outer_far + outer_corner,
     )
     near, far = kernel_call(
         outer_kernel, partial_sums, pieces=[[active], outer_weights]
@@ -761,7 +788,7 @@
         [
             shaped(own),
             shaped(own, jnp.float32),
-            own_parts,
+            shaped(own),
             shaped((8, model_width), jnp.float32),
         ],
         scalars=[ranks, seq_lengths],
@@ -769,7 +796,7 @@
         pieces=[*terms, [first], [out_grad]],
     )
 
-    branch_rows = gather_rows(branch_grad)
+    branch_rows = gather_rows(branch_grad, joined=False)
     outer_cuts = kernel_call(
         single_grad_kernel,
         weight_cuts(model_width, inner_width),
@@ -786,36 +813,56 @@
         pieces=[branch_rows, outer_weights, [slope], inner_weights],
         marks=[outer_cuts[0]],
     )
-    terms = scatter_rows(near, far)
-    inner_state = scatter_first(
-        kernel_call(
+
+    def first_back_part(near, far, norm_rows, hidden_grad, rest):
+        terms = scatter_rows(near, far)
+        inner_cuts = kernel_call(
             single_grad_kernel,
             weight_cuts(model_width, inner_width),
             pieces=[norm_rows, [hidden_grad]],
-            marks=[outer_state[0], terms[1][0]],
+            marks=[terms[1][0][0]],
         )
-    )
-    mix_grad, proj_grad, sums = kernel_call(
-        partial(first_back_kernel, in_slots),
-        [shaped(own, jnp.float32), own_parts, shaped((8, model_width), jnp.float32)],
-        scalars=[ranks],
-        whole=[unit_scale, small, second_sums],
-        pieces=[*terms, [second_grad], [unit]],
-    )
-    proj_rows = gather_rows(proj_grad)
-    outer_state, outer_mark = scatter_second(outer_state, proj_grad[:1])
-    sums = sums + swap(sums, "tensor", 1)
-    sums = sums + swap(sums, "tensor", 2)
-    qkv_grad, near, far, attn_sums = kernel_call(
-        partial(attention_back_kernel, scale),
-        [
-            shaped((group_rows, 3 * head_width)),
-            *partial_sums,
-            shaped((1, model_width), jnp.float32),
-        ],
-        pieces=[proj_rows, attn_weights, [qkv], [probs]],
-        marks=[*outer_mark, sums],
-        scratch=[pltpu.VMEM((group_rows, head_width), jnp.bfloat16)],
+        second_grad, unit, *small_operands = rest
+        return inner_cuts, kernel_call(
+            partial(first_back_kernel, in_slots),
+            [shaped(own, jnp.float32), shaped(own), shaped((8, model_width), jnp.float32)],
+            scalars=[ranks],
+            whole=small_operands,
+            pieces=[*terms, [second_grad], [unit]],
+            marks=inner_cuts[:1],
+        )
+
+    inner_cuts, (mix_grad, proj_grad, sums) = region(
+        flag,
+        first_back_part,
+        near,
+        far,
+        norm_rows,
+        hidden_grad,
+        [second_grad, unit, unit_scale, small, second_sums],
+    )
+    outer_terms, outer_beside, outer_mark = scatter_second(outer_state, [proj_grad])
+    inner_state = scatter_first(inner_cuts)
+
+    def attention_back_part(proj_grad, qkv, probs, marks):
+        proj_rows = gather_rows(proj_grad)
+        return (
+            proj_rows,
+            kernel_call(
+                partial(attention_back_kernel, scale),
+                [
+                    shaped((group_rows, 3 * head_width)),
+                    *partial_sums,
+                    shaped((1, model_width), jnp.float32),
+                ],
+                pieces=[proj_rows, attn_weights, [qkv], [probs]],
+                marks=marks,
+                scratch=[pltpu.VMEM((group_rows, head_width), jnp.bfloat16)],
+            ),
+        )
+
+    proj_rows, (qkv_grad, near, far, attn_sums) = region(
+        flag, attention_back_part, proj_grad, qkv, probs, outer_mark
     )
     attn_state = scatter_first(
         kernel_call(
@@ -824,47 +871,79 @@
             pieces=[token_rows, [qkv_grad], proj_rows, [context]],
         )
     )
-    inner_state, inner_mark = scatter_second(inner_state, [attn_state[0], *outer_state[2:]])
-    terms = scatter_rows(near, far, inner_mark)
+    inner_terms, inner_beside, _ = scatter_second(
+        inner_state, [attn_state[0], *outer_terms[2:]]
+    )
+
+    offsets = [1 << bit for bit in range(lax.axis_size("dp").bit_length() - 1)]
+
+    def sums_part(sums, inner_sums, attn_sums, mark):
+        sums = sums + swap(sums, "tensor", 1)
+        sums = sums + swap(sums, "tensor", 2)
+        sums = jnp.concatenate([sums[:6], inner_sums, attn_sums], axis=0)
+        for offset in offsets[:-1]:
+            sums = sums + swap(sums, "dp", offset)
+        return sums
+
+    sums = region(flag, sums_part, sums, inner_sums, attn_sums, attn_state[0])
+    waiting = [outer_beside, inner_beside] if in_slots else []
+    attn_terms, beside, attn_mark = scatter_second(
+        attn_state, [sums, *inner_terms[2:]], waiting
+    )
+    besides = [[]] * 3
+    if in_slots:
+        besides = swap(beside, "dp", 1)
+        besides = [[part(besides, k * shard_rows, shard_rows)] for k in range(3)]
+
+    def tokens_part(near, far, mix_grad, mark):
+        terms = scatter_rows(near, far)
+        return kernel_call(
+            partial(tokens_grad_kernel, in_slots),
+            [shaped(own, jnp.float32)],
+            scalars=[ranks],
+            pieces=[*terms, [mix_grad]],
+            marks=[mark],
+        )[0]
+
+    tokens_grad = region(flag, tokens_part, near, far, mix_grad, attn_mark[0])
+    *shared, db_inner, db_query, db_value = kernel_call(
+        finish_kernel,
+        [shaped((model_width,), jnp.float32)] * 6
+        + [shaped(b.shape, jnp.float32) for b in (b_inner, b_query, b_value)],
+        whole=[sums, swap(sums, "dp", offsets[-1])],
+        marks=[tokens_grad],
+    )
+    dw_query, dw_key, dw_value, dw_proj = scatter_last(
+        attn_terms + besides[0],
+        write_attention,
+        [shaped(w.shape, jnp.float32) for w in (w_query, w_key, w_value, w_proj)],
+        [tokens_grad],
+    )
     dw_outer = scatter_last(
-        outer_state, write_turned, [shaped(w_outer.shape, jnp.float32)], inner_mark
-    )[0]
-    attn_state, attn_mark = scatter_second(attn_state, inner_mark)
-    tokens_grad = kernel_call(
-        partial(tokens_grad_kernel, in_slots),
-        [shaped(own, jnp.float32)],
-        scalars=[ranks],
-        pieces=[*terms, [mix_grad]],
-        marks=attn_mark,
+        outer_terms + besides[1], write_turned, [shaped(w_outer.shape, jnp.float32)], [tokens_grad]
     )[0]
     dw_inner = scatter_last(
-        inner_state, write_plain, [shaped(w_inner.shape, jnp.float32)], [tokens_grad]
+        inner_terms + besides[2], write_plain, [shaped(w_inner.shape, jnp.float32)], [tokens_grad]
     )[0]
-    dw_query, dw_key, dw_value, dw_proj = scatter_last(
-        attn_state,
-        write_attention,
-        [shaped(w.shape, jnp.float32) for w in (w_query, w_key, w_value, w_proj)],
-    )
-
-    sums = sum_dp_ranks(jnp.concatenate([sums[:6], inner_sums, attn_sums], axis=0))
+    db_proj, dgain_attn, dshift_attn, db_outer, dgain_ffn, dshift_ffn = shared
     return (
         layer_out,
         tokens_grad,
         dw_query,
-        sums[7, :head_width],
+        db_query,
         dw_key,
         dw_value,
-        sums[7, 2 * head_width : 3 * head_width],
+        db_value,
         dw_proj,
-        sums[0],
-        sums[1],
-        sums[2],
+        db_proj,
+        dgain_attn,
+        dshift_attn,
         dw_inner,
-        sums[6],
+        db_inner,
         dw_outer,
-        sums[3],
-        sums[4],
-        sums[5],
+        db_outer,
+        dgain_ffn,
+        dshift_ffn,
     )
 
 

time: 280 us -> 264 us (0.943)
  starting transfers between devices: 77 us -> 54.8 us
  waiting for transfers between devices: 102 us -> 107 us
  other arithmetic: 1.99 us -> 5.45 us
    ppermute x66 -> x50, starting transfers between devices: 77 us -> 54.8 us  [swap(): lax.ppermute(block, axis_name, [(i, i ^ offset) for i in range(count)])]
    convert_element_type x0 -> x4, other arithmetic: none -> 5.31 us  [low(): return value.astype(jnp.bfloat16)]
    ppermute x66 -> x50, waiting for transfers between devices: 102 us -> 107 us  [swap(): lax.ppermute(block, axis_name, [(i, i ^ offset) for i in range(count)])]
  transfers between devices with their start and end apart: 66 -> 50, of which waited for: 26 -> 25; matrix products, arithmetic and copies ran while one was open for 2% -> 2% of each run, Pallas kernels for 24% -> 25%
where the time goes in v3:
time: 264 us; the launch traced here: 263 us
  waiting for transfers between devices  107 us (41%)
  Pallas kernels  87.3 us (33%)
  starting transfers between devices  54.8 us (21%)
  local copies, waits for them, and re-layouts  7.26 us (3%)
  other arithmetic  5.45 us (2%)
    ppermute x50, waiting for transfers between devices, swap(): lax.ppermute(block, axis_name, [(i, i ^ offset) for i in range(count)])  107 us
    pallas_call x27, Pallas kernels, kernel_call(): pl.pallas_call(run, out_shape=flat_out, in_specs=[pl.BlockSpec(memory_spa...  87.3 us
    ppermute x50, starting transfers between devices, swap(): lax.ppermute(block, axis_name, [(i, i ^ offset) for i in range(count)])  54.8 us
    convert_element_type x4, other arithmetic, low(): return value.astype(jnp.bfloat16)  5.31 us
  transfers between devices with their start and end apart: 50, of which 25 were waited for; matrix products, arithmetic and copies ran while one was open for 2% of the time, Pallas kernels for 25%

profile of v3, /device:TPU:0, one launch (start us, length us, event | category | flops | bytes accessed | tf_op | source)
XLA Modules:
  0.0 263.2 jit_solution(11542610308706455487)
XLA Ops:
  12.0 13.7 %conditional.7 = (bf16[128,1024]{1,0:T(8,128)(2,1)}, bf16[128,1024]{1,0:T(8,128)(2,1)}, f32[8,1024]{1,0:T(8,128)S(1)}, bf16[256,1024]{1,0:T(8,128)(2,1)}, bf16[256,1024]{1,0:T(8,128)(2,1)}) conditional(s32[]{:T(128)} %bitcast.3, () %tuple.59, (s32[2]{0:T(128)S(1)}, bf16[128,1024]{1,0:T(8,128)(2,1)}, bf16[128,1024]{1,0:T(8,128)(2,1)}, ...), branch_computations={%region_0.0_spmd, %region_1.0_spmd} | conditional | flops 22000000 | bytes 3215848 | solution.py:134
  15.5 6.0 %collective-permute-done.refs_1_ = bf16[128,1024]{1,0:T(8,128)(2,1)} collective-permute-done((bf16[128,1024]{1,0:T(8,128)(2,1)}, bf16[128,1024]{1,0:T(8,128)(2,1)}, u32[]{:S(2)}, u32[]{:S(2)}) %collective-permute-start) | collective-permute-done | bytes 262176 | tf_op jit(solution)/shard_map/cond/branch_1_fun/ppermute | solution.py:54
  25.7 5.6 %collective-permute-done.16.refs_1_.refs_7_.refs_2_ = bf16[128,1024]{1,0:T(8,128)(2,1)} collective-permute-done((bf16[128,1024]{1,0:T(8,128)(2,1)}, bf16[128,1024]{1,0:T(8,128)(2,1)}, u32[]{:S(2)}, u32[]{:S(2)}) %collective-permute-start.16) | collective-permute-done | bytes 262176 | tf_op jit(solution)/shard_map/ppermute | solution.py:54
  39.2 13.1 %collective-permute-done.19.refs_9_.refs_4_ = bf16[384,1024]{1,0:T(8,128)(2,1)} collective-permute-done((bf16[384,1024]{1,0:T(8,128)(2,1)}, bf16[384,1024]{1,0:T(8,128)(2,1)}, u32[]{:S(2)}, u32[]{:S(2)}) %collective-permute-start.19) | collective-permute-done | bytes 786464 | tf_op jit(solution)/shard_map/ppermute | solution.py:54
  52.3 6.9 %shard_map.320 = (bf16[512,768]{1,0:T(8,128)(2,1)}, bf16[4,512,512]{2,1,0:T(8,128)(2,1)}, bf16[512,256]{1,0:T(8,128)(2,1)}) custom-call(s32[2]{0:T(128)S(1)} %pad_add_fusion.refs_0_, s32[1,4]{1,0:T(1,128)} %refs_1_.7, s32[4,128]{1,0:T(4,128)} %bitcast.21, f32[1,768]{1,0:T(1,128)} %broadcast_in_dim.10.refs_3_, ...), custom_call_target="tpu_custom_call" | custom-call | flops 11000000 | bytes 35000 | tf_op jit(solution)/shard_map/pallas_call | solution.py:110
  60.4 3.6 %shard_map.321 = (f32[256,1024]{1,0:T(8,128)}, bf16[256,1024]{1,0:T(8,128)(2,1)}, bf16[128,1024]{1,0:T(8,128)(2,1)}, bf16[384,1024]{1,0:T(8,128)(2,1)}) custom-call(bf16[512,256]{1,0:T(8,128)(2,1)} %get-tuple-element.268.refs_0_.refs_5_, bf16[128,1024]{1,0:T(8,128)(2,1)} %shard_map.317.refs_0_.refs_6_.refs_1_, ...), custom_call_target="tpu_custom_call" | custom-call | flops 11000000 | bytes 35000 | tf_op jit(solution)/shard_map/pallas_call | solution.py:110
  69.7 15.8 %conditional.8 = ((f32[128,1024]{1,0:T(8,128)}, f32[128,1024]{1,0:T(8,128)}, f32[128,1]{1,0:T(8,128)S(1)}, bf16[128,1024]{1,0:T(8,128)(2,1)})) conditional(s32[]{:T(128)} %bitcast.3, () %tuple.62, (bf16[256,1024]{1,0:T(8,128)(2,1)}, f32[256,1024]{1,0:T(8,128)}, f32[8,1024]{1,0:T(8,128)S(1)}, bf16[128,1024]{1,0:T(8,128)(2,1)}) %tuple.63), branch_computations={%region_2.0_spmd, %region_3.0_spmd} | conditional | flops 11393216 | bytes 7375176 | solution.py:134
  75.3 6.9 %collective-permute-done.7.refs_3_ = bf16[128,1024]{1,0:T(8,128)(2,1)S(1)} collective-permute-done((bf16[128,1024]{1,0:T(8,128)(2,1)S(1)}, bf16[128,1024]{1,0:T(8,128)(2,1)S(1)}, u32[]{:S(2)}, u32[]{:S(2)}) %collective-permute-start.7) | collective-permute-done | bytes 262176 | tf_op jit(solution)/shard_map/cond/branch_1_fun/ppermute | solution.py:54
  87.7 17.1 %conditional.9 = (bf16[256,1024]{1,0:T(8,128)(2,1)}, bf16[256,1024]{1,0:T(8,128)(2,1)}, bf16[512,1024]{1,0:T(8,128)(2,1)}, f32[512,1024]{1,0:T(8,128)}) conditional(s32[]{:T(128)} %bitcast.3, () %tuple.61, (bf16[128,1024]{1,0:T(8,128)(2,1)}, f32[1024]{0:T(1024)S(1)}, bf16[128,1024]{1,0:T(8,128)(2,1)}, bf16[128,1024]{1,0:T(8,128)(2,1)}, ...), branch_computations={%region_4.0_spmd, %region_5.0_spmd} | conditional | flops 22000000 | bytes 4194346 | solution.py:134
  89.3 5.8 %collective-permute-done.2.refs_1_ = bf16[128,1024]{1,0:T(8,128)(2,1)} collective-permute-done((bf16[128,1024]{1,0:T(8,128)(2,1)}, bf16[128,1024]{1,0:T(8,128)(2,1)}, u32[]{:S(2)}, u32[]{:S(2)}) %collective-permute-start.2) | collective-permute-done | bytes 262176 | tf_op jit(solution)/shard_map/cond/branch_1_fun/ppermute | solution.py:54
  99.2 5.4 %branch_1_fun.14 = (bf16[512,1024]{1,0:T(8,128)(2,1)}, f32[512,1024]{1,0:T(8,128)}) custom-call(f32[1,1024]{1,0:T(1,128)S(1)} %bitcast.15, bf16[256,1024]{1,0:T(8,128)(2,1)} %branch_1_fun.13.refs_1_, bf16[256,1024]{1,0:T(8,128)(2,1)} %collective-permute-done.3.refs_2_, bf16[128,1024]{1,0:T(8,128)(2,1)} %get-tuple-element.115.refs_3_, ...), custom_call_target="tpu_custom_call" | custom-call | flops 11000000 | bytes 35000 | tf_op jit(solution)/shard_map/cond/branch_1_fun/pallas_call | solution.py:110
  104.8 4.3 %shard_map.322 = (f32[256,1024]{1,0:T(8,128)}, bf16[256,1024]{1,0:T(8,128)(2,1)}) custom-call(bf16[512,1024]{1,0:T(8,128)(2,1)} %get-tuple-element.274.refs_0_.refs_4_, bf16[128,1024]{1,0:T(8,128)(2,1)} %get-tuple-element.273.refs_1_.refs_4_, bf16[128,1024]{1,0:T(8,128)(2,1)} %collective-permute-done.25.refs_2_.refs_5_, ...), custom_call_target="tpu_custom_call" | custom-call | flops 11000000 | bytes 35000 | tf_op jit(solution)/shard_map/pallas_call | solution.py:110
  114.8 7.0 %collective-permute-done.32.refs_5_ = bf16[128,1024]{1,0:T(8,128)(2,1)} collective-permute-done((bf16[128,1024]{1,0:T(8,128)(2,1)S(1)}, bf16[128,1024]{1,0:T(8,128)(2,1)}, u32[]{:S(2)}, u32[]{:S(2)}) %collective-permute-start.32) | collective-permute-done | bytes 262176 | tf_op jit(solution)/shard_map/ppermute | solution.py:54
  121.7 3.7 %shard_map.323 = (bf16[128,1024]{1,0:T(8,128)(2,1)}, f32[128,1024]{1,0:T(8,128)}, bf16[128,1024]{1,0:T(8,128)(2,1)}, f32[8,1024]{1,0:T(8,128)S(1)}) custom-call(s32[2]{0:T(128)S(1)} %pad_add_fusion.refs_0_, s32[1,4]{1,0:T(1,128)} %refs_1_.7, f32[8,1024]{1,0:T(8,128)S(1)} %get-tuple-element.262.refs_2_, f32[256,1024]{1,0:T(8,128)} %get-tuple-element.275.refs_3_, ...), custom_call_target="tpu_custom_call" | custom-call | flops 11000000 | bytes 35000 | tf_op jit(solution)/shard_map/pallas_call | solution.py:110
  127.0 6.2 %collective-permute-done.33.refs_1_ = bf16[128,1024]{1,0:T(8,128)(2,1)S(1)} collective-permute-done((bf16[128,1024]{1,0:T(8,128)(2,1)}, bf16[128,1024]{1,0:T(8,128)(2,1)S(1)}, u32[]{:S(2)}, u32[]{:S(2)}) %collective-permute-start.33) | collective-permute-done | bytes 262176 | tf_op jit(solution)/shard_map/ppermute | solution.py:54
  135.6 3.6 %shard_map.324 = (f32[128,1024]{1,0:T(8,128)}, bf16[256,1024]{1,0:T(8,128)(2,1)}, bf16[256,1024]{1,0:T(8,128)(2,1)}, bf16[256,1024]{1,0:T(8,128)(2,1)}, bf16[128,1024]{1,0:T(8,128)(2,1)}) custom-call(bf16[128,1024]{1,0:T(8,128)(2,1)} %get-tuple-element.280.refs_0_, bf16[128,1024]{1,0:T(8,128)(2,1)} %copy-done.7, ...), custom_call_target="tpu_custom_call" | custom-call | flops 11000000 | bytes 35000 | tf_op jit(solution)/shard_map/pallas_call | solution.py:110
  142.5 6.3 %shard_map.325 = (bf16[512,1024]{1,0:T(8,128)(2,1)}, f32[256,1024]{1,0:T(8,128)}, bf16[256,1024]{1,0:T(8,128)(2,1)}, f32[1,1024]{1,0:T(1,128)S(1)}) custom-call(bf16[128,1024]{1,0:T(8,128)(2,1)} %get-tuple-element.280.refs_0_, bf16[128,1024]{1,0:T(8,128)(2,1)} %copy-done.7, bf16[128,1024]{1,0:T(8,128)(2,1)} %collective-permute-done.34.refs_2_, ...), custom_call_target="tpu_custom_call" | custom-call | flops 11000000 | bytes 35000 | tf_op jit(solution)/shard_map/pallas_call | solution.py:110
  148.8 16.9 %conditional.10 = (f32[128,1024]{1,0:T(8,128)}, bf16[256,1024]{1,0:T(8,128)(2,1)}, bf16[256,1024]{1,0:T(8,128)(2,1)}, bf16[256,1024]{1,0:T(8,128)(2,1)}, bf16[12...) conditional(s32[]{:T(128)} %bitcast.3, () %tuple.67, ...), branch_computations={%region_6.0_spmd, %region_7.0_spmd} | conditional | flops 22393216 | bytes 6361628 | solution.py:134
  155.2 3.7 %branch_1_fun.15 = (f32[128,1024]{1,0:T(8,128)}, bf16[256,1024]{1,0:T(8,128)(2,1)}, bf16[256,1024]{1,0:T(8,128)(2,1)}, bf16[256,1024]{1,0:T(8,128)(2,1)}, bf16[128,1024]{1,0:T(8,128)(2,1)}) custom-call(bf16[256,1024]{1,0:T(8,128)(2,1)} %get-tuple-element.126.refs_0_, bf16[256,1024]{1,0:T(8,128)(2,1)} %get-tuple-element.127.refs_1_, ...), custom_call_target="tpu_custom_call" | custom-call | flops 11000000 | bytes 35000 | tf_op jit(solution)/shard_map/cond/branch_1_fun/pallas_call | solution.py:110
  158.8 3.5 %collective-permute-done.9.refs_6_ = bf16[128,1024]{1,0:T(8,128)(2,1)} collective-permute-done((bf16[128,1024]{1,0:T(8,128)(2,1)}, bf16[128,1024]{1,0:T(8,128)(2,1)}, u32[]{:S(2)}, u32[]{:S(2)}) %collective-permute-start.9) | collective-permute-done | bytes 262176 | tf_op jit(solution)/shard_map/cond/branch_1_fun/ppermute | solution.py:54
  162.3 3.4 %branch_1_fun.16 = (f32[128,1024]{1,0:T(8,128)}, bf16[128,1024]{1,0:T(8,128)(2,1)}, f32[8,1024]{1,0:T(8,128)S(1)}) custom-call(s32[2]{0:T(128)S(1)} %get-tuple-element.135.refs_0_, f32[128,1]{1,0:T(8,128)S(1)} %get-tuple-element.136.refs_1_, f32[8,1024]{1,0:T(8,128)S(1)} %get-tuple-element.137.refs_2_, f32[8,1024]{1,0:T(8,128)S(1)} %get-tuple-element.138.refs_3_, ...), custom_call_target="tpu_custom_call" | custom-call | flops 11000000 | bytes 35000 | tf_op jit(solution)/shard_map/cond/branch_1_fun/pallas_call | solution.py:110
  172.2 19.2 %conditional.11 = (bf16[256,1024]{1,0:T(8,128)(2,1)}, bf16[256,1024]{1,0:T(8,128)(2,1)}, bf16[512,768]{1,0:T(8,128)(2,1)}, f32[256,1024]{1,0:T(8,128)}, bf16[256...) conditional(s32[]{:T(128)} %bitcast.3, () %tuple.66, (bf16[128,1024]{1,0:T(8,128)(2,1)}, bf16[128,1024]{1,0:T(8,128)(2,1)}, ...), branch_computations={%region_8.0_spmd, %region_9.0_spmd} | conditional | flops 22000000 | bytes 3412032 | solution.py:134
  173.7 5.2 %collective-permute-done.4.refs_1_ = bf16[128,1024]{1,0:T(8,128)(2,1)} collective-permute-done((bf16[128,1024]{1,0:T(8,128)(2,1)}, bf16[128,1024]{1,0:T(8,128)(2,1)}, u32[]{:S(2)}, u32[]{:S(2)}) %collective-permute-start.4) | collective-permute-done | bytes 262176 | tf_op jit(solution)/shard_map/cond/branch_1_fun/ppermute | solution.py:54
  183.1 8.3 %branch_1_fun.18 = (bf16[512,768]{1,0:T(8,128)(2,1)}, f32[256,1024]{1,0:T(8,128)}, bf16[256,1024]{1,0:T(8,128)(2,1)}, f32[1,1024]{1,0:T(1,128)S(1)}) custom-call(bf16[256,1024]{1,0:T(8,128)(2,1)} %branch_1_fun.17.refs_0_, bf16[256,1024]{1,0:T(8,128)(2,1)} %collective-permute-done.5.refs_1_, bf16[128,1024]{1,0:T(8,128)(2,1)} %get-tuple-element.146.refs_2_, ...), custom_call_target="tpu_custom_call" | custom-call | flops 11000000 | bytes 35000 | tf_op jit(solution)/shard_map/cond/branch_1_fun/pallas_call | solution.py:110
  191.4 4.4 %shard_map.327 = (f32[128,1024]{1,0:T(8,128)}, bf16[256,1024]{1,0:T(8,128)(2,1)}, bf16[256,1024]{1,0:T(8,128)(2,1)}, bf16[256,1024]{1,0:T(8,128)(2,1)}, bf16[128,1024]{1,0:T(8,128)(2,1)}) custom-call(bf16[256,1024]{1,0:T(8,128)(2,1)} %get-tuple-element.263.refs_4_.refs_0_, bf16[256,1024]{1,0:T(8,128)(2,1)} %get-tuple-element.264.refs_5_.refs_1_, ...), custom_call_target="tpu_custom_call" | custom-call | flops 11000000 | bytes 35000 | tf_op jit(solution)/shard_map/pallas_call | solution.py:110
  203.2 18.7 %conditional.12 = (f32[8,1024]{1,0:T(8,128)S(1)}) conditional(s32[]{:T(128)} %bitcast.3, () %tuple.70, (f32[8,1024]{1,0:T(8,128)S(1)}, f32[1,1024]{1,0:T(1,128)S(1)}, f32[1,1024]{1,0:T(1,128)S(1)}) %tuple.71), branch_computations={%region_10.0_spmd, %region_11.0_spmd} | conditional | flops 63488 | bytes 958632 | solution.py:134
  209.0 3.4 %collective-permute-done.14 = f32[8,1024]{1,0:T(8,128)S(1)} collective-permute-done((f32[8,1024]{1,0:T(8,128)S(1)}, f32[8,1024]{1,0:T(8,128)S(1)}, u32[]{:S(2)}, u32[]{:S(2)}) %collective-permute-start.14) | collective-permute-done | bytes 32800 | tf_op jit(solution)/shard_map/cond/branch_1_fun/ppermute | solution.py:54
  214.5 7.4 %collective-permute-done.15 = f32[8,1024]{1,0:T(8,128)S(1)} collective-permute-done((f32[8,1024]{1,0:T(8,128)S(1)}, f32[8,1024]{1,0:T(8,128)S(1)}, u32[]{:S(2)}, u32[]{:S(2)}) %collective-permute-start.15) | collective-permute-done | bytes 32800 | tf_op jit(solution)/shard_map/cond/branch_1_fun/ppermute | solution.py:54
  222.0 4.1 %collective-permute-done.45.refs_8_.refs_3_ = bf16[128,1024]{1,0:T(8,128)(2,1)} collective-permute-done((bf16[128,1024]{1,0:T(8,128)(2,1)}, bf16[128,1024]{1,0:T(8,128)(2,1)}, u32[]{:S(2)}, u32[]{:S(2)}) %collective-permute-start.45) | collective-permute-done | bytes 262176 | tf_op jit(solution)/shard_map/ppermute | solution.py:54
  234.6 14.6 %conditional.13 = (f32[128,1024]{1,0:T(8,128)S(1)}) conditional(s32[]{:T(128)} %bitcast.3, () %tuple.65, (bf16[256,1024]{1,0:T(8,128)(2,1)}, f32[256,1024]{1,0:T(8,128)}, s32[2]{0:T(128)S(1)}, f32[128,1024]{1,0:T(8,128)}, bf16[384,1024]{1,0:T(8,128)(2,1)}) %tuple.72), branch_computations={%region_12.0_spmd, %region_13.0_spmd} | conditional | flops 11393216 | bytes 7375176 | solution.py:134
  239.5 6.9 %collective-permute-done.11.refs_3_ = bf16[128,1024]{1,0:T(8,128)(2,1)S(1)} collective-permute-done((bf16[128,1024]{1,0:T(8,128)(2,1)S(1)}, bf16[128,1024]{1,0:T(8,128)(2,1)S(1)}, u32[]{:S(2)}, u32[]{:S(2)}) %collective-permute-start.11) | collective-permute-done | bytes 262176 | tf_op jit(solution)/shard_map/cond/branch_1_fun/ppermute | solution.py:54
  249.2 4.2 %collective-permute-done.49.refs_1_ = f32[8,1024]{1,0:T(8,128)S(1)} collective-permute-done((f32[8,1024]{1,0:T(8,128)S(1)}, f32[8,1024]{1,0:T(8,128)S(1)}, u32[]{:S(2)}, u32[]{:S(2)}) %collective-permute-start.49) | collective-permute-done | bytes 32800 | tf_op jit(solution)/shard_map/ppermute | solution.py:54
  (161 shorter events, 122.7 us)
Async XLA Ops:
  2.5 23.2 %collective-permute-start.18 = (bf16[128,1024]{1,0:T(8,128)(2,1)}, bf16[128,1024]{1,0:T(8,128)(2,1)}, u32[]{:S(2)}, u32[]{:S(2)}) collective-permute-start(bf16[128,1024]{1,0:T(8,128)(2,1)} %shard_map.317.refs_0_.refs_6_.refs_1_), channel_id=1, source_target_pairs={{0,8},{4,12},{8,0},{12,4},{16,24},{20,28},{24,16},{28,20},{1,9},{5... | collective-permute-start | bytes 786440 | tf_op jit(solution)/shard_map/ppermute | solution.py:54
  5.5 20.2 %collective-permute-start.17 = (bf16[128,1024]{1,0:T(8,128)(2,1)}, bf16[128,1024]{1,0:T(8,128)(2,1)}, u32[]{:S(2)}, u32[]{:S(2)}) collective-permute-start(bf16[128,1024]{1,0:T(8,128)(2,1)} %shard_map.317.refs_0_.refs_6_.refs_1_), channel_id=1, source_target_pairs={{0,24},{4,28},{8,16},{12,20},{16,8},{20,12},{24,0},{28,4},{1,25},{... | collective-permute-start | bytes 786440 | tf_op jit(solution)/shard_map/ppermute | solution.py:54
  8.0 23.3 %collective-permute-start.16 = (bf16[128,1024]{1,0:T(8,128)(2,1)}, bf16[128,1024]{1,0:T(8,128)(2,1)}, u32[]{:S(2)}, u32[]{:S(2)}) collective-permute-start(bf16[128,1024]{1,0:T(8,128)(2,1)} %shard_map.317.refs_0_.refs_6_.refs_1_), channel_id=1, source_target_pairs={{0,16},{4,20},{8,24},{12,28},{16,0},{20,4},{24,8},{28,12},{1,17},{... | collective-permute-start | bytes 786440 | tf_op jit(solution)/shard_map/ppermute | solution.py:54
  10.2 29.0 %collective-permute-start.20 = (bf16[384,1024]{1,0:T(8,128)(2,1)}, bf16[384,1024]{1,0:T(8,128)(2,1)S(1)}, u32[]{:S(2)}, u32[]{:S(2)}) collective-permute-start(bf16[384,1024]{1,0:T(8,128)(2,1)} %shard_map.318.refs_0_.refs_7_), channel_id=1, source_target_pairs={{0,4},{4,0},{8,12},{12,8},{16,20},{20,16},{24,28},{28,24},{1,5},{5... | collective-permute-start | bytes 2359304 | tf_op jit(solution)/shard_map/ppermute | solution.py:54
  33.6 18.8 %collective-permute-start.19 = (bf16[384,1024]{1,0:T(8,128)(2,1)}, bf16[384,1024]{1,0:T(8,128)(2,1)}, u32[]{:S(2)}, u32[]{:S(2)}) collective-permute-start(bf16[384,1024]{1,0:T(8,128)(2,1)} %get-tuple-element.266), channel_id=1, source_target_pairs={{0,4},{4,0},{8,12},{12,8},{16,20},{20,16},{24,28},{28,24},{1,5},{5... | collective-permute-start | bytes 2359304 | tf_op jit(solution)/shard_map/ppermute | solution.py:54
  35.1 24.1 %collective-permute-start.23 = (bf16[128,1024]{1,0:T(8,128)(2,1)}, bf16[128,1024]{1,0:T(8,128)(2,1)}, u32[]{:S(2)}, u32[]{:S(2)}) collective-permute-start(bf16[128,1024]{1,0:T(8,128)(2,1)} %get-tuple-element.267.refs_12_.refs_13_), channel_id=1, source_target_pairs={{0,8},{4,12},{8,0},{12,4},{16,24},{20,28},{24,16},{28,20},{1,9},{5... | collective-permute-start | bytes 786440 | tf_op jit(solution)/shard_map/ppermute | solution.py:54
  35.1 24.1 %collective-permute-start.22 = (bf16[128,1024]{1,0:T(8,128)(2,1)}, bf16[128,1024]{1,0:T(8,128)(2,1)}, u32[]{:S(2)}, u32[]{:S(2)}) collective-permute-start(bf16[128,1024]{1,0:T(8,128)(2,1)} %get-tuple-element.267.refs_12_.refs_13_), channel_id=1, source_target_pairs={{0,24},{4,28},{8,16},{12,20},{16,8},{20,12},{24,0},{28,4},{1,25},{... | collective-permute-start | bytes 786440 | tf_op jit(solution)/shard_map/ppermute | solution.py:54
  37.8 22.6 %collective-permute-start.21 = (bf16[128,1024]{1,0:T(8,128)(2,1)}, bf16[128,1024]{1,0:T(8,128)(2,1)}, u32[]{:S(2)}, u32[]{:S(2)}) collective-permute-start(bf16[128,1024]{1,0:T(8,128)(2,1)} %get-tuple-element.267.refs_12_.refs_13_), channel_id=1, source_target_pairs={{0,16},{4,20},{8,24},{12,28},{16,0},{20,4},{24,8},{28,12},{1,17},{... | collective-permute-start | bytes 786440 | tf_op jit(solution)/shard_map/ppermute | solution.py:54
  64.0 23.7 %collective-permute-start.24 = (bf16[384,1024]{1,0:T(8,128)(2,1)}, bf16[384,1024]{1,0:T(8,128)(2,1)}, u32[]{:S(2)}, u32[]{:S(2)}) collective-permute-start(bf16[384,1024]{1,0:T(8,128)(2,1)} %get-tuple-element.272), channel_id=1, source_target_pairs={{0,4},{4,0},{8,12},{12,8},{16,20},{20,16},{24,28},{28,24},{1,5},{5... | collective-permute-start | bytes 2359304 | tf_op jit(solution)/shard_map/ppermute | solution.py:54
  64.6 21.0 %collective-permute-start.26 = (bf16[128,1024]{1,0:T(8,128)(2,1)}, bf16[128,1024]{1,0:T(8,128)(2,1)}, u32[]{:S(2)}, u32[]{:S(2)}) collective-permute-start(bf16[128,1024]{1,0:T(8,128)(2,1)} %get-tuple-element.273.refs_1_.refs_4_), channel_id=1, source_target_pairs={{0,24},{4,28},{8,16},{12,20},{16,8},{20,12},{24,0},{28,4},{1,25},{... | collective-permute-start | bytes 786440 | tf_op jit(solution)/shard_map/ppermute | solution.py:54
  66.9 20.3 %collective-permute-start.25 = (bf16[128,1024]{1,0:T(8,128)(2,1)}, bf16[128,1024]{1,0:T(8,128)(2,1)}, u32[]{:S(2)}, u32[]{:S(2)}) collective-permute-start(bf16[128,1024]{1,0:T(8,128)(2,1)} %get-tuple-element.273.refs_1_.refs_4_), channel_id=1, source_target_pairs={{0,16},{4,20},{8,24},{12,28},{16,0},{20,4},{24,8},{28,12},{1,17},{... | collective-permute-start | bytes 786440 | tf_op jit(solution)/shard_map/ppermute | solution.py:54
  67.6 20.1 %collective-permute-start.27 = (bf16[128,1024]{1,0:T(8,128)(2,1)}, bf16[128,1024]{1,0:T(8,128)(2,1)}, u32[]{:S(2)}, u32[]{:S(2)}) collective-permute-start(bf16[128,1024]{1,0:T(8,128)(2,1)} %slice.42), channel_id=1, source_target_pairs={{0,8},{4,12},{8,0},{12,4},{16,24},{20,28},{24,16},{28,20},{1,9},{5... | collective-permute-start | bytes 786440 | tf_op jit(solution)/shard_map/ppermute | solution.py:54
  85.5 19.3 %collective-permute-start.30 = (bf16[128,1024]{1,0:T(8,128)(2,1)}, bf16[128,1024]{1,0:T(8,128)(2,1)}, u32[]{:S(2)}, u32[]{:S(2)}) collective-permute-start(bf16[128,1024]{1,0:T(8,128)(2,1)} %get-tuple-element.273.refs_1_.refs_4_), channel_id=1, source_target_pairs={{0,8},{4,12},{8,0},{12,4},{16,24},{20,28},{24,16},{28,20},{1,9},{5... | collective-permute-start | bytes 786440 | tf_op jit(solution)/shard_map/ppermute | solution.py:54
  85.6 19.2 %collective-permute-start.29 = (bf16[128,1024]{1,0:T(8,128)(2,1)}, bf16[128,1024]{1,0:T(8,128)(2,1)}, u32[]{:S(2)}, u32[]{:S(2)}) collective-permute-start(bf16[128,1024]{1,0:T(8,128)(2,1)} %collective-permute-done.26.refs_3_.refs_6_), channel_id=1, source_target_pairs={{0,4},{4,0},{8,12},{12,8},{16,20},{20,16},{24,28},{28,24},{1,5},{5... | collective-permute-start | bytes 786440 | tf_op jit(solution)/shard_map/ppermute | solution.py:54
  87.2 17.6 %collective-permute-start.28 = (bf16[128,1024]{1,0:T(8,128)(2,1)}, bf16[128,1024]{1,0:T(8,128)(2,1)}, u32[]{:S(2)}, u32[]{:S(2)}) collective-permute-start(bf16[128,1024]{1,0:T(8,128)(2,1)} %collective-permute-done.25.refs_2_.refs_5_), channel_id=1, source_target_pairs={{0,4},{4,0},{8,12},{12,8},{16,20},{20,16},{24,28},{28,24},{1,5},{5... | collective-permute-start | bytes 786440 | tf_op jit(solution)/shard_map/ppermute | solution.py:54
  113.2 8.5 %collective-permute-start.32 = (bf16[128,1024]{1,0:T(8,128)(2,1)S(1)}, bf16[128,1024]{1,0:T(8,128)(2,1)}, u32[]{:S(2)}, u32[]{:S(2)}) collective-permute-start(bf16[128,1024]{1,0:T(8,128)(2,1)S(1)} %add_convert_fusion.3), channel_id=1, source_target_pairs={{0,2},{1,3},{2,0},{3,1},{4,6},{5,7},{6,4},{7,5},{8,10},{9,11},{10,... | collective-permute-start | bytes 786440 | tf_op jit(solution)/shard_map/ppermute | solution.py:54
  139.3 27.4 %collective-permute-start.36 = (bf16[256,1024]{1,0:T(8,128)(2,1)}, bf16[256,1024]{1,0:T(8,128)(2,1)}, u32[]{:S(2)}, u32[]{:S(2)}) collective-permute-start(bf16[256,1024]{1,0:T(8,128)(2,1)} %get-tuple-element.296), channel_id=1, source_target_pairs={{0,4},{4,0},{8,12},{12,8},{16,20},{20,16},{24,28},{28,24},{1,5},{5... | collective-permute-start | bytes 1572872 | tf_op jit(solution)/shard_map/ppermute | solution.py:54
  140.9 25.8 %collective-permute-start.37 = (bf16[256,1024]{1,0:T(8,128)(2,1)}, bf16[256,1024]{1,0:T(8,128)(2,1)}, u32[]{:S(2)}, u32[]{:S(2)}) collective-permute-start(bf16[256,1024]{1,0:T(8,128)(2,1)} %get-tuple-element.298), channel_id=1, source_target_pairs={{0,8},{4,12},{8,0},{12,4},{16,24},{20,28},{24,16},{28,20},{1,9},{5... | collective-permute-start | bytes 1572872 | tf_op jit(solution)/shard_map/ppermute | solution.py:54
  153.7 8.7 %collective-permute-start.9 = (bf16[128,1024]{1,0:T(8,128)(2,1)}, bf16[128,1024]{1,0:T(8,128)(2,1)}, u32[]{:S(2)}, u32[]{:S(2)}) collective-permute-start(bf16[128,1024]{1,0:T(8,128)(2,1)} %add_convert_fusion.1), channel_id=1, source_target_pairs={{0,2},{1,3},{2,0},{3,1},{4,6},{5,7},{6,4},{7,5},{8,10},{9,11},{10,... | collective-permute-start | bytes 786440 | tf_op jit(solution)/shard_map/cond/branch_1_fun/ppermute | solution.py:54
  165.7 31.6 %collective-permute-start.40 = (bf16[256,1024]{1,0:T(8,128)(2,1)}, bf16[256,1024]{1,0:T(8,128)(2,1)}, u32[]{:S(2)}, u32[]{:S(2)}) collective-permute-start(bf16[256,1024]{1,0:T(8,128)(2,1)} %get-tuple-element.311), channel_id=1, source_target_pairs={{0,4},{4,0},{8,12},{12,8},{16,20},{20,16},{24,28},{28,24},{1,5},{5... | collective-permute-start | bytes 1572872 | tf_op jit(solution)/shard_map/ppermute | solution.py:54
  166.3 32.3 %collective-permute-start.41 = (bf16[256,1024]{1,0:T(8,128)(2,1)}, bf16[256,1024]{1,0:T(8,128)(2,1)}, u32[]{:S(2)}, u32[]{:S(2)}) collective-permute-start(bf16[256,1024]{1,0:T(8,128)(2,1)} %get-tuple-element.313), channel_id=1, source_target_pairs={{0,8},{4,12},{8,0},{12,4},{16,24},{20,28},{24,16},{28,20},{1,9},{5... | collective-permute-start | bytes 1572872 | tf_op jit(solution)/shard_map/ppermute | solution.py:54
  169.0 29.6 %collective-permute-start.42 = (bf16[128,1024]{1,0:T(8,128)(2,1)}, bf16[128,1024]{1,0:T(8,128)(2,1)}, u32[]{:S(2)}, u32[]{:S(2)}) collective-permute-start(bf16[128,1024]{1,0:T(8,128)(2,1)} %get-tuple-element.315), channel_id=1, source_target_pairs={{0,24},{4,28},{8,16},{12,20},{16,8},{20,12},{24,0},{28,4},{1,25},{... | collective-permute-start | bytes 786440 | tf_op jit(solution)/shard_map/ppermute | solution.py:54
  171.4 27.2 %collective-permute-start.43 = (bf16[128,1024]{1,0:T(8,128)(2,1)}, bf16[128,1024]{1,0:T(8,128)(2,1)}, u32[]{:S(2)}, u32[]{:S(2)}) collective-permute-start(bf16[128,1024]{1,0:T(8,128)(2,1)} %get-tuple-element.316), channel_id=1, source_target_pairs={{0,16},{4,20},{8,24},{12,28},{16,0},{20,4},{24,8},{28,12},{1,17},{... | collective-permute-start | bytes 786440 | tf_op jit(solution)/shard_map/ppermute | solution.py:54
  195.7 26.2 %collective-permute-start.38 = (bf16[256,1024]{1,0:T(8,128)(2,1)}, bf16[256,1024]{1,0:T(8,128)(2,1)}, u32[]{:S(2)}, u32[]{:S(2)}) collective-permute-start(bf16[256,1024]{1,0:T(8,128)(2,1)} %get-tuple-element.307), channel_id=1, source_target_pairs={{0,4},{4,0},{8,12},{12,8},{16,20},{20,16},{24,28},{28,24},{1,5},{5... | collective-permute-start | bytes 1572872 | tf_op jit(solution)/shard_map/ppermute | solution.py:54
  197.3 24.6 %collective-permute-start.39 = (bf16[256,1024]{1,0:T(8,128)(2,1)}, bf16[256,1024]{1,0:T(8,128)(2,1)S(1)}, u32[]{:S(2)}, u32[]{:S(2)}) collective-permute-start(bf16[256,1024]{1,0:T(8,128)(2,1)} %get-tuple-element.309), channel_id=1, source_target_pairs={{0,8},{4,12},{8,0},{12,4},{16,24},{20,28},{24,16},{28,20},{1,9},{5... | collective-permute-start | bytes 1572872 | tf_op jit(solution)/shard_map/ppermute | solution.py:54
  200.9 21.1 %collective-permute-start.44 = (bf16[128,1024]{1,0:T(8,128)(2,1)}, bf16[128,1024]{1,0:T(8,128)(2,1)S(1)}, u32[]{:S(2)}, u32[]{:S(2)}) collective-permute-start(bf16[128,1024]{1,0:T(8,128)(2,1)} %get-tuple-element.321), channel_id=1, source_target_pairs={{0,24},{4,28},{8,16},{12,20},{16,8},{20,12},{24,0},{28,4},{1,25},{... | collective-permute-start | bytes 786440 | tf_op jit(solution)/shard_map/ppermute | solution.py:54
  203.2 22.9 %collective-permute-start.45 = (bf16[128,1024]{1,0:T(8,128)(2,1)}, bf16[128,1024]{1,0:T(8,128)(2,1)}, u32[]{:S(2)}, u32[]{:S(2)}) collective-permute-start(bf16[128,1024]{1,0:T(8,128)(2,1)} %get-tuple-element.322), channel_id=1, source_target_pairs={{0,16},{4,20},{8,24},{12,28},{16,0},{20,4},{24,8},{28,12},{1,17},{... | collective-permute-start | bytes 786440 | tf_op jit(solution)/shard_map/ppermute | solution.py:54
  212.4 9.6 %collective-permute-start.15 = (f32[8,1024]{1,0:T(8,128)S(1)}, f32[8,1024]{1,0:T(8,128)S(1)}, u32[]{:S(2)}, u32[]{:S(2)}) collective-permute-start(f32[8,1024]{1,0:T(8,128)S(1)} %fusion), channel_id=1, source_target_pairs={{0,8},{4,12},{8,0},{12,4},{16,24},{20,28},{24,16},{28,20},{1,9},{5... | collective-permute-start | bytes 98312 | tf_op jit(solution)/shard_map/cond/branch_1_fun/ppermute | solution.py:54
  228.7 26.7 %collective-permute-start.48 = (bf16[384,1024]{1,0:T(8,128)(2,1)}, bf16[384,1024]{1,0:T(8,128)(2,1)}, u32[]{:S(2)}, u32[]{:S(2)}) collective-permute-start(bf16[384,1024]{1,0:T(8,128)(2,1)} %get-tuple-element.323), channel_id=1, source_target_pairs={{0,4},{4,0},{8,12},{12,8},{16,20},{20,16},{24,28},{28,24},{1,5},{5... | collective-permute-start | bytes 2359304 | tf_op jit(solution)/shard_map/ppermute | solution.py:54
  229.3 30.7 %collective-permute-start.46 = (bf16[128,1024]{1,0:T(8,128)(2,1)}, bf16[128,1024]{1,0:T(8,128)(2,1)S(1)}, u32[]{:S(2)}, u32[]{:S(2)}) collective-permute-start(bf16[128,1024]{1,0:T(8,128)(2,1)} %get-tuple-element.324), channel_id=1, source_target_pairs={{0,24},{4,28},{8,16},{12,20},{16,8},{20,12},{24,0},{28,4},{1,25},{... | collective-permute-start | bytes 786440 | tf_op jit(solution)/shard_map/ppermute | solution.py:54
  231.6 28.4 %collective-permute-start.47 = (bf16[128,1024]{1,0:T(8,128)(2,1)}, bf16[128,1024]{1,0:T(8,128)(2,1)}, u32[]{:S(2)}, u32[]{:S(2)}) collective-permute-start(bf16[128,1024]{1,0:T(8,128)(2,1)} %get-tuple-element.325), channel_id=1, source_target_pairs={{0,16},{4,20},{8,24},{12,28},{16,0},{20,4},{24,8},{28,12},{1,17},{... | collective-permute-start | bytes 786440 | tf_op jit(solution)/shard_map/ppermute | solution.py:54
  231.6 21.8 %collective-permute-start.49 = (f32[8,1024]{1,0:T(8,128)S(1)}, f32[8,1024]{1,0:T(8,128)S(1)}, u32[]{:S(2)}, u32[]{:S(2)}) collective-permute-start(f32[8,1024]{1,0:T(8,128)S(1)} %get-tuple-element.401.refs_6_.refs_0_), channel_id=1, source_target_pairs={{0,16},{4,20},{8,24},{12,28},{16,0},{20,4},{24,8},{28,12},{1,17},{... | collective-permute-start | bytes 98312 | tf_op jit(solution)/shard_map/ppermute | solution.py:54
  (40 other events, 263.4 us)

commit v4 on v3

--- a/solution.py
+++ b/solution.py
@@ -41,6 +41,10 @@
     return value.astype(jnp.float32)
 
 
+VMEM_LIMIT = 63 << 20
+QUICK, SLOW = 0.01, 2
+
+
 def shaped(shape, dtype=jnp.bfloat16):
     return jax.ShapeDtypeStruct(shape, dtype)
 
@@ -58,7 +62,7 @@
     return array, start, rows
 
 
-def kernel_call(body, out_shape, whole=(), pieces=(), scalars=(), marks=(), scratch=()):
+def kernel_call(body, out_shape, whole=(), pieces=(), scalars=(), marks=(), scratch=(), us=QUICK):
     pieces = [
         [p if isinstance(p, tuple) else (p, 0, p.shape[0]) for p in some] for some in pieces
     ]
@@ -112,26 +116,36 @@
         out_shape=flat_out,
         in_specs=[pl.BlockSpec(memory_space=pltpu.SMEM)] * len(scalars)
         + [inside] * len(whole)
-        + [anywhere] * (len(flat) + len(marks)),
+        + [pl.BlockSpec(memory_space=pltpu.HBM)] * len(flat)
+        + [anywhere] * len(marks),
         out_specs=[inside] * len(flat_out),
         scratch_shapes=buffers + semaphores + list(scratch),
         compiler_params=pltpu.CompilerParams(vmem_limit_bytes=VMEM_LIMIT),
         cost_estimate=pl.CostEstimate(
-            flops=int(QUICK * 1.1e9), bytes_accessed=int(QUICK * 3.5e6), transcendentals=0
+            flops=int(us * 1.1e9), bytes_accessed=int(us * 3.5e6), transcendentals=0
         ),
     )(*scalars, *whole, *[p[0] for p in flat], *marks)
     return jax.tree.unflatten(tree, results)
 
 
-VMEM_LIMIT = 63 << 20
-QUICK = 0.01
-
-
 def region(flag, body, *operands):
     def nothing(*some):
         return jax.tree.map(lambda x: jnp.zeros(x.shape, x.dtype), jax.eval_shape(body, *operands))
 
     return lax.cond(flag, body, nothing, *operands)
+
+
+RIDERS = 8
+
+
+def pack(value):
+    high = wide(low(value))
+    return low(jnp.concatenate([high, value - high], axis=0))
+
+
+def unpack(packed):
+    value = wide(packed[...])
+    return value[:RIDERS] + value[RIDERS:]
 
 
 def join_kernel(need, own_ref, across_ref, out_ref):
@@ -191,20 +205,32 @@
     ]
 
 
+def weight_cuts_with_sums(width, columns):
+    cuts = weight_cuts(width, columns)
+    for k in (2, 3):
+        if paired():
+            cuts[k] = shaped((cuts[k].shape[0] + 2 * RIDERS, columns))
+    return cuts + [shaped((2 * RIDERS, columns))]
+
+
 def weight_grad_into(pairs, out_refs):
-    column = 0
-    for left_ref, right_ref in pairs:
-        right = right_ref[...]
-        columns = slice(column, column + right.shape[1])
-        column += right.shape[1]
-        start = 0
-        for out_ref in out_refs:
-            for place in range(0, out_ref.shape[0], 128):
-                block = left_ref[:, start : start + 128]
-                out_ref[place : place + 128, columns] = matmul_tn(block, right).astype(
-                    out_ref.dtype
-                )
-                start += 128
+    places, start = [], 0
+    for out_ref in out_refs:
+        rows = out_ref.shape[0] // 128 * 128
+        places.append((out_ref, start, start + rows))
+        start += rows
+    for first in range(0, start, 512):
+        last, column = min(first + 512, start), 0
+        for left_ref, right_ref in pairs:
+            columns = slice(column, column + right_ref.shape[1])
+            column += right_ref.shape[1]
+            block = matmul_tn(left_ref[:, first:last], right_ref[...])
+            for out_ref, low_row, high_row in places:
+                begin, end = max(first, low_row), min(last, high_row)
+                if begin < end:
+                    out_ref[begin - low_row : end - low_row, columns] = block[
+                        begin - first : end - first
+                    ].astype(out_ref.dtype)
 
 
 def scatter_first(cuts):
@@ -214,58 +240,68 @@
     return kept, far, beside, swap(far_beside, "dp", 1), swap(above, "dp", 2)
 
 
-def combine_kernel(
-    need, far_ref, far_in_ref, beside_ref, above_ref, *rest
-):
+def combine_kernel(with_sums, need, far_ref, far_in_ref, beside_ref, above_ref, *rest):
     *waiting, far_out, farther_out, beside_out = rest
-    block = far_out.shape[0]
+    block = far_ref.shape[0] // 2
     need(0)
     need(1)
-    farther_out[...] = low(wide(far_ref[block:]) + wide(far_in_ref[block:]))
-    far_out[...] = low(wide(far_ref[:block]) + wide(far_in_ref[:block]))
+    farther_out[:block] = low(wide(far_ref[block:]) + wide(far_in_ref[block : 2 * block]))
+    far_out[:block] = low(wide(far_ref[:block]) + wide(far_in_ref[:block]))
     need(2)
     need(3)
-    beside_out[:block] = low(wide(beside_ref[...]) + wide(above_ref[...]))
+    beside_out[:block] = low(wide(beside_ref[...]) + wide(above_ref[:block]))
+    sums, waiting = waiting[:with_sums], waiting[with_sums:]
+    place = block
     for number, ref in enumerate(waiting):
-        need(4 + number)
-        beside_out[(number + 1) * block : (number + 2) * block] = ref[...]
-
-
-def scatter_second(state, marks, waiting=()):
+        need(4 + with_sums + number)
+        beside_out[place : place + block] = ref[...]
+        place += block
+    if with_sums:
+        need(4)
+        packed = pack(unpack(sums[0]) + unpack(far_in_ref[2 * block :]))
+        far_out[block:] = packed
+        farther_out[block:] = packed
+        beside_out[place:] = above_ref[block:]
+
+
+def scatter_second(state, marks, waiting=(), sums=(), us=QUICK):
     if not paired():
-        return state, None, list(marks)
+        return state, None, []
     kept, far, beside, far_in, above = state
     block, columns = kept.shape
+    extra = 2 * RIDERS * len(sums)
+    first = [part(above, 0, block)] + [part(above, 2 * block, extra)] * len(sums)
     far_out, farther_out, beside_out = kernel_call(
-        combine_kernel,
-        [shaped(kept.shape)] * 2 + [shaped((block * (1 + len(waiting)), columns))],
-        pieces=[[far], [far_in], [beside], [part(above, 0, block)], *[[w] for w in waiting]],
+        partial(combine_kernel, len(sums)),
+        [shaped((block + extra, columns))] * 2
+        + [shaped((block * (1 + len(waiting)) + extra, columns))],
+        pieces=[[far], [far_in], [beside], first, *[[x] for x in (*sums, *waiting)]],
         marks=marks,
-    )
-    terms = [
-        kept,
-        part(above, block, block),
-        swap(farther_out, "dp", 6),
-        swap(far_out, "dp", 4),
-    ]
-    return terms, beside_out, [beside_out]
-
-
-def last_kernel(write, count, need, *refs):
+        us=us,
+    )
+    arrived = [swap(farther_out, "dp", 6), swap(far_out, "dp", 4)]
+    terms = [kept, part(above, block, block), *[part(x, 0, block) for x in arrived]]
+    riders = [part(x, block, extra) for x in (far_out, *arrived)]
+    return terms, beside_out, [*riders, part(above, 2 * block, extra)] if sums else []
+
+
+def last_kernel(write, count, riders, need, *refs):
     total = None
     for number, ref in enumerate(refs[:count]):
         need(number)
         total = wide(ref[...]) if total is None else total + wide(ref[...])
+    for number in range(riders):
+        need(count + number)
     write(total, *refs[count:])
 
 
-def scatter_last(state, write, out_shape, marks=()):
+def scatter_last(state, write, out_shape, marks=(), riders=()):
     if not paired():
         state = [lax.psum_scatter(state[0], "dp", scatter_dimension=0, tiled=True)]
     return kernel_call(
-        partial(last_kernel, write, len(state)),
+        partial(last_kernel, write, len(state), len(riders)),
         out_shape,
-        pieces=[[term] for term in state],
+        pieces=[[term] for term in [*state, *riders]],
         marks=marks,
     )
 
@@ -496,11 +532,14 @@
 def hidden_grad_kernel(
     need, rows_ref, outer_ref, slope_ref, inner_ref, hidden_grad_ref, near_ref, far_ref, sums_ref
 ):
-    for number in range(3):
-        need(number)
+    need(0)
+    need(1)
     for start in range(0, hidden_grad_ref.shape[1], 256):
         columns = slice(start, start + 256)
-        grad = low(matmul(rows_ref[...], outer_ref[:, columns]) * slope_ref[:, columns])
+        product = matmul(rows_ref[...], outer_ref[:, columns])
+        if start == 0:
+            need(2)
+        grad = low(product * slope_ref[:, columns])
         hidden_grad_ref[:, columns] = grad
         sums_ref[0:1, columns] = jnp.sum(wide(grad), axis=0, keepdims=True)
     need(3)
@@ -529,6 +568,7 @@
     low_ref,
     sums_ref,
 ):
+    rows = mix_ref.shape[0]
     need(3)
     need(4)
     cot = second_grad_ref[...] + own_sum(need, near_ref, arrived_ref, across_ref)
@@ -541,7 +581,7 @@
     )
     mix_ref[...] = mix
     rounded = low(mix)
-    low_ref[...] = rounded
+    low_ref[:rows] = rounded
     sums = jnp.concatenate(
         [
             jnp.sum(wide(rounded), axis=0, keepdims=True),
@@ -553,21 +593,26 @@
         axis=0,
     )
     from_slots(sums, ranks_ref[0], in_slots, sums_ref)
+    low_ref[rows:] = pack(sums_ref[...])
 
 
 def attention_back_kernel(
     scale,
     need,
+    inner_sums_ref,
     rows_ref,
     weights_ref,
     qkv_ref,
     probs_ref,
+    tokens_ref,
+    context_ref,
+    riders_ref,
     grads_ref,
     near_ref,
     far_ref,
-    sums_ref,
-    context_grad_ref,
+    *rest,
 ):
+    *cut_refs, context_grad_ref = rest
     head_width = context_grad_ref.shape[1]
     need(0)
     need(1)
@@ -591,15 +636,21 @@
         value_grad = low(matmul_tn(probs, context_grad))
         for place, grad in zip(columns, (query_grad, key_grad, value_grad)):
             grads_ref[:, place] = grad
-    sums_ref[...] = jnp.zeros_like(sums_ref)
-    sums_ref[0:1, : 3 * head_width] = jnp.sum(wide(grads_ref[...]), axis=0, keepdims=True)
+    for number in range(4, 7):
+        need(number)
+    *cut_refs, packed_ref = cut_refs
+    own, across, beside, corner = (
+        unpack(riders_ref[k * 2 * RIDERS : (k + 1) * 2 * RIDERS]) for k in range(4)
+    )
+    sums = (own + across) + (beside + corner)
+    mine = jnp.sum(wide(grads_ref[...]), axis=0, keepdims=True)
+    mine = jnp.concatenate([mine, jnp.zeros((1, head_width), jnp.float32)], axis=1)
+    packed = pack(jnp.concatenate([sums[: RIDERS - 2], inner_sums_ref[...], mine], axis=0))
+    packed_ref[...] = packed
+    for ref in cut_refs[2:4]:
+        ref[ref.shape[0] - 2 * RIDERS :] = packed
+    weight_grad_into([(tokens_ref, grads_ref), (rows_ref, context_ref)], cut_refs)
     back_into(grads_ref, weights_ref, slice(0, 3 * head_width), near_ref, far_ref)
-
-
-def attention_grad_kernel(need, tokens_ref, qkv_grad_ref, rows_ref, context_ref, *out_refs):
-    for number in range(4):
-        need(number)
-    weight_grad_into([(tokens_ref, qkv_grad_ref), (rows_ref, context_ref)], out_refs)
 
 
 def tokens_grad_kernel(
@@ -610,16 +661,6 @@
     from_slots(total, ranks_ref[0], in_slots, out_ref)
 
 
-def finish_kernel(need, sums_ref, arrived_ref, *out_refs):
-    *row_refs, query_ref, value_ref = out_refs
-    for k, ref in enumerate(row_refs):
-        ref[...] = sums_ref[k, :] + arrived_ref[k, :]
-    width = query_ref.shape[0]
-    k = len(row_refs)
-    query_ref[...] = sums_ref[k, :width] + arrived_ref[k, :width]
-    value_ref[...] = sums_ref[k, 2 * width : 3 * width] + arrived_ref[k, 2 * width : 3 * width]
-
-
 def write_turned(total, out_ref):
     out_ref[...] = total.T
 
@@ -628,11 +669,24 @@
     out_ref[...] = total
 
 
-def write_attention(total, query_ref, key_ref, value_ref, proj_ref):
+def write_attention(total, *refs):
+    riders, refs = refs[: len(refs) - 13], refs[len(refs) - 13 :]
+    query_ref, key_ref, value_ref, proj_ref, inner_sum_ref, query_sum_ref, value_sum_ref = refs[:7]
     width = query_ref.shape[1]
     for place, ref in enumerate((query_ref, key_ref, value_ref)):
         ref[...] = total[:, place * width : (place + 1) * width]
     proj_ref[...] = total[:, 3 * width :].T
+    if len(riders) > 1:
+        own, farther, far, above, beside = (unpack(ref) for ref in riders)
+        above = unpack(pack(above + beside))
+        sums = (own + above) + (far + farther)
+    else:
+        sums = unpack(riders[0])
+    for k, ref in enumerate(refs[7:]):
+        ref[...] = sums[k, :]
+    inner_sum_ref[...] = sums[6, :]
+    query_sum_ref[...] = sums[7, :width]
+    value_sum_ref[...] = sums[7, 2 * width : 3 * width]
 
 
 def on_device(
@@ -763,8 +817,8 @@
     )
 
     def inner_part(first_low, arrived, marks):
-        norm_rows = gather_rows(first_low)
-        return norm_rows, kernel_call(
+        norm_rows = gather_rows(first_low, joined=False)
+        return norm_rows[1:], kernel_call(
             inner_kernel,
             [shaped((group_rows, inner_width)), shaped((group_rows, inner_width), jnp.float32)],
             whole=[b_inner[None, :]],
@@ -772,13 +826,14 @@
             marks=marks,
         )
 
-    norm_rows, (active, slope) = region(
+    other_rows, (active, slope) = region(
         flag,
         inner_part,
         first_low,
         inner_weights[: len(inner_weights) - len(inner_beside)],
         outer_far + outer_corner,
     )
+    norm_rows = [first_low, *other_rows]
     near, far = kernel_call(
         outer_kernel, partial_sums, pieces=[[active], outer_weights]
     )
@@ -814,7 +869,7 @@
         marks=[outer_cuts[0]],
     )
 
-    def first_back_part(near, far, norm_rows, hidden_grad, rest):
+    def inner_grad_part(near, far, norm_rows, hidden_grad):
         terms = scatter_rows(near, far)
         inner_cuts = kernel_call(
             single_grad_kernel,
@@ -822,78 +877,61 @@
             pieces=[norm_rows, [hidden_grad]],
             marks=[terms[1][0][0]],
         )
-        second_grad, unit, *small_operands = rest
-        return inner_cuts, kernel_call(
-            partial(first_back_kernel, in_slots),
-            [shaped(own, jnp.float32), shaped(own), shaped((8, model_width), jnp.float32)],
-            scalars=[ranks],
-            whole=small_operands,
-            pieces=[*terms, [second_grad], [unit]],
-            marks=inner_cuts[:1],
-        )
-
-    inner_cuts, (mix_grad, proj_grad, sums) = region(
-        flag,
-        first_back_part,
-        near,
-        far,
-        norm_rows,
-        hidden_grad,
-        [second_grad, unit, unit_scale, small, second_sums],
-    )
-    outer_terms, outer_beside, outer_mark = scatter_second(outer_state, [proj_grad])
+        return inner_cuts, [some[0][0] if isinstance(some[0], tuple) else some[0] for some in terms[1:]]
+
+    inner_cuts, (arrived, across) = region(
+        flag, inner_grad_part, near, far, norm_rows, hidden_grad
+    )
+    outer_terms, outer_beside, _ = scatter_second(outer_state, [across])
+    outer_mark = [outer_beside] if in_slots else []
+    mix_grad, proj_grad = kernel_call(
+        partial(first_back_kernel, in_slots),
+        [shaped(own, jnp.float32), shaped((piece_rows + 2 * RIDERS, model_width))],
+        scalars=[ranks],
+        whole=[unit_scale, small, second_sums],
+        pieces=[
+            [part(near, 0, piece_rows)],
+            [part(arrived, 0, piece_rows)],
+            [across],
+            [second_grad],
+            [unit],
+        ],
+        scratch=[pltpu.VMEM((RIDERS, model_width), jnp.float32)],
+    )
     inner_state = scatter_first(inner_cuts)
 
-    def attention_back_part(proj_grad, qkv, probs, marks):
-        proj_rows = gather_rows(proj_grad)
-        return (
-            proj_rows,
-            kernel_call(
-                partial(attention_back_kernel, scale),
-                [
-                    shaped((group_rows, 3 * head_width)),
-                    *partial_sums,
-                    shaped((1, model_width), jnp.float32),
-                ],
-                pieces=[proj_rows, attn_weights, [qkv], [probs]],
-                marks=marks,
-                scratch=[pltpu.VMEM((group_rows, head_width), jnp.bfloat16)],
-            ),
-        )
-
-    proj_rows, (qkv_grad, near, far, attn_sums) = region(
-        flag, attention_back_part, proj_grad, qkv, probs, outer_mark
-    )
-    attn_state = scatter_first(
-        kernel_call(
-            attention_grad_kernel,
-            weight_cuts(model_width, 4 * head_width),
-            pieces=[token_rows, [qkv_grad], proj_rows, [context]],
-        )
-    )
+    def row_parts(gathered, first, rows):
+        whole = gathered[0].shape[0] // 2
+        return [part(g, k * whole + first, rows) for g in gathered for k in range(2)]
+
+    def attention_back_part(proj_grad, marks):
+        gathered = gather_rows(proj_grad)
+        return kernel_call(
+            partial(attention_back_kernel, scale),
+            [
+                shaped((group_rows, 3 * head_width)),
+                *partial_sums,
+                *weight_cuts_with_sums(model_width, 4 * head_width),
+            ],
+            whole=[inner_sums],
+            pieces=[
+                row_parts(gathered, 0, piece_rows),
+                attn_weights,
+                [qkv],
+                [probs],
+                token_rows,
+                [context],
+                row_parts(gathered, piece_rows, 2 * RIDERS),
+            ],
+            marks=marks,
+            scratch=[pltpu.VMEM((group_rows, head_width), jnp.bfloat16)],
+        )[1:]
+
+    near, far, *attn_cuts, sums = region(flag, attention_back_part, proj_grad, outer_mark)
+    attn_state = scatter_first(attn_cuts)
     inner_terms, inner_beside, _ = scatter_second(
-        inner_state, [attn_state[0], *outer_terms[2:]]
-    )
-
-    offsets = [1 << bit for bit in range(lax.axis_size("dp").bit_length() - 1)]
-
-    def sums_part(sums, inner_sums, attn_sums, mark):
-        sums = sums + swap(sums, "tensor", 1)
-        sums = sums + swap(sums, "tensor", 2)
-        sums = jnp.concatenate([sums[:6], inner_sums, attn_sums], axis=0)
-        for offset in offsets[:-1]:
-            sums = sums + swap(sums, "dp", offset)
-        return sums
-
-    sums = region(flag, sums_part, sums, inner_sums, attn_sums, attn_state[0])
-    waiting = [outer_beside, inner_beside] if in_slots else []
-    attn_terms, beside, attn_mark = scatter_second(
-        attn_state, [sums, *inner_terms[2:]], waiting
-    )
-    besides = [[]] * 3
-    if in_slots:
-        besides = swap(beside, "dp", 1)
-        besides = [[part(besides, k * shard_rows, shard_rows)] for k in range(3)]
+        inner_state, [attn_state[0], *[t[0] for t in outer_terms[2:]]], us=SLOW
+    )
 
     def tokens_part(near, far, mix_grad, mark):
         terms = scatter_rows(near, far)
@@ -905,26 +943,33 @@
             marks=[mark],
         )[0]
 
-    tokens_grad = region(flag, tokens_part, near, far, mix_grad, attn_mark[0])
-    *shared, db_inner, db_query, db_value = kernel_call(
-        finish_kernel,
-        [shaped((model_width,), jnp.float32)] * 6
-        + [shaped(b.shape, jnp.float32) for b in (b_inner, b_query, b_value)],
-        whole=[sums, swap(sums, "dp", offsets[-1])],
-        marks=[tokens_grad],
-    )
-    dw_query, dw_key, dw_value, dw_proj = scatter_last(
+    tokens_grad = region(flag, tokens_part, near, far, mix_grad, attn_state[0])
+    waiting = [outer_beside, inner_beside] if in_slots else []
+    attn_terms, beside, riders = scatter_second(
+        attn_state, [tokens_grad, *[t[0] for t in inner_terms[2:]]], waiting, [sums] * in_slots
+    )
+    besides = [[]] * 3
+    if in_slots:
+        besides = swap(beside, "dp", 1)
+        riders.append(part(besides, 3 * shard_rows, 2 * RIDERS))
+        besides = [[part(besides, k * shard_rows, shard_rows)] for k in range(3)]
+    else:
+        riders = [pack(lax.psum(unpack(sums), "dp"))]
+    dw_outer = scatter_last(
+        outer_terms + besides[1], write_turned, [shaped(w_outer.shape, jnp.float32)]
+    )[0]
+    dw_inner = scatter_last(
+        inner_terms + besides[2], write_plain, [shaped(w_inner.shape, jnp.float32)]
+    )[0]
+    dw_query, dw_key, dw_value, dw_proj, db_inner, db_query, db_value, *shared = scatter_last(
         attn_terms + besides[0],
         write_attention,
-        [shaped(w.shape, jnp.float32) for w in (w_query, w_key, w_value, w_proj)],
-        [tokens_grad],
-    )
-    dw_outer = scatter_last(
-        outer_terms + besides[1], write_turned, [shaped(w_outer.shape, jnp.float32)], [tokens_grad]
-    )[0]
-    dw_inner = scatter_last(
-        inner_terms + besides[2], write_plain, [shaped(w_inner.shape, jnp.float32)], [tokens_grad]
-    )[0]
+        [shaped(w.shape, jnp.float32) for w in (w_query, w_key, w_value, w_proj)]
+        + [shaped(b.shape, jnp.float32) for b in (b_inner, b_query, b_value)]
+        + [shaped((model_width,), jnp.float32)] * 6,
+        [dw_outer, dw_inner],
+        riders,
+    )
     db_proj, dgain_attn, dshift_attn, db_outer, dgain_ffn, dshift_ffn = shared
     return (
         layer_out,

time: 264 us -> 256 us (0.970)
  starting transfers between devices: 54.8 us -> 47.5 us
  waiting for transfers between devices: 107 us -> 111 us
  Pallas kernels: 87.3 us -> 83.5 us
    ppermute x50 -> x46, starting transfers between devices: 54.8 us -> 47.5 us  [swap(): lax.ppermute(block, axis_name, [(i, i ^ offset) for i in range(count)])]
    ppermute x50 -> x46, waiting for transfers between devices: 107 us -> 111 us  [swap(): lax.ppermute(block, axis_name, [(i, i ^ offset) for i in range(count)])]
    pallas_call x27 -> x24, Pallas kernels: 87.3 us -> 83.5 us  [kernel_call(): pl.pallas_call(run, out_shape=flat_out, in_specs=[pl.BlockSpec(memory_spa...]
  transfers between devices with their start and end apart: 50 -> 46, of which waited for: 25 -> 22; matrix products, arithmetic and copies ran while one was open for 2% -> 2% of each run, Pallas kernels for 25% -> 24%
where the time goes in v4:
time: 256 us; the launch traced here: 255 us
  waiting for transfers between devices  111 us (43%)
  Pallas kernels  83.5 us (33%)
  starting transfers between devices  47.5 us (19%)
  local copies, waits for them, and re-layouts  6.76 us (3%)
  other arithmetic  5.29 us (2%)
    ppermute x46, waiting for transfers between devices, swap(): lax.ppermute(block, axis_name, [(i, i ^ offset) for i in range(count)])  111 us
    pallas_call x24, Pallas kernels, kernel_call(): pl.pallas_call(run, out_shape=flat_out, in_specs=[pl.BlockSpec(memory_spa...  83.5 us
    ppermute x46, starting transfers between devices, swap(): lax.ppermute(block, axis_name, [(i, i ^ offset) for i in range(count)])  47.5 us
    convert_element_type x4, other arithmetic, low(): return value.astype(jnp.bfloat16)  5.2 us
  transfers between devices with their start and end apart: 46, of which 22 were waited for; matrix products, arithmetic and copies ran while one was open for 2% of the time, Pallas kernels for 24%

profile of v4, /device:TPU:0, one launch (start us, length us, event | category | flops | bytes accessed | tf_op | source)
XLA Modules:
  0.0 255.4 jit_solution(7654564850841710125)
XLA Ops:
  2.5 3.0 %collective-permute-start.15 = (bf16[128,1024]{1,0:T(8,128)(2,1)}, bf16[128,1024]{1,0:T(8,128)(2,1)}, u32[]{:S(2)}, u32[]{:S(2)}) collective-permute-start(bf16[128,1024]{1,0:T(8,128)(2,1)} %shard_map.317.refs_0_.refs_6_.refs_1_), channel_id=1, source_target_pairs={{0,8},{4,12},{8,0},{12,4},{16,24},{20,28},{24,16},{28,20},{1,9},{5... | collective-permute-start | bytes 786440 | tf_op jit(solution)/shard_map/ppermute | solution.py:58
  12.1 13.7 %conditional.6 = (bf16[128,1024]{1,0:T(8,128)(2,1)}, bf16[128,1024]{1,0:T(8,128)(2,1)}, f32[8,1024]{1,0:T(8,128)S(1)}, bf16[256,1024]{1,0:T(8,128)(2,1)}, bf16[256,1024]{1,0:T(8,128)(2,1)}) conditional(s32[]{:T(128)} %bitcast.3, () %tuple.53, (s32[2]{0:T(128)S(1)}, bf16[128,1024]{1,0:T(8,128)(2,1)}, bf16[128,1024]{1,0:T(8,128)(2,1)}, ...), branch_computations={%region_0.0_spmd, %region_1.0_spmd} | conditional | flops 22000000 | bytes 3215848 | solution.py:135
  15.5 6.0 %collective-permute-done.refs_1_ = bf16[128,1024]{1,0:T(8,128)(2,1)} collective-permute-done((bf16[128,1024]{1,0:T(8,128)(2,1)}, bf16[128,1024]{1,0:T(8,128)(2,1)}, u32[]{:S(2)}, u32[]{:S(2)}) %collective-permute-start) | collective-permute-done | bytes 262176 | tf_op jit(solution)/shard_map/cond/branch_1_fun/ppermute | solution.py:58
  25.7 5.6 %collective-permute-done.13.refs_1_.refs_7_.refs_2_ = bf16[128,1024]{1,0:T(8,128)(2,1)} collective-permute-done((bf16[128,1024]{1,0:T(8,128)(2,1)}, bf16[128,1024]{1,0:T(8,128)(2,1)}, u32[]{:S(2)}, u32[]{:S(2)}) %collective-permute-start.13) | collective-permute-done | bytes 262176 | tf_op jit(solution)/shard_map/ppermute | solution.py:58
  39.2 13.1 %collective-permute-done.16.refs_9_.refs_4_ = bf16[384,1024]{1,0:T(8,128)(2,1)} collective-permute-done((bf16[384,1024]{1,0:T(8,128)(2,1)}, bf16[384,1024]{1,0:T(8,128)(2,1)}, u32[]{:S(2)}, u32[]{:S(2)}) %collective-permute-start.16) | collective-permute-done | bytes 786464 | tf_op jit(solution)/shard_map/ppermute | solution.py:58
  52.3 6.9 %shard_map.320 = (bf16[512,768]{1,0:T(8,128)(2,1)}, bf16[4,512,512]{2,1,0:T(8,128)(2,1)}, bf16[512,256]{1,0:T(8,128)(2,1)}) custom-call(s32[2]{0:T(128)S(1)} %pad_add_fusion.refs_0_, s32[1,4]{1,0:T(1,128)} %refs_1_.7, s32[4,128]{1,0:T(4,128)} %bitcast.21, f32[1,768]{1,0:T(1,128)} %broadcast_in_dim.10.refs_3_, bf16[256,1024]{1,0:T(8,128)(2,1)} %get-tuple-element.251.refs_4_, ...), custom_call_target="tpu_custom_call" | custom-call | flops 11000000 | bytes 35000 | tf_op jit(solution)/shard_map/pallas_call | solution.py:114
  60.4 3.6 %shard_map.321 = (f32[256,1024]{1,0:T(8,128)}, bf16[256,1024]{1,0:T(8,128)(2,1)}, bf16[128,1024]{1,0:T(8,128)(2,1)}, bf16[384,1024]{1,0:T(8,128)(2,1)}) custom-call(bf16[512,256]{1,0:T(8,128)(2,1)} %get-tuple-element.256.refs_0_, bf16[128,1024]{1,0:T(8,128)(2,1)} %shard_map.317.refs_0_.refs_6_.refs_1_, ...), custom_call_target="tpu_custom_call" | custom-call | flops 11000000 | bytes 35000 | tf_op jit(solution)/shard_map/pallas_call | solution.py:114
  69.7 15.9 %conditional.7 = ((f32[128,1024]{1,0:T(8,128)}, f32[128,1024]{1,0:T(8,128)}, f32[128,1]{1,0:T(8,128)S(1)}, bf16[128,1024]{1,0:T(8,128)(2,1)})) conditional(s32[]{:T(128)} %bitcast.3, () %tuple.56, (bf16[256,1024]{1,0:T(8,128)(2,1)}, f32[256,1024]{1,0:T(8,128)}, f32[8,1024]{1,0:T(8,128)S(1)}, bf16[128,1024]{1,0:T(8,128)(2,1)}) %tuple.57), branch_computations={%region_2.0_spmd, %region_3.0_spmd} | conditional | flops 11393216 | bytes 7375176 | solution.py:135
  75.3 6.9 %collective-permute-done.8.refs_3_ = bf16[128,1024]{1,0:T(8,128)(2,1)S(1)} collective-permute-done((bf16[128,1024]{1,0:T(8,128)(2,1)S(1)}, bf16[128,1024]{1,0:T(8,128)(2,1)S(1)}, u32[]{:S(2)}, u32[]{:S(2)}) %collective-permute-start.8) | collective-permute-done | bytes 262176 | tf_op jit(solution)/shard_map/cond/branch_1_fun/ppermute | solution.py:58
  82.9 2.7 %branch_1_fun.10 = (f32[128,1024]{1,0:T(8,128)}, f32[128,1024]{1,0:T(8,128)}, f32[128,1]{1,0:T(8,128)S(1)}, bf16[128,1024]{1,0:T(8,128)(2,1)}) custom-call(f32[8,1024]{1,0:T(8,128)S(1)} %get-tuple-element.100.refs_0_, f32[256,1024]{1,0:T(8,128)} %get-tuple-element.101.refs_1_, bf16[256,1024]{1,0:T(8,128)(2,1)} %copy-done.4, bf16[128,1024]{1,0:T(8,128)(2,1)} %copy-done.7, ...), custom_call_target="tpu_custom_call" | custom-call | flops 11000000 | bytes 35000 | tf_op jit(solution)/shard_map/cond/branch_1_fun/pallas_call | solution.py:114
  87.8 14.9 %conditional.8 = (bf16[128,1024]{1,0:T(8,128)(2,1)}, bf16[128,1024]{1,0:T(8,128)(2,1)}, bf16[128,1024]{1,0:T(8,128)(2,1)}, bf16[512,1024]{1,0:T(8,128)(2,1)}, f32[512,1024]{1,0:T(8,128)}) conditional(s32[]{:T(128)} %bitcast.3, () %tuple.55, (bf16[128,1024]{1,0:T(8,128)(2,1)}, f32[1024]{0:T(1024)S(1)}, bf16[128,1024]{1,0:T(8,128)(2,1)}, ...), branch_computations={%region_4.0_spmd, %region_5.0_spmd} | conditional | flops 11000000 | bytes 3932212 | solution.py:135
  89.4 5.8 %collective-permute-done.2.refs_2_ = bf16[128,1024]{1,0:T(8,128)(2,1)} collective-permute-done((bf16[128,1024]{1,0:T(8,128)(2,1)}, bf16[128,1024]{1,0:T(8,128)(2,1)}, u32[]{:S(2)}, u32[]{:S(2)}) %collective-permute-start.2) | collective-permute-done | bytes 262176 | tf_op jit(solution)/shard_map/cond/branch_1_fun/ppermute | solution.py:58
  97.0 5.4 %branch_1_fun.11 = (bf16[512,1024]{1,0:T(8,128)(2,1)}, f32[512,1024]{1,0:T(8,128)}) custom-call(f32[1,1024]{1,0:T(1,128)S(1)} %bitcast.15, bf16[128,1024]{1,0:T(8,128)(2,1)} %get-tuple-element.104.refs_1_, bf16[128,1024]{1,0:T(8,128)(2,1)} %collective-permute-done.2.refs_2_, bf16[128,1024]{1,0:T(8,128)(2,1)} %collective-permute-done.3.refs_3_, ...), custom_call_target="tpu_custom_call" | custom-call | flops 11000000 | bytes 35000 | tf_op jit(solution)/shard_map/cond/branch_1_fun/pallas_call | solution.py:114
  102.7 4.2 %shard_map.322 = (f32[256,1024]{1,0:T(8,128)}, bf16[256,1024]{1,0:T(8,128)(2,1)}) custom-call(bf16[512,1024]{1,0:T(8,128)(2,1)} %get-tuple-element.262.refs_0_.refs_4_, bf16[128,1024]{1,0:T(8,128)(2,1)} %get-tuple-element.261.refs_1_.refs_4_, bf16[128,1024]{1,0:T(8,128)(2,1)} %collective-permute-done.22.refs_2_.refs_5_, ...), custom_call_target="tpu_custom_call" | custom-call | flops 11000000 | bytes 35000 | tf_op jit(solution)/shard_map/pallas_call | solution.py:114
  112.5 7.0 %collective-permute-done.29.refs_5_ = bf16[128,1024]{1,0:T(8,128)(2,1)} collective-permute-done((bf16[128,1024]{1,0:T(8,128)(2,1)S(1)}, bf16[128,1024]{1,0:T(8,128)(2,1)}, u32[]{:S(2)}, u32[]{:S(2)}) %collective-permute-start.29) | collective-permute-done | bytes 262176 | tf_op jit(solution)/shard_map/ppermute | solution.py:58
  119.5 3.7 %shard_map.323 = (bf16[128,1024]{1,0:T(8,128)(2,1)}, f32[128,1024]{1,0:T(8,128)}, bf16[128,1024]{1,0:T(8,128)(2,1)}, f32[8,1024]{1,0:T(8,128)}) custom-call(s32[2]{0:T(128)S(1)} %pad_add_fusion.refs_0_, s32[1,4]{1,0:T(1,128)} %refs_1_.7, f32[8,1024]{1,0:T(8,128)S(1)} %get-tuple-element.250.refs_2_, f32[256,1024]{1,0:T(8,128)} %get-tuple-element.263.refs_3_, ...), custom_call_target="tpu_custom_call" | custom-call | flops 11000000 | bytes 35000 | tf_op jit(solution)/shard_map/pallas_call | solution.py:114
  124.8 6.2 %collective-permute-done.30.refs_1_ = bf16[128,1024]{1,0:T(8,128)(2,1)S(1)} collective-permute-done((bf16[128,1024]{1,0:T(8,128)(2,1)}, bf16[128,1024]{1,0:T(8,128)(2,1)S(1)}, u32[]{:S(2)}, u32[]{:S(2)}) %collective-permute-start.30) | collective-permute-done | bytes 262176 | tf_op jit(solution)/shard_map/ppermute | solution.py:58
  133.4 3.8 %shard_map.324 = (f32[128,1024]{1,0:T(8,128)}, bf16[256,1024]{1,0:T(8,128)(2,1)}, bf16[256,1024]{1,0:T(8,128)(2,1)}, bf16[256,1024]{1,0:T(8,128)(2,1)}, bf16[128,1024]{1,0:T(8,128)(2,1)}) custom-call(bf16[128,1024]{1,0:T(8,128)(2,1)} %get-tuple-element.270.refs_0_, bf16[128,1024]{1,0:T(8,128)(2,1)} %copy-done.6, ...), custom_call_target="tpu_custom_call" | custom-call | flops 11000000 | bytes 35000 | tf_op jit(solution)/shard_map/pallas_call | solution.py:114
  140.4 6.4 %shard_map.325 = (bf16[512,1024]{1,0:T(8,128)(2,1)}, f32[256,1024]{1,0:T(8,128)}, bf16[256,1024]{1,0:T(8,128)(2,1)}, f32[1,1024]{1,0:T(1,128)S(1)}) custom-call(bf16[128,1024]{1,0:T(8,128)(2,1)} %get-tuple-element.270.refs_0_, bf16[128,1024]{1,0:T(8,128)(2,1)} %copy-done.6, bf16[128,1024]{1,0:T(8,128)(2,1)} %collective-permute-done.31.refs_2_, ...), custom_call_target="tpu_custom_call" | custom-call | flops 11000000 | bytes 35000 | tf_op jit(solution)/shard_map/pallas_call | solution.py:114
  146.9 12.9 %conditional.9 = (f32[128,1024]{1,0:T(8,128)}, bf16[256,1024]{1,0:T(8,128)(2,1)}, bf16[256,1024]{1,0:T(8,128)(2,1)}, bf16[256,1024]{1,0:T(8,128)(2,1)}, bf16[128...) conditional(s32[]{:T(128)} %bitcast.3, () %tuple.61, (bf16[256,1024]{1,0:T(8,128)(2,1)}, ...), branch_computations={%region_6.0_spmd, %region_7.0_spmd} | conditional | flops 11393216 | bytes 4229440 | solution.py:135
  152.6 3.9 %branch_1_fun.12 = (f32[128,1024]{1,0:T(8,128)}, bf16[256,1024]{1,0:T(8,128)(2,1)}, bf16[256,1024]{1,0:T(8,128)(2,1)}, bf16[256,1024]{1,0:T(8,128)(2,1)}, bf16[128,1024]{1,0:T(8,128)(2,1)}) custom-call(bf16[128,1024]{1,0:T(8,128)(2,1)} %get-tuple-element.117.refs_0_, bf16[128,1024]{1,0:T(8,128)(2,1)} %get-tuple-element.118.refs_1_, ...), custom_call_target="tpu_custom_call" | custom-call | flops 11000000 | bytes 35000 | tf_op jit(solution)/shard_map/cond/branch_1_fun/pallas_call | solution.py:114
  156.4 3.3 %collective-permute-done.10 = bf16[128,1024]{1,0:T(8,128)(2,1)} collective-permute-done((bf16[128,1024]{1,0:T(8,128)(2,1)}, bf16[128,1024]{1,0:T(8,128)(2,1)}, u32[]{:S(2)}, u32[]{:S(2)}) %collective-permute-start.10) | collective-permute-done | bytes 262176 | tf_op jit(solution)/shard_map/cond/branch_1_fun/ppermute | solution.py:58
  166.1 3.7 %shard_map.326 = (f32[128,1024]{1,0:T(8,128)}, bf16[144,1024]{1,0:T(8,128)(2,1)}) custom-call(s32[2]{0:T(128)S(1)} %pad_add_fusion.refs_0_, f32[128,1]{1,0:T(8,128)S(1)} %get-tuple-element.268.refs_1_, f32[8,1024]{1,0:T(8,128)S(1)} %get-tuple-element.250.refs_2_, f32[8,1024]{1,0:T(8,128)} %get-tuple-element.269.refs_3_, ...), custom_call_target="tpu_custom_call" | custom-call | flops 11000000 | bytes 35000 | tf_op jit(solution)/shard_map/pallas_call | solution.py:114
  169.8 22.3 %conditional.10 = (f32[256,1024]{1,0:T(8,128)}, bf16[256,1024]{1,0:T(8,128)(2,1)}, f32[128,1024]{1,0:T(8,128)}, bf16[256,1024]{1,0:T(8,128)(2,1)}, bf16[272,1024...) conditional(s32[]{:T(128)} %bitcast.3, () %tuple.60, ...), branch_computations={%region_8.0_spmd, %region_9.0_spmd} | conditional | flops 22000000 | bytes 4030548 | solution.py:135
  171.6 5.9 %collective-permute-done.5.refs_1_ = bf16[144,1024]{1,0:T(8,128)(2,1)} collective-permute-done((bf16[144,1024]{1,0:T(8,128)(2,1)}, bf16[144,1024]{1,0:T(8,128)(2,1)}, u32[]{:S(2)}, u32[]{:S(2)}) %collective-permute-start.5) | collective-permute-done | bytes 294944 | tf_op jit(solution)/shard_map/cond/branch_1_fun/ppermute | solution.py:58
  181.9 10.2 %branch_1_fun.14 = (bf16[512,768]{1,0:T(8,128)(2,1)}, f32[256,1024]{1,0:T(8,128)}, bf16[256,1024]{1,0:T(8,128)(2,1)}, f32[128,1024]{1,0:T(8,128)}, bf16[256,1024...) custom-call(f32[1,1024]{1,0:T(1,128)S(1)} %get-tuple-element.129.ref, ...), custom_call_target="tpu_custom_call" | custom-call | flops 11000000 | bytes 35000 | tf_op jit(solution)/shard_map/cond/branch_1_fun/pallas_call | solution.py:114
  199.6 15.4 %conditional.11 = (f32[128,1024]{1,0:T(8,128)}) conditional(s32[]{:T(128)} %bitcast.3, () %tuple.59, (bf16[256,1024]{1,0:T(8,128)(2,1)}, f32[256,1024]{1,0:T(8,128)}, s32[2]{0:T(128)S(1)}, f32[128,1024]{1,0:T(8,128)}, f32[128,1024]{1,0:T(8,128)}) %tuple.64), branch_computations={%region_10.0_spmd, %region_11.0_spmd} | conditional | flops 11393216 | bytes 6326572 | solution.py:135
  205.2 7.0 %collective-permute-done.12.refs_3_ = bf16[128,1024]{1,0:T(8,128)(2,1)} collective-permute-done((bf16[128,1024]{1,0:T(8,128)(2,1)S(1)}, bf16[128,1024]{1,0:T(8,128)(2,1)}, u32[]{:S(2)}, u32[]{:S(2)}) %collective-permute-start.12) | collective-permute-done | bytes 262176 | tf_op jit(solution)/shard_map/cond/branch_1_fun/ppermute | solution.py:58
  212.1 2.9 %branch_1_fun.15 = f32[128,1024]{1,0:T(8,128)} custom-call(s32[2]{0:T(128)S(1)} %get-tuple-element.151.refs_0_, f32[256,1024]{1,0:T(8,128)} %get-tuple-element.152.refs_1_, bf16[256,1024]{1,0:T(8,128)(2,1)} %copy-done.5, bf16[128,1024]{1,0:T(8,128)(2,1)} %collective-permute-done.12.refs_3_, f32[128,1024]{1,0:T(8,128)} %get-tuple-element.154.refs_4_, ...), custom_call_target="tpu_custom_call" | custom-call | flops 11000000 | bytes 35000 | tf_op jit(solution)/shard_map/cond/branch_1_fun/pallas_call | solution.py:114
  215.1 7.4 %collective-permute-done.42.refs_10_.refs_3_ = bf16[128,1024]{1,0:T(8,128)(2,1)} collective-permute-done((bf16[128,1024]{1,0:T(8,128)(2,1)}, bf16[128,1024]{1,0:T(8,128)(2,1)}, u32[]{:S(2)}, u32[]{:S(2)}) %collective-permute-start.42) | collective-permute-done | bytes 262176 | tf_op jit(solution)/shard_map/ppermute | solution.py:58
  223.3 2.8 %shard_map.329 = (bf16[144,1024]{1,0:T(8,128)(2,1)}, bf16[144,1024]{1,0:T(8,128)(2,1)}, bf16[400,1024]{1,0:T(8,128)(2,1)}) custom-call(bf16[256,1024]{1,0:T(8,128)(2,1)} %get-tuple-element.297.refs_0_, bf16[272,1024]{1,0:T(8,128)(2,1)} %collective-permute-done.36.refs_1_, bf16[128,1024]{1,0:T(8,128)(2,1)} %get-tuple-element.299.refs_2_, ...), custom_call_target="tpu_custom_call" | custom-call | flops 11000000 | bytes 35000 | tf_op jit(solution)/shard_map/pallas_call | solution.py:114
  228.9 16.3 %collective-permute-done.45.refs_4_.refs_9_ = bf16[400,1024]{1,0:T(8,128)(2,1)} collective-permute-done((bf16[400,1024]{1,0:T(8,128)(2,1)}, bf16[400,1024]{1,0:T(8,128)(2,1)}, u32[]{:S(2)}, u32[]{:S(2)}) %collective-permute-start.45) | collective-permute-done | bytes 819232 | tf_op jit(solution)/shard_map/ppermute | solution.py:58
  (136 shorter events, 100.0 us)
Async XLA Ops:
  2.5 23.2 %collective-permute-start.15 = (bf16[128,1024]{1,0:T(8,128)(2,1)}, bf16[128,1024]{1,0:T(8,128)(2,1)}, u32[]{:S(2)}, u32[]{:S(2)}) collective-permute-start(bf16[128,1024]{1,0:T(8,128)(2,1)} %shard_map.317.refs_0_.refs_6_.refs_1_), channel_id=1, source_target_pairs={{0,8},{4,12},{8,0},{12,4},{16,24},{20,28},{24,16},{28,20},{1,9},{5... | collective-permute-start | bytes 786440 | tf_op jit(solution)/shard_map/ppermute | solution.py:58
  5.5 20.2 %collective-permute-start.14 = (bf16[128,1024]{1,0:T(8,128)(2,1)}, bf16[128,1024]{1,0:T(8,128)(2,1)}, u32[]{:S(2)}, u32[]{:S(2)}) collective-permute-start(bf16[128,1024]{1,0:T(8,128)(2,1)} %shard_map.317.refs_0_.refs_6_.refs_1_), channel_id=1, source_target_pairs={{0,24},{4,28},{8,16},{12,20},{16,8},{20,12},{24,0},{28,4},{1,25},{... | collective-permute-start | bytes 786440 | tf_op jit(solution)/shard_map/ppermute | solution.py:58
  8.0 23.3 %collective-permute-start.13 = (bf16[128,1024]{1,0:T(8,128)(2,1)}, bf16[128,1024]{1,0:T(8,128)(2,1)}, u32[]{:S(2)}, u32[]{:S(2)}) collective-permute-start(bf16[128,1024]{1,0:T(8,128)(2,1)} %shard_map.317.refs_0_.refs_6_.refs_1_), channel_id=1, source_target_pairs={{0,16},{4,20},{8,24},{12,28},{16,0},{20,4},{24,8},{28,12},{1,17},{... | collective-permute-start | bytes 786440 | tf_op jit(solution)/shard_map/ppermute | solution.py:58
  10.3 28.9 %collective-permute-start.17 = (bf16[384,1024]{1,0:T(8,128)(2,1)}, bf16[384,1024]{1,0:T(8,128)(2,1)S(1)}, u32[]{:S(2)}, u32[]{:S(2)}) collective-permute-start(bf16[384,1024]{1,0:T(8,128)(2,1)} %shard_map.318.refs_0_.refs_7_), channel_id=1, source_target_pairs={{0,4},{4,0},{8,12},{12,8},{16,20},{20,16},{24,28},{28,24},{1,5},{5... | collective-permute-start | bytes 2359304 | tf_op jit(solution)/shard_map/ppermute | solution.py:58
  33.5 18.8 %collective-permute-start.16 = (bf16[384,1024]{1,0:T(8,128)(2,1)}, bf16[384,1024]{1,0:T(8,128)(2,1)}, u32[]{:S(2)}, u32[]{:S(2)}) collective-permute-start(bf16[384,1024]{1,0:T(8,128)(2,1)} %get-tuple-element.254), channel_id=1, source_target_pairs={{0,4},{4,0},{8,12},{12,8},{16,20},{20,16},{24,28},{28,24},{1,5},{5... | collective-permute-start | bytes 2359304 | tf_op jit(solution)/shard_map/ppermute | solution.py:58
  35.1 24.1 %collective-permute-start.20 = (bf16[128,1024]{1,0:T(8,128)(2,1)}, bf16[128,1024]{1,0:T(8,128)(2,1)}, u32[]{:S(2)}, u32[]{:S(2)}) collective-permute-start(bf16[128,1024]{1,0:T(8,128)(2,1)} %get-tuple-element.255.refs_12_.refs_13_), channel_id=1, source_target_pairs={{0,8},{4,12},{8,0},{12,4},{16,24},{20,28},{24,16},{28,20},{1,9},{5... | collective-permute-start | bytes 786440 | tf_op jit(solution)/shard_map/ppermute | solution.py:58
  35.1 24.1 %collective-permute-start.19 = (bf16[128,1024]{1,0:T(8,128)(2,1)}, bf16[128,1024]{1,0:T(8,128)(2,1)}, u32[]{:S(2)}, u32[]{:S(2)}) collective-permute-start(bf16[128,1024]{1,0:T(8,128)(2,1)} %get-tuple-element.255.refs_12_.refs_13_), channel_id=1, source_target_pairs={{0,24},{4,28},{8,16},{12,20},{16,8},{20,12},{24,0},{28,4},{1,25},{... | collective-permute-start | bytes 786440 | tf_op jit(solution)/shard_map/ppermute | solution.py:58
  37.7 22.6 %collective-permute-start.18 = (bf16[128,1024]{1,0:T(8,128)(2,1)}, bf16[128,1024]{1,0:T(8,128)(2,1)}, u32[]{:S(2)}, u32[]{:S(2)}) collective-permute-start(bf16[128,1024]{1,0:T(8,128)(2,1)} %get-tuple-element.255.refs_12_.refs_13_), channel_id=1, source_target_pairs={{0,16},{4,20},{8,24},{12,28},{16,0},{20,4},{24,8},{28,12},{1,17},{... | collective-permute-start | bytes 786440 | tf_op jit(solution)/shard_map/ppermute | solution.py:58
  64.0 23.8 %collective-permute-start.21 = (bf16[384,1024]{1,0:T(8,128)(2,1)}, bf16[384,1024]{1,0:T(8,128)(2,1)}, u32[]{:S(2)}, u32[]{:S(2)}) collective-permute-start(bf16[384,1024]{1,0:T(8,128)(2,1)} %get-tuple-element.260), channel_id=1, source_target_pairs={{0,4},{4,0},{8,12},{12,8},{16,20},{20,16},{24,28},{28,24},{1,5},{5... | collective-permute-start | bytes 2359304 | tf_op jit(solution)/shard_map/ppermute | solution.py:58
  64.6 21.1 %collective-permute-start.23 = (bf16[128,1024]{1,0:T(8,128)(2,1)}, bf16[128,1024]{1,0:T(8,128)(2,1)}, u32[]{:S(2)}, u32[]{:S(2)}) collective-permute-start(bf16[128,1024]{1,0:T(8,128)(2,1)} %get-tuple-element.261.refs_1_.refs_4_), channel_id=1, source_target_pairs={{0,24},{4,28},{8,16},{12,20},{16,8},{20,12},{24,0},{28,4},{1,25},{... | collective-permute-start | bytes 786440 | tf_op jit(solution)/shard_map/ppermute | solution.py:58
  66.8 20.4 %collective-permute-start.22 = (bf16[128,1024]{1,0:T(8,128)(2,1)}, bf16[128,1024]{1,0:T(8,128)(2,1)}, u32[]{:S(2)}, u32[]{:S(2)}) collective-permute-start(bf16[128,1024]{1,0:T(8,128)(2,1)} %get-tuple-element.261.refs_1_.refs_4_), channel_id=1, source_target_pairs={{0,16},{4,20},{8,24},{12,28},{16,0},{20,4},{24,8},{28,12},{1,17},{... | collective-permute-start | bytes 786440 | tf_op jit(solution)/shard_map/ppermute | solution.py:58
  67.6 20.2 %collective-permute-start.24 = (bf16[128,1024]{1,0:T(8,128)(2,1)}, bf16[128,1024]{1,0:T(8,128)(2,1)}, u32[]{:S(2)}, u32[]{:S(2)}) collective-permute-start(bf16[128,1024]{1,0:T(8,128)(2,1)} %slice.37), channel_id=1, source_target_pairs={{0,8},{4,12},{8,0},{12,4},{16,24},{20,28},{24,16},{28,20},{1,9},{5... | collective-permute-start | bytes 786440 | tf_op jit(solution)/shard_map/ppermute | solution.py:58
  73.8 8.4 %collective-permute-start.8 = (bf16[128,1024]{1,0:T(8,128)(2,1)S(1)}, bf16[128,1024]{1,0:T(8,128)(2,1)S(1)}, u32[]{:S(2)}, u32[]{:S(2)}) collective-permute-start(bf16[128,1024]{1,0:T(8,128)(2,1)S(1)} %add_convert_fusion), channel_id=1, source_target_pairs={{0,2},{1,3},{2,0},{3,1},{4,6},{5,7},{6,4},{7,5},{8,10},{9,11},{10,... | collective-permute-start | bytes 786440 | tf_op jit(solution)/shard_map/cond/branch_1_fun/ppermute | solution.py:58
  85.6 17.1 %collective-permute-start.27 = (bf16[128,1024]{1,0:T(8,128)(2,1)}, bf16[128,1024]{1,0:T(8,128)(2,1)}, u32[]{:S(2)}, u32[]{:S(2)}) collective-permute-start(bf16[128,1024]{1,0:T(8,128)(2,1)} %get-tuple-element.261.refs_1_.refs_4_), channel_id=1, source_target_pairs={{0,8},{4,12},{8,0},{12,4},{16,24},{20,28},{24,16},{28,20},{1,9},{5... | collective-permute-start | bytes 786440 | tf_op jit(solution)/shard_map/ppermute | solution.py:58
  85.7 17.0 %collective-permute-start.26 = (bf16[128,1024]{1,0:T(8,128)(2,1)}, bf16[128,1024]{1,0:T(8,128)(2,1)}, u32[]{:S(2)}, u32[]{:S(2)}) collective-permute-start(bf16[128,1024]{1,0:T(8,128)(2,1)} %collective-permute-done.23.refs_3_.refs_6_), channel_id=1, source_target_pairs={{0,4},{4,0},{8,12},{12,8},{16,20},{20,16},{24,28},{28,24},{1,5},{5... | collective-permute-start | bytes 786440 | tf_op jit(solution)/shard_map/ppermute | solution.py:58
  87.3 15.4 %collective-permute-start.25 = (bf16[128,1024]{1,0:T(8,128)(2,1)}, bf16[128,1024]{1,0:T(8,128)(2,1)}, u32[]{:S(2)}, u32[]{:S(2)}) collective-permute-start(bf16[128,1024]{1,0:T(8,128)(2,1)} %collective-permute-done.22.refs_2_.refs_5_), channel_id=1, source_target_pairs={{0,4},{4,0},{8,12},{12,8},{16,20},{20,16},{24,28},{28,24},{1,5},{5... | collective-permute-start | bytes 786440 | tf_op jit(solution)/shard_map/ppermute | solution.py:58
  111.0 8.5 %collective-permute-start.29 = (bf16[128,1024]{1,0:T(8,128)(2,1)S(1)}, bf16[128,1024]{1,0:T(8,128)(2,1)}, u32[]{:S(2)}, u32[]{:S(2)}) collective-permute-start(bf16[128,1024]{1,0:T(8,128)(2,1)S(1)} %add_convert_fusion.3), channel_id=1, source_target_pairs={{0,2},{1,3},{2,0},{3,1},{4,6},{5,7},{6,4},{7,5},{8,10},{9,11},{10,... | collective-permute-start | bytes 786440 | tf_op jit(solution)/shard_map/ppermute | solution.py:58
  137.2 23.4 %collective-permute-start.33 = (bf16[256,1024]{1,0:T(8,128)(2,1)}, bf16[256,1024]{1,0:T(8,128)(2,1)}, u32[]{:S(2)}, u32[]{:S(2)}) collective-permute-start(bf16[256,1024]{1,0:T(8,128)(2,1)} %get-tuple-element.288), channel_id=1, source_target_pairs={{0,4},{4,0},{8,12},{12,8},{16,20},{20,16},{24,28},{28,24},{1,5},{5... | collective-permute-start | bytes 1572872 | tf_op jit(solution)/shard_map/ppermute | solution.py:58
  138.8 21.9 %collective-permute-start.34 = (bf16[256,1024]{1,0:T(8,128)(2,1)}, bf16[256,1024]{1,0:T(8,128)(2,1)}, u32[]{:S(2)}, u32[]{:S(2)}) collective-permute-start(bf16[256,1024]{1,0:T(8,128)(2,1)} %get-tuple-element.290), channel_id=1, source_target_pairs={{0,8},{4,12},{8,0},{12,4},{16,24},{20,28},{24,16},{28,20},{1,9},{5... | collective-permute-start | bytes 1572872 | tf_op jit(solution)/shard_map/ppermute | solution.py:58
  151.1 8.7 %collective-permute-start.10 = (bf16[128,1024]{1,0:T(8,128)(2,1)}, bf16[128,1024]{1,0:T(8,128)(2,1)}, u32[]{:S(2)}, u32[]{:S(2)}) collective-permute-start(bf16[128,1024]{1,0:T(8,128)(2,1)} %add_convert_fusion.1), channel_id=1, source_target_pairs={{0,2},{1,3},{2,0},{3,1},{4,6},{5,7},{6,4},{7,5},{8,10},{9,11},{10,... | collective-permute-start | bytes 786440 | tf_op jit(solution)/shard_map/cond/branch_1_fun/ppermute | solution.py:58
  159.7 33.6 %collective-permute-start.37 = (bf16[256,1024]{1,0:T(8,128)(2,1)}, bf16[256,1024]{1,0:T(8,128)(2,1)}, u32[]{:S(2)}, u32[]{:S(2)}) collective-permute-start(bf16[256,1024]{1,0:T(8,128)(2,1)} %get-tuple-element.302), channel_id=1, source_target_pairs={{0,4},{4,0},{8,12},{12,8},{16,20},{20,16},{24,28},{28,24},{1,5},{5... | collective-permute-start | bytes 1572872 | tf_op jit(solution)/shard_map/ppermute | solution.py:58
  160.3 34.6 %collective-permute-start.38 = (bf16[256,1024]{1,0:T(8,128)(2,1)}, bf16[256,1024]{1,0:T(8,128)(2,1)}, u32[]{:S(2)}, u32[]{:S(2)}) collective-permute-start(bf16[256,1024]{1,0:T(8,128)(2,1)} %get-tuple-element.304), channel_id=1, source_target_pairs={{0,8},{4,12},{8,0},{12,4},{16,24},{20,28},{24,16},{28,20},{1,9},{5... | collective-permute-start | bytes 1572872 | tf_op jit(solution)/shard_map/ppermute | solution.py:58
  162.9 32.0 %collective-permute-start.39 = (bf16[128,1024]{1,0:T(8,128)(2,1)}, bf16[128,1024]{1,0:T(8,128)(2,1)}, u32[]{:S(2)}, u32[]{:S(2)}) collective-permute-start(bf16[128,1024]{1,0:T(8,128)(2,1)} %get-tuple-element.305), channel_id=1, source_target_pairs={{0,24},{4,28},{8,16},{12,20},{16,8},{20,12},{24,0},{28,4},{1,25},{... | collective-permute-start | bytes 786440 | tf_op jit(solution)/shard_map/ppermute | solution.py:58
  165.3 29.6 %collective-permute-start.40 = (bf16[128,1024]{1,0:T(8,128)(2,1)}, bf16[128,1024]{1,0:T(8,128)(2,1)}, u32[]{:S(2)}, u32[]{:S(2)}) collective-permute-start(bf16[128,1024]{1,0:T(8,128)(2,1)} %get-tuple-element.306), channel_id=1, source_target_pairs={{0,16},{4,20},{8,24},{12,28},{16,0},{20,4},{24,8},{28,12},{1,17},{... | collective-permute-start | bytes 786440 | tf_op jit(solution)/shard_map/ppermute | solution.py:58
  192.1 30.4 %collective-permute-start.35 = (bf16[272,1024]{1,0:T(8,128)(2,1)}, bf16[272,1024]{1,0:T(8,128)(2,1)S(1)}, u32[]{:S(2)}, u32[]{:S(2)}) collective-permute-start(bf16[272,1024]{1,0:T(8,128)(2,1)} %get-tuple-element.296), channel_id=1, source_target_pairs={{0,8},{4,12},{8,0},{12,4},{16,24},{20,28},{24,16},{28,20},{1,9},{5... | collective-permute-start | bytes 1671176 | tf_op jit(solution)/shard_map/ppermute | solution.py:58
  193.4 29.1 %collective-permute-start.36 = (bf16[272,1024]{1,0:T(8,128)(2,1)}, bf16[272,1024]{1,0:T(8,128)(2,1)}, u32[]{:S(2)}, u32[]{:S(2)}) collective-permute-start(bf16[272,1024]{1,0:T(8,128)(2,1)} %get-tuple-element.298), channel_id=1, source_target_pairs={{0,4},{4,0},{8,12},{12,8},{16,20},{20,16},{24,28},{28,24},{1,5},{5... | collective-permute-start | bytes 1671176 | tf_op jit(solution)/shard_map/ppermute | solution.py:58
  197.2 17.8 %collective-permute-start.41 = (bf16[128,1024]{1,0:T(8,128)(2,1)}, bf16[128,1024]{1,0:T(8,128)(2,1)}, u32[]{:S(2)}, u32[]{:S(2)}) collective-permute-start(bf16[128,1024]{1,0:T(8,128)(2,1)} %get-tuple-element.308), channel_id=1, source_target_pairs={{0,24},{4,28},{8,16},{12,20},{16,8},{20,12},{24,0},{28,4},{1,25},{... | collective-permute-start | bytes 786440 | tf_op jit(solution)/shard_map/ppermute | solution.py:58
  199.6 22.9 %collective-permute-start.42 = (bf16[128,1024]{1,0:T(8,128)(2,1)}, bf16[128,1024]{1,0:T(8,128)(2,1)}, u32[]{:S(2)}, u32[]{:S(2)}) collective-permute-start(bf16[128,1024]{1,0:T(8,128)(2,1)} %get-tuple-element.309), channel_id=1, source_target_pairs={{0,16},{4,20},{8,24},{12,28},{16,0},{20,4},{24,8},{28,12},{1,17},{... | collective-permute-start | bytes 786440 | tf_op jit(solution)/shard_map/ppermute | solution.py:58
  203.6 8.5 %collective-permute-start.12 = (bf16[128,1024]{1,0:T(8,128)(2,1)S(1)}, bf16[128,1024]{1,0:T(8,128)(2,1)}, u32[]{:S(2)}, u32[]{:S(2)}) collective-permute-start(bf16[128,1024]{1,0:T(8,128)(2,1)S(1)} %add_convert_fusion.2), channel_id=1, source_target_pairs={{0,2},{1,3},{2,0},{3,1},{4,6},{5,7},{6,4},{7,5},{8,10},{9,11},{10,... | collective-permute-start | bytes 786440 | tf_op jit(solution)/shard_map/cond/branch_1_fun/ppermute | solution.py:58
  226.0 19.2 %collective-permute-start.45 = (bf16[400,1024]{1,0:T(8,128)(2,1)}, bf16[400,1024]{1,0:T(8,128)(2,1)}, u32[]{:S(2)}, u32[]{:S(2)}) collective-permute-start(bf16[400,1024]{1,0:T(8,128)(2,1)} %get-tuple-element.312), channel_id=1, source_target_pairs={{0,4},{4,0},{8,12},{12,8},{16,20},{20,16},{24,28},{28,24},{1,5},{5... | collective-permute-start | bytes 2457608 | tf_op jit(solution)/shard_map/ppermute | solution.py:58
  226.6 23.2 %collective-permute-start.43 = (bf16[144,1024]{1,0:T(8,128)(2,1)}, bf16[144,1024]{1,0:T(8,128)(2,1)S(1)}, u32[]{:S(2)}, u32[]{:S(2)}) collective-permute-start(bf16[144,1024]{1,0:T(8,128)(2,1)} %get-tuple-element.310), channel_id=1, source_target_pairs={{0,24},{4,28},{8,16},{12,20},{16,8},{20,12},{24,0},{28,4},{1,25},{... | collective-permute-start | bytes 884744 | tf_op jit(solution)/shard_map/ppermute | solution.py:58
  228.9 23.3 %collective-permute-start.44 = (bf16[144,1024]{1,0:T(8,128)(2,1)}, bf16[144,1024]{1,0:T(8,128)(2,1)S(1)}, u32[]{:S(2)}, u32[]{:S(2)}) collective-permute-start(bf16[144,1024]{1,0:T(8,128)(2,1)} %get-tuple-element.311.refs_5_), channel_id=1, source_target_pairs={{0,16},{4,20},{8,24},{12,28},{16,0},{20,4},{24,8},{28,12},{1,17},{... | collective-permute-start | bytes 884744 | tf_op jit(solution)/shard_map/ppermute | solution.py:58
  (32 other events, 216.9 us)

commit v5 on v4

--- a/solution.py
+++ b/solution.py
@@ -58,16 +58,19 @@
     return lax.ppermute(block, axis_name, [(i, i ^ offset) for i in range(count)])
 
 
-def part(array, start, rows):
-    return array, start, rows
-
-
-def kernel_call(body, out_shape, whole=(), pieces=(), scalars=(), marks=(), scratch=(), us=QUICK):
+def part(array, start, rows, columns=None):
+    return array, start, rows, columns
+
+
+def kernel_call(body, out_shape, whole=(), pieces=(), scalars=(), marks=(), scratch=(), us=QUICK, pinned=True):
     pieces = [
-        [p if isinstance(p, tuple) else (p, 0, p.shape[0]) for p in some] for some in pieces
+        [p if isinstance(p, tuple) else part(p, 0, p.shape[0]) for p in some] for some in pieces
     ]
     buffers = [
-        pltpu.VMEM((sum(p[2] for p in some), *some[0][0].shape[1:]), some[0][0].dtype)
+        pltpu.VMEM(
+            (sum(p[2] for p in some), *((some[0][3][1],) if some[0][3] else some[0][0].shape[1:])),
+            some[0][0].dtype,
+        )
         for some in pieces
     ]
     flat = [p for some in pieces for p in some]
@@ -87,10 +90,11 @@
             k = 0
             for some, buffer in zip(pieces, buffer_refs):
                 row, mine = 0, []
-                for _, first, rows in some:
+                for _, first, rows, columns in some:
+                    place = (pl.ds(first, rows), pl.ds(*columns)) if columns else pl.ds(first, rows)
                     mine.append(
                         pltpu.make_async_copy(
-                            piece_refs[k].at[pl.ds(first, rows)],
+                            piece_refs[k].at[place],
                             buffer.at[pl.ds(row, rows)],
                             done.at[k],
                         )
@@ -116,7 +120,7 @@
         out_shape=flat_out,
         in_specs=[pl.BlockSpec(memory_space=pltpu.SMEM)] * len(scalars)
         + [inside] * len(whole)
-        + [pl.BlockSpec(memory_space=pltpu.HBM)] * len(flat)
+        + [pl.BlockSpec(memory_space=pltpu.HBM) if pinned else anywhere] * len(flat)
         + [anywhere] * len(marks),
         out_specs=[inside] * len(flat_out),
         scratch_shapes=buffers + semaphores + list(scratch),
@@ -128,6 +132,18 @@
     return jax.tree.unflatten(tree, results)
 
 
+def tie(blocks, marks):
+    pinned = pl.BlockSpec(memory_space=pltpu.HBM)
+    return pl.pallas_call(
+        lambda *refs: None,
+        out_shape=[shaped(b.shape, b.dtype) for b in blocks],
+        in_specs=[pinned] * len(blocks) + [pl.BlockSpec(memory_space=pl.ANY)] * len(marks),
+        out_specs=[pinned] * len(blocks),
+        input_output_aliases={k: k for k in range(len(blocks))},
+        cost_estimate=pl.CostEstimate(flops=0, bytes_accessed=0, transcendentals=0),
+    )(*blocks, *marks)
+
+
 def region(flag, body, *operands):
     def nothing(*some):
         return jax.tree.map(lambda x: jnp.zeros(x.shape, x.dtype), jax.eval_shape(body, *operands))
@@ -165,11 +181,24 @@
     return [pair, swap(pair, "tensor", 1)]
 
 
+def turn_kernel(need, near_ref, arrived_ref, out_ref):
+    need(0)
+    need(1)
+    out_ref[...] = low(near_ref[...] + wide(arrived_ref[...]))
+
+
 def scatter_rows(near, far):
     half = near.shape[0] // 2
-    arrived = swap(far, "tensor", 1)
-    turned = low(near[half:] + wide(arrived[half:]))
-    return [[part(near, 0, half)], [part(arrived, 0, half)], [swap(turned, "tensor", 2)]]
+    if isinstance(far, list):
+        beside, corner = (swap(f, "tensor", 1) for f in far)
+        turned = kernel_call(
+            turn_kernel, [shaped(corner.shape)], pieces=[[part(near, half, half)], [corner]]
+        )[0]
+    else:
+        arrived = swap(far, "tensor", 1)
+        beside = part(arrived, 0, half)
+        turned = low(near[half:] + wide(arrived[half:]))
+    return [[part(near, 0, half)], [beside], [swap(turned, "tensor", 2)]]
 
 
 def own_sum(need, near_ref, arrived_ref, across_ref):
@@ -278,6 +307,7 @@
         pieces=[[far], [far_in], [beside], first, *[[x] for x in (*sums, *waiting)]],
         marks=marks,
         us=us,
+        pinned=not sums,
     )
     arrived = [swap(farther_out, "dp", 6), swap(far_out, "dp", 4)]
     terms = [kept, part(above, block, block), *[part(x, 0, block) for x in arrived]]
@@ -295,7 +325,7 @@
     write(total, *refs[count:])
 
 
-def scatter_last(state, write, out_shape, marks=(), riders=()):
+def scatter_last(state, write, out_shape, marks=(), riders=(), pinned=True):
     if not paired():
         state = [lax.psum_scatter(state[0], "dp", scatter_dimension=0, tiled=True)]
     return kernel_call(
@@ -303,6 +333,7 @@
         out_shape,
         pieces=[[term] for term in [*state, *riders]],
         marks=marks,
+        pinned=pinned,
     )
 
 
@@ -371,7 +402,10 @@
         columns = slice(start, start + 256)
         total = matmul_nt(left_ref[...], right_ref[columns, inner])
         near_ref[:, columns] = total[:half]
-        far_ref[:, columns] = low(total[half:])
+        fars = far_ref if isinstance(far_ref, list) else [far_ref]
+        rows = half // len(fars)
+        for k, ref in enumerate(fars):
+            ref[:, columns] = low(total[half + k * rows : half + (k + 1) * rows])
 
 
 def attention_kernel(
@@ -434,8 +468,7 @@
         out_ref[...] = in_ref[...]
     need(0)
     need(1)
-    width = context_ref.shape[1]
-    back_into(context_ref, weights_ref, slice(3 * width, None), near_ref, far_ref)
+    back_into(context_ref, weights_ref, slice(None), near_ref, far_ref)
 
 
 def first_norm_kernel(
@@ -768,6 +801,7 @@
     )
     inner_far = far_of(inner_shard)
     inner_above = above_of(inner_shard)
+    outer_corner = above_of(beside[2 * shard_rows :]) if in_slots else []
     qkv_bias = jnp.concatenate([b_query, jnp.zeros_like(b_query), b_value])[None, :]
     qkv, probs, context = kernel_call(
         partial(attention_kernel, scale),
@@ -782,17 +816,22 @@
         marks=[inner_shard],
         scratch=[pltpu.VMEM((group_rows, group_rows), jnp.float32)],
     )
+    proj_columns = (3 * head_width, head_width)
+    proj_weights = [
+        part(*p[:3], proj_columns) if isinstance(p, tuple) else part(p, 0, p.shape[0], proj_columns)
+        for p in attn_weights
+    ]
     near, far, outer_shard, *inner_joined = kernel_call(
         project_kernel,
         [*partial_sums, shaped(inner_shard.shape), *joined],
-        pieces=[[context], attn_weights, [part(shards, 2 * shard_rows, shard_rows)]]
+        pieces=[[context], proj_weights, [part(shards, 2 * shard_rows, shard_rows)]]
         + [inner_far + inner_above] * in_slots,
+        marks=outer_corner,
     )
     inner_weights = weight_pieces(
         inner_shard, inner_far, rest_of(inner_joined), inner_above, inner_beside
     )
     outer_far = far_of(outer_shard)
-    outer_corner = above_of(beside[2 * shard_rows :]) if in_slots else []
     def first_part(near, far, tokens, small):
         terms = scatter_rows(near, far)
         return kernel_call(
@@ -808,6 +847,7 @@
         )
 
     first, unit, unit_scale, first_low = region(flag, first_part, near, far, tokens, small)
+    *outer_far, outer_shard = tie([*outer_far, outer_shard], [first_low])
     outer_weights = weight_pieces(
         outer_shard,
         outer_far,
@@ -831,7 +871,7 @@
         inner_part,
         first_low,
         inner_weights[: len(inner_weights) - len(inner_beside)],
-        outer_far + outer_corner,
+        [],
     )
     norm_rows = [first_low, *other_rows]
     near, far = kernel_call(
@@ -862,27 +902,22 @@
         hidden_grad_kernel,
         [
             shaped((group_rows, inner_width)),
-            *partial_sums,
+            partial_sums[0],
+            [shaped(own)] * 2,
             shaped((1, inner_width), jnp.float32),
         ],
         pieces=[branch_rows, outer_weights, [slope], inner_weights],
         marks=[outer_cuts[0]],
     )
 
-    def inner_grad_part(near, far, norm_rows, hidden_grad):
-        terms = scatter_rows(near, far)
-        inner_cuts = kernel_call(
-            single_grad_kernel,
-            weight_cuts(model_width, inner_width),
-            pieces=[norm_rows, [hidden_grad]],
-            marks=[terms[1][0][0]],
-        )
-        return inner_cuts, [some[0][0] if isinstance(some[0], tuple) else some[0] for some in terms[1:]]
-
-    inner_cuts, (arrived, across) = region(
-        flag, inner_grad_part, near, far, norm_rows, hidden_grad
-    )
-    outer_terms, outer_beside, _ = scatter_second(outer_state, [across])
+    terms = scatter_rows(near, far)
+    inner_cuts = kernel_call(
+        single_grad_kernel,
+        weight_cuts(model_width, inner_width),
+        pieces=[norm_rows, [hidden_grad]],
+        marks=terms[1],
+    )
+    outer_terms, outer_beside, _ = scatter_second(outer_state, [inner_cuts[0]])
     outer_mark = [outer_beside] if in_slots else []
     mix_grad, proj_grad = kernel_call(
         partial(first_back_kernel, in_slots),
@@ -890,13 +925,12 @@
         scalars=[ranks],
         whole=[unit_scale, small, second_sums],
         pieces=[
-            [part(near, 0, piece_rows)],
-            [part(arrived, 0, piece_rows)],
-            [across],
+            *terms,
             [second_grad],
             [unit],
         ],
         scratch=[pltpu.VMEM((RIDERS, model_width), jnp.float32)],
+        us=4 * SLOW,
     )
     inner_state = scatter_first(inner_cuts)
 
@@ -930,7 +964,7 @@
     near, far, *attn_cuts, sums = region(flag, attention_back_part, proj_grad, outer_mark)
     attn_state = scatter_first(attn_cuts)
     inner_terms, inner_beside, _ = scatter_second(
-        inner_state, [attn_state[0], *[t[0] for t in outer_terms[2:]]], us=SLOW
+        inner_state, [attn_state[0], *[t[0] for t in outer_terms[2:]]], us=8 * SLOW
     )
 
     def tokens_part(near, far, mix_grad, mark):
@@ -969,6 +1003,7 @@
         + [shaped((model_width,), jnp.float32)] * 6,
         [dw_outer, dw_inner],
         riders,
+        False,
     )
     db_proj, dgain_attn, dshift_attn, db_outer, dgain_ffn, dshift_ffn = shared
     return (

time: 256 us -> 253 us (0.988)
  starting transfers between devices: 47.5 us -> 44.8 us
    ppermute x46 -> x47, starting transfers between devices: 47.5 us -> 44.8 us  [swap(): lax.ppermute(block, axis_name, [(i, i ^ offset) for i in range(count)])]
    convert_element_type x4 -> x3, other arithmetic: 5.2 us -> 3.31 us  [low(): return value.astype(jnp.bfloat16)]
    pallas_call x24 -> x25, Pallas kernels: 83.5 us -> 85 us  [kernel_call(): pl.pallas_call(run, out_shape=flat_out, in_specs=[pl.BlockSpec(memory_spa...]
    ppermute x46 -> x47, waiting for transfers between devices: 111 us -> 110 us  [swap(): lax.ppermute(block, axis_name, [(i, i ^ offset) for i in range(count)])]
  transfers between devices with their start and end apart: 46 -> 47, of which waited for: 22 -> 22; matrix products, arithmetic and copies ran while one was open for 2% -> 1% of each run, Pallas kernels for 24% -> 25%
where the time goes in v5:
time: 253 us; the launch traced here: 252 us
  waiting for transfers between devices  110 us (43%)
  Pallas kernels  85 us (34%)
  starting transfers between devices  44.8 us (18%)
  local copies, waits for them, and re-layouts  6.74 us (3%)
  other arithmetic  3.4 us (1%)
    ppermute x47, waiting for transfers between devices, swap(): lax.ppermute(block, axis_name, [(i, i ^ offset) for i in range(count)])  110 us
    pallas_call x25, Pallas kernels, kernel_call(): pl.pallas_call(run, out_shape=flat_out, in_specs=[pl.BlockSpec(memory_spa...  85 us
    ppermute x47, starting transfers between devices, swap(): lax.ppermute(block, axis_name, [(i, i ^ offset) for i in range(count)])  44.8 us
  transfers between devices with their start and end apart: 47, of which 22 were waited for; matrix products, arithmetic and copies ran while one was open for 1% of the time, Pallas kernels for 25%

profile of v5, /device:TPU:0, one launch (start us, length us, event | category | flops | bytes accessed | tf_op | source)
XLA Modules:
  0.0 252.1 jit_solution(17721524357533533719)
XLA Ops:
  2.5 3.0 %collective-permute-start.13 = (bf16[128,1024]{1,0:T(8,128)(2,1)}, bf16[128,1024]{1,0:T(8,128)(2,1)}, u32[]{:S(2)}, u32[]{:S(2)}) collective-permute-start(bf16[128,1024]{1,0:T(8,128)(2,1)} %shard_map.317.refs_0_.refs_6_.refs_1_), channel_id=1, source_target_pairs={{0,8},{4,12},{8,0},{12,4},{16,24},{20,28},{24,16},{28,20},{1,9},{5... | collective-permute-start | bytes 786440 | tf_op jit(solution)/shard_map/ppermute | solution.py:58
  12.1 13.7 %conditional.5 = (bf16[128,1024]{1,0:T(8,128)(2,1)}, bf16[128,1024]{1,0:T(8,128)(2,1)}, f32[8,1024]{1,0:T(8,128)S(1)}, bf16[256,1024]{1,0:T(8,128)(2,1)}, bf16[256,1024]{1,0:T(8,128)(2,1)}) conditional(s32[]{:T(128)} %bitcast.3, () %tuple.45, (s32[2]{0:T(128)S(1)}, bf16[128,1024]{1,0:T(8,128)(2,1)}, bf16[128,1024]{1,0:T(8,128)(2,1)}, ...), branch_computations={%region_0.0_spmd, %region_1.0_spmd} | conditional | flops 22000000 | bytes 3215848 | solution.py:151
  15.5 6.0 %collective-permute-done.refs_1_ = bf16[128,1024]{1,0:T(8,128)(2,1)} collective-permute-done((bf16[128,1024]{1,0:T(8,128)(2,1)}, bf16[128,1024]{1,0:T(8,128)(2,1)}, u32[]{:S(2)}, u32[]{:S(2)}) %collective-permute-start) | collective-permute-done | bytes 262176 | tf_op jit(solution)/shard_map/cond/branch_1_fun/ppermute | solution.py:58
  25.8 5.6 %collective-permute-done.11.refs_1_.refs_7_.refs_2_ = bf16[128,1024]{1,0:T(8,128)(2,1)} collective-permute-done((bf16[128,1024]{1,0:T(8,128)(2,1)}, bf16[128,1024]{1,0:T(8,128)(2,1)}, u32[]{:S(2)}, u32[]{:S(2)}) %collective-permute-start.11) | collective-permute-done | bytes 262176 | tf_op jit(solution)/shard_map/ppermute | solution.py:58
  35.1 2.6 %collective-permute-start.17 = (bf16[128,1024]{1,0:T(8,128)(2,1)}, bf16[128,1024]{1,0:T(8,128)(2,1)}, u32[]{:S(2)}, u32[]{:S(2)}) collective-permute-start(bf16[128,1024]{1,0:T(8,128)(2,1)} %get-tuple-element.222.refs_12_.refs_13_), channel_id=1, source_target_pairs={{0,24},{4,28},{8,16},{12,20},{16,8},{20,12},{24,0},{28,4},{1,25},{... | collective-permute-start | bytes 786440 | tf_op jit(solution)/shard_map/ppermute | solution.py:58
  40.8 11.5 %collective-permute-done.14.refs_9_.refs_4_ = bf16[384,1024]{1,0:T(8,128)(2,1)} collective-permute-done((bf16[384,1024]{1,0:T(8,128)(2,1)}, bf16[384,1024]{1,0:T(8,128)(2,1)}, u32[]{:S(2)}, u32[]{:S(2)}) %collective-permute-start.14) | collective-permute-done | bytes 786464 | tf_op jit(solution)/shard_map/ppermute | solution.py:58
  52.3 6.9 %shard_map.320 = (bf16[512,768]{1,0:T(8,128)(2,1)}, bf16[4,512,512]{2,1,0:T(8,128)(2,1)}, bf16[512,256]{1,0:T(8,128)(2,1)}) custom-call(s32[2]{0:T(128)S(1)} %pad_add_fusion.refs_0_, s32[1,4]{1,0:T(1,128)} %refs_1_.7, s32[4,128]{1,0:T(4,128)} %bitcast.21, f32[1,768]{1,0:T(1,128)} %broadcast_in_dim.10.refs_3_, bf16[256,1024]{1,0:T(8,128)(2,1)} %get-tuple-element.218.refs_4_, ...), custom_call_target="tpu_custom_call" | custom-call | flops 11000000 | bytes 35000 | tf_op jit(solution)/shard_map/pallas_call | solution.py:118
  60.4 3.3 %shard_map.321 = (f32[256,1024]{1,0:T(8,128)}, bf16[256,1024]{1,0:T(8,128)(2,1)}, bf16[128,1024]{1,0:T(8,128)(2,1)}, bf16[384,1024]{1,0:T(8,128)(2,1)}) custom-call(bf16[512,256]{1,0:T(8,128)(2,1)} %get-tuple-element.223.refs_0_, bf16[128,1024]{1,0:T(8,128)(2,1)} %shard_map.317.refs_0_.refs_6_.refs_1_, ...), custom_call_target="tpu_custom_call" | custom-call | flops 11000000 | bytes 35000 | tf_op jit(solution)/shard_map/pallas_call | solution.py:118
  66.5 15.9 %conditional.6 = ((f32[128,1024]{1,0:T(8,128)}, f32[128,1024]{1,0:T(8,128)}, f32[128,1]{1,0:T(8,128)S(1)}, bf16[128,1024]{1,0:T(8,128)(2,1)})) conditional(s32[]{:T(128)} %bitcast.3, () %tuple.48, (bf16[256,1024]{1,0:T(8,128)(2,1)}, f32[256,1024]{1,0:T(8,128)}, f32[8,1024]{1,0:T(8,128)S(1)}, bf16[128,1024]{1,0:T(8,128)(2,1)}) %tuple.49), branch_computations={%region_2.0_spmd, %region_3.0_spmd} | conditional | flops 11393216 | bytes 7375176 | solution.py:151
  72.2 6.9 %collective-permute-done.8.refs_3_ = bf16[128,1024]{1,0:T(8,128)(2,1)S(1)} collective-permute-done((bf16[128,1024]{1,0:T(8,128)(2,1)S(1)}, bf16[128,1024]{1,0:T(8,128)(2,1)S(1)}, u32[]{:S(2)}, u32[]{:S(2)}) %collective-permute-start.8) | collective-permute-done | bytes 262176 | tf_op jit(solution)/shard_map/cond/branch_1_fun/ppermute | solution.py:58
  79.7 2.7 %branch_1_fun.9 = (f32[128,1024]{1,0:T(8,128)}, f32[128,1024]{1,0:T(8,128)}, f32[128,1]{1,0:T(8,128)S(1)}, bf16[128,1024]{1,0:T(8,128)(2,1)}) custom-call(f32[8,1024]{1,0:T(8,128)S(1)} %get-tuple-element.80.refs_0_, f32[256,1024]{1,0:T(8,128)} %get-tuple-element.81.refs_1_, bf16[256,1024]{1,0:T(8,128)(2,1)} %copy-done.4, bf16[128,1024]{1,0:T(8,128)(2,1)} %copy-done.7, ...), custom_call_target="tpu_custom_call" | custom-call | flops 11000000 | bytes 35000 | tf_op jit(solution)/shard_map/cond/branch_1_fun/pallas_call | solution.py:118
  82.4 3.8 %collective-permute-done.21.refs_0_ = bf16[128,1024]{1,0:T(8,128)(2,1)} collective-permute-done((bf16[128,1024]{1,0:T(8,128)(2,1)}, bf16[128,1024]{1,0:T(8,128)(2,1)}, u32[]{:S(2)}, u32[]{:S(2)}) %collective-permute-start.21) | collective-permute-done | bytes 262176 | tf_op jit(solution)/shard_map/ppermute | solution.py:58
  88.3 14.2 %conditional.7 = (bf16[128,1024]{1,0:T(8,128)(2,1)}, bf16[128,1024]{1,0:T(8,128)(2,1)}, bf16[128,1024]{1,0:T(8,128)(2,1)}, bf16[512,1024]{1,0:T(8,128)(2,1)}, f32[512,1024]{1,0:T(8,128)}) conditional(s32[]{:T(128)} %bitcast.3, () %tuple.47, (bf16[128,1024]{1,0:T(8,128)(2,1)}, f32[1024]{0:T(1024)S(1)}, bf16[128,1024]{1,0:T(8,128)(2,1)}, ...), branch_computations={%region_4.0_spmd, %region_5.0_spmd} | conditional | flops 11000000 | bytes 3932212 | solution.py:151
  89.8 5.2 %collective-permute-done.2.refs_2_ = bf16[128,1024]{1,0:T(8,128)(2,1)} collective-permute-done((bf16[128,1024]{1,0:T(8,128)(2,1)}, bf16[128,1024]{1,0:T(8,128)(2,1)}, u32[]{:S(2)}, u32[]{:S(2)}) %collective-permute-start.2) | collective-permute-done | bytes 262176 | tf_op jit(solution)/shard_map/cond/branch_1_fun/ppermute | solution.py:58
  96.9 5.4 %branch_1_fun.10 = (bf16[512,1024]{1,0:T(8,128)(2,1)}, f32[512,1024]{1,0:T(8,128)}) custom-call(f32[1,1024]{1,0:T(1,128)S(1)} %bitcast.20, bf16[128,1024]{1,0:T(8,128)(2,1)} %get-tuple-element.84.refs_1_, bf16[128,1024]{1,0:T(8,128)(2,1)} %collective-permute-done.2.refs_2_, bf16[128,1024]{1,0:T(8,128)(2,1)} %collective-permute-done.3.refs_3_, ...), custom_call_target="tpu_custom_call" | custom-call | flops 11000000 | bytes 35000 | tf_op jit(solution)/shard_map/cond/branch_1_fun/pallas_call | solution.py:118
  102.5 4.2 %shard_map.323 = (f32[256,1024]{1,0:T(8,128)}, bf16[256,1024]{1,0:T(8,128)(2,1)}) custom-call(bf16[512,1024]{1,0:T(8,128)(2,1)} %get-tuple-element.228.refs_0_.refs_4_, bf16[128,1024]{1,0:T(8,128)(2,1)} %get-tuple-element.230.refs_1_.refs_4_, bf16[128,1024]{1,0:T(8,128)(2,1)} %get-tuple-element.231.refs_2_.refs_5_, ...), custom_call_target="tpu_custom_call" | custom-call | flops 11000000 | bytes 35000 | tf_op jit(solution)/shard_map/pallas_call | solution.py:118
  112.4 7.0 %collective-permute-done.27.refs_5_ = bf16[128,1024]{1,0:T(8,128)(2,1)} collective-permute-done((bf16[128,1024]{1,0:T(8,128)(2,1)S(1)}, bf16[128,1024]{1,0:T(8,128)(2,1)}, u32[]{:S(2)}, u32[]{:S(2)}) %collective-permute-start.27) | collective-permute-done | bytes 262176 | tf_op jit(solution)/shard_map/ppermute | solution.py:58
  119.3 3.7 %shard_map.324 = (bf16[128,1024]{1,0:T(8,128)(2,1)}, f32[128,1024]{1,0:T(8,128)}, bf16[128,1024]{1,0:T(8,128)(2,1)}, f32[8,1024]{1,0:T(8,128)}) custom-call(s32[2]{0:T(128)S(1)} %pad_add_fusion.refs_0_, s32[1,4]{1,0:T(1,128)} %refs_1_.7, f32[8,1024]{1,0:T(8,128)S(1)} %get-tuple-element.217.refs_2_, f32[256,1024]{1,0:T(8,128)} %get-tuple-element.233.refs_3_, ...), custom_call_target="tpu_custom_call" | custom-call | flops 11000000 | bytes 35000 | tf_op jit(solution)/shard_map/pallas_call | solution.py:118
  124.6 6.2 %collective-permute-done.28.refs_1_ = bf16[128,1024]{1,0:T(8,128)(2,1)S(1)} collective-permute-done((bf16[128,1024]{1,0:T(8,128)(2,1)}, bf16[128,1024]{1,0:T(8,128)(2,1)S(1)}, u32[]{:S(2)}, u32[]{:S(2)}) %collective-permute-start.28) | collective-permute-done | bytes 262176 | tf_op jit(solution)/shard_map/ppermute | solution.py:58
  133.2 3.8 %shard_map.325 = (f32[128,1024]{1,0:T(8,128)}, bf16[256,1024]{1,0:T(8,128)(2,1)}, bf16[256,1024]{1,0:T(8,128)(2,1)}, bf16[256,1024]{1,0:T(8,128)(2,1)}, bf16[128,1024]{1,0:T(8,128)(2,1)}) custom-call(bf16[128,1024]{1,0:T(8,128)(2,1)} %get-tuple-element.240.refs_0_, bf16[128,1024]{1,0:T(8,128)(2,1)} %copy-done.6, ...), custom_call_target="tpu_custom_call" | custom-call | flops 11000000 | bytes 35000 | tf_op jit(solution)/shard_map/pallas_call | solution.py:118
  140.4 6.4 %shard_map.326 = (bf16[512,1024]{1,0:T(8,128)(2,1)}, f32[256,1024]{1,0:T(8,128)}, bf16[128,1024]{1,0:T(8,128)(2,1)}, bf16[128,1024]{1,0:T(8,128)(2,1)}, f32[1,1024]{1,0:T(1,128)S(1)}) custom-call(bf16[128,1024]{1,0:T(8,128)(2,1)} %get-tuple-element.240.refs_0_, bf16[128,1024]{1,0:T(8,128)(2,1)} %copy-done.6, ...), custom_call_target="tpu_custom_call" | custom-call | flops 11000000 | bytes 35000 | tf_op jit(solution)/shard_map/pallas_call | solution.py:118
  152.1 3.9 %shard_map.329 = (f32[128,1024]{1,0:T(8,128)}, bf16[256,1024]{1,0:T(8,128)(2,1)}, bf16[256,1024]{1,0:T(8,128)(2,1)}, bf16[256,1024]{1,0:T(8,128)(2,1)}, bf16[128,1024]{1,0:T(8,128)(2,1)}) custom-call(bf16[128,1024]{1,0:T(8,128)(2,1)} %get-tuple-element.226.refs_3_.refs_0_, bf16[128,1024]{1,0:T(8,128)(2,1)} %get-tuple-element.256.refs_1_, ...), custom_call_target="tpu_custom_call" | custom-call | flops 11000000 | bytes 35000 | tf_op jit(solution)/shard_map/pallas_call | solution.py:118
  162.7 3.7 %shard_map.328 = (f32[128,1024]{1,0:T(8,128)}, bf16[144,1024]{1,0:T(8,128)(2,1)}) custom-call(s32[2]{0:T(128)S(1)} %pad_add_fusion.refs_0_, f32[128,1]{1,0:T(8,128)S(1)} %get-tuple-element.238.refs_1_, f32[8,1024]{1,0:T(8,128)S(1)} %get-tuple-element.217.refs_2_, f32[8,1024]{1,0:T(8,128)} %get-tuple-element.239.refs_3_, ...), custom_call_target="tpu_custom_call" | custom-call | flops 8800000000 | bytes 28000000 | tf_op jit(solution)/shard_map/pallas_call | solution.py:118
  166.4 22.8 %conditional.8 = (f32[256,1024]{1,0:T(8,128)}, bf16[256,1024]{1,0:T(8,128)(2,1)}, f32[128,1024]{1,0:T(8,128)}, bf16[256,1024]{1,0:T(8,128)(2,1)}, bf16[272,1024]...) conditional(s32[]{:T(128)} %bitcast.3, () %tuple.52, ...), branch_computations={%region_6.0_spmd, %region_7.0_spmd} | conditional | flops 22000000 | bytes 4030548 | solution.py:151
  167.2 7.4 %collective-permute-done.5.refs_1_ = bf16[144,1024]{1,0:T(8,128)(2,1)} collective-permute-done((bf16[144,1024]{1,0:T(8,128)(2,1)}, bf16[144,1024]{1,0:T(8,128)(2,1)}, u32[]{:S(2)}, u32[]{:S(2)}) %collective-permute-start.5) | collective-permute-done | bytes 294944 | tf_op jit(solution)/shard_map/cond/branch_1_fun/ppermute | solution.py:58
  179.0 10.1 %branch_1_fun.12 = (bf16[512,768]{1,0:T(8,128)(2,1)}, f32[256,1024]{1,0:T(8,128)}, bf16[256,1024]{1,0:T(8,128)(2,1)}, f32[128,1024]{1,0:T(8,128)}, bf16[256,1024...) custom-call(f32[1,1024]{1,0:T(1,128)S(1)} %get-tuple-element.94.refs, ...), custom_call_target="tpu_custom_call" | custom-call | flops 11000000 | bytes 35000 | tf_op jit(solution)/shard_map/cond/branch_1_fun/pallas_call | solution.py:118
  196.3 15.4 %conditional.9 = (f32[128,1024]{1,0:T(8,128)}) conditional(s32[]{:T(128)} %bitcast.3, () %tuple.51, (bf16[256,1024]{1,0:T(8,128)(2,1)}, f32[256,1024]{1,0:T(8,128)}, s32[2]{0:T(128)S(1)}, f32[128,1024]{1,0:T(8,128)}, f32[128,1024]{1,0:T(8,128)}) %tuple.54), branch_computations={%region_8.0_spmd, %region_9.0_spmd} | conditional | flops 11393216 | bytes 6326572 | solution.py:151
  200.9 7.9 %collective-permute-done.10.refs_3_ = bf16[128,1024]{1,0:T(8,128)(2,1)} collective-permute-done((bf16[128,1024]{1,0:T(8,128)(2,1)S(1)}, bf16[128,1024]{1,0:T(8,128)(2,1)}, u32[]{:S(2)}, u32[]{:S(2)}) %collective-permute-start.10) | collective-permute-done | bytes 262176 | tf_op jit(solution)/shard_map/cond/branch_1_fun/ppermute | solution.py:58
  208.9 2.9 %branch_1_fun.13 = f32[128,1024]{1,0:T(8,128)} custom-call(s32[2]{0:T(128)S(1)} %get-tuple-element.116.refs_0_, f32[256,1024]{1,0:T(8,128)} %get-tuple-element.117.refs_1_, bf16[256,1024]{1,0:T(8,128)(2,1)} %copy-done.5, bf16[128,1024]{1,0:T(8,128)(2,1)} %collective-permute-done.10.refs_3_, f32[128,1024]{1,0:T(8,128)} %get-tuple-element.119.refs_4_, ...), custom_call_target="tpu_custom_call" | custom-call | flops 11000000 | bytes 35000 | tf_op jit(solution)/shard_map/cond/branch_1_fun/pallas_call | solution.py:118
  211.8 7.5 %collective-permute-done.43.refs_10_.refs_3_ = bf16[128,1024]{1,0:T(8,128)(2,1)} collective-permute-done((bf16[128,1024]{1,0:T(8,128)(2,1)}, bf16[128,1024]{1,0:T(8,128)(2,1)}, u32[]{:S(2)}, u32[]{:S(2)}) %collective-permute-start.43) | collective-permute-done | bytes 262176 | tf_op jit(solution)/shard_map/ppermute | solution.py:58
  220.1 2.8 %shard_map.332 = (bf16[144,1024]{1,0:T(8,128)(2,1)}, bf16[144,1024]{1,0:T(8,128)(2,1)}, bf16[400,1024]{1,0:T(8,128)(2,1)}) custom-call(bf16[256,1024]{1,0:T(8,128)(2,1)} %get-tuple-element.267.refs_0_, bf16[272,1024]{1,0:T(8,128)(2,1)} %collective-permute-done.37.refs_1_, bf16[128,1024]{1,0:T(8,128)(2,1)} %get-tuple-element.269.refs_2_, ...), custom_call_target="tpu_custom_call" | custom-call | flops 11000000 | bytes 35000 | tf_op jit(solution)/shard_map/pallas_call | solution.py:118
  225.7 16.3 %collective-permute-done.46.refs_4_.refs_9_ = bf16[400,1024]{1,0:T(8,128)(2,1)} collective-permute-done((bf16[400,1024]{1,0:T(8,128)(2,1)}, bf16[400,1024]{1,0:T(8,128)(2,1)}, u32[]{:S(2)}, u32[]{:S(2)}) %collective-permute-start.46) | collective-permute-done | bytes 819232 | tf_op jit(solution)/shard_map/ppermute | solution.py:58
  (138 shorter events, 93.6 us)
Async XLA Ops:
  2.5 23.3 %collective-permute-start.13 = (bf16[128,1024]{1,0:T(8,128)(2,1)}, bf16[128,1024]{1,0:T(8,128)(2,1)}, u32[]{:S(2)}, u32[]{:S(2)}) collective-permute-start(bf16[128,1024]{1,0:T(8,128)(2,1)} %shard_map.317.refs_0_.refs_6_.refs_1_), channel_id=1, source_target_pairs={{0,8},{4,12},{8,0},{12,4},{16,24},{20,28},{24,16},{28,20},{1,9},{5... | collective-permute-start | bytes 786440 | tf_op jit(solution)/shard_map/ppermute | solution.py:58
  5.5 20.2 %collective-permute-start.12 = (bf16[128,1024]{1,0:T(8,128)(2,1)}, bf16[128,1024]{1,0:T(8,128)(2,1)}, u32[]{:S(2)}, u32[]{:S(2)}) collective-permute-start(bf16[128,1024]{1,0:T(8,128)(2,1)} %shard_map.317.refs_0_.refs_6_.refs_1_), channel_id=1, source_target_pairs={{0,24},{4,28},{8,16},{12,20},{16,8},{20,12},{24,0},{28,4},{1,25},{... | collective-permute-start | bytes 786440 | tf_op jit(solution)/shard_map/ppermute | solution.py:58
  8.0 23.3 %collective-permute-start.11 = (bf16[128,1024]{1,0:T(8,128)(2,1)}, bf16[128,1024]{1,0:T(8,128)(2,1)}, u32[]{:S(2)}, u32[]{:S(2)}) collective-permute-start(bf16[128,1024]{1,0:T(8,128)(2,1)} %shard_map.317.refs_0_.refs_6_.refs_1_), channel_id=1, source_target_pairs={{0,16},{4,20},{8,24},{12,28},{16,0},{20,4},{24,8},{28,12},{1,17},{... | collective-permute-start | bytes 786440 | tf_op jit(solution)/shard_map/ppermute | solution.py:58
  10.3 28.3 %collective-permute-start.15 = (bf16[384,1024]{1,0:T(8,128)(2,1)}, bf16[384,1024]{1,0:T(8,128)(2,1)S(1)}, u32[]{:S(2)}, u32[]{:S(2)}) collective-permute-start(bf16[384,1024]{1,0:T(8,128)(2,1)} %shard_map.318.refs_0_.refs_7_), channel_id=1, source_target_pairs={{0,4},{4,0},{8,12},{12,8},{16,20},{20,16},{24,28},{28,24},{1,5},{5... | collective-permute-start | bytes 2359304 | tf_op jit(solution)/shard_map/ppermute | solution.py:58
  33.5 18.8 %collective-permute-start.14 = (bf16[384,1024]{1,0:T(8,128)(2,1)}, bf16[384,1024]{1,0:T(8,128)(2,1)}, u32[]{:S(2)}, u32[]{:S(2)}) collective-permute-start(bf16[384,1024]{1,0:T(8,128)(2,1)} %get-tuple-element.221), channel_id=1, source_target_pairs={{0,4},{4,0},{8,12},{12,8},{16,20},{20,16},{24,28},{28,24},{1,5},{5... | collective-permute-start | bytes 2359304 | tf_op jit(solution)/shard_map/ppermute | solution.py:58
  35.1 24.1 %collective-permute-start.18 = (bf16[128,1024]{1,0:T(8,128)(2,1)}, bf16[128,1024]{1,0:T(8,128)(2,1)}, u32[]{:S(2)}, u32[]{:S(2)}) collective-permute-start(bf16[128,1024]{1,0:T(8,128)(2,1)} %get-tuple-element.222.refs_12_.refs_13_), channel_id=1, source_target_pairs={{0,8},{4,12},{8,0},{12,4},{16,24},{20,28},{24,16},{28,20},{1,9},{5... | collective-permute-start | bytes 786440 | tf_op jit(solution)/shard_map/ppermute | solution.py:58
  35.1 24.1 %collective-permute-start.17 = (bf16[128,1024]{1,0:T(8,128)(2,1)}, bf16[128,1024]{1,0:T(8,128)(2,1)}, u32[]{:S(2)}, u32[]{:S(2)}) collective-permute-start(bf16[128,1024]{1,0:T(8,128)(2,1)} %get-tuple-element.222.refs_12_.refs_13_), channel_id=1, source_target_pairs={{0,24},{4,28},{8,16},{12,20},{16,8},{20,12},{24,0},{28,4},{1,25},{... | collective-permute-start | bytes 786440 | tf_op jit(solution)/shard_map/ppermute | solution.py:58
  37.7 22.6 %collective-permute-start.16 = (bf16[128,1024]{1,0:T(8,128)(2,1)}, bf16[128,1024]{1,0:T(8,128)(2,1)}, u32[]{:S(2)}, u32[]{:S(2)}) collective-permute-start(bf16[128,1024]{1,0:T(8,128)(2,1)} %get-tuple-element.222.refs_12_.refs_13_), channel_id=1, source_target_pairs={{0,16},{4,20},{8,24},{12,28},{16,0},{20,4},{24,8},{28,12},{1,17},{... | collective-permute-start | bytes 786440 | tf_op jit(solution)/shard_map/ppermute | solution.py:58
  39.3 21.0 %collective-permute-start.19 = (bf16[128,1024]{1,0:T(8,128)(2,1)}, bf16[128,1024]{1,0:T(8,128)(2,1)}, u32[]{:S(2)}, u32[]{:S(2)}) collective-permute-start(bf16[128,1024]{1,0:T(8,128)(2,1)} %slice.30), channel_id=1, source_target_pairs={{0,8},{4,12},{8,0},{12,4},{16,24},{20,28},{24,16},{28,20},{1,9},{5... | collective-permute-start | bytes 786440 | tf_op jit(solution)/shard_map/ppermute | solution.py:58
  63.7 24.6 %collective-permute-start.20 = (bf16[384,1024]{1,0:T(8,128)(2,1)}, bf16[384,1024]{1,0:T(8,128)(2,1)}, u32[]{:S(2)}, u32[]{:S(2)}) collective-permute-start(bf16[384,1024]{1,0:T(8,128)(2,1)} %get-tuple-element.227), channel_id=1, source_target_pairs={{0,4},{4,0},{8,12},{12,8},{16,20},{20,16},{24,28},{28,24},{1,5},{5... | collective-permute-start | bytes 2359304 | tf_op jit(solution)/shard_map/ppermute | solution.py:58
  64.2 18.2 %collective-permute-start.22 = (bf16[128,1024]{1,0:T(8,128)(2,1)}, bf16[128,1024]{1,0:T(8,128)(2,1)}, u32[]{:S(2)}, u32[]{:S(2)}) collective-permute-start(bf16[128,1024]{1,0:T(8,128)(2,1)} %get-tuple-element.229.refs_2_), channel_id=1, source_target_pairs={{0,24},{4,28},{8,16},{12,20},{16,8},{20,12},{24,0},{28,4},{1,25},{... | collective-permute-start | bytes 786440 | tf_op jit(solution)/shard_map/ppermute | solution.py:58
  66.5 19.7 %collective-permute-start.21 = (bf16[128,1024]{1,0:T(8,128)(2,1)}, bf16[128,1024]{1,0:T(8,128)(2,1)}, u32[]{:S(2)}, u32[]{:S(2)}) collective-permute-start(bf16[128,1024]{1,0:T(8,128)(2,1)} %get-tuple-element.229.refs_2_), channel_id=1, source_target_pairs={{0,16},{4,20},{8,24},{12,28},{16,0},{20,4},{24,8},{28,12},{1,17},{... | collective-permute-start | bytes 786440 | tf_op jit(solution)/shard_map/ppermute | solution.py:58
  70.6 8.4 %collective-permute-start.8 = (bf16[128,1024]{1,0:T(8,128)(2,1)S(1)}, bf16[128,1024]{1,0:T(8,128)(2,1)S(1)}, u32[]{:S(2)}, u32[]{:S(2)}) collective-permute-start(bf16[128,1024]{1,0:T(8,128)(2,1)S(1)} %add_convert_fusion), channel_id=1, source_target_pairs={{0,2},{1,3},{2,0},{3,1},{4,6},{5,7},{6,4},{7,5},{8,10},{9,11},{10,... | collective-permute-start | bytes 786440 | tf_op jit(solution)/shard_map/cond/branch_1_fun/ppermute | solution.py:58
  86.3 16.2 %collective-permute-start.25 = (bf16[128,1024]{1,0:T(8,128)(2,1)}, bf16[128,1024]{1,0:T(8,128)(2,1)}, u32[]{:S(2)}, u32[]{:S(2)}) collective-permute-start(bf16[128,1024]{1,0:T(8,128)(2,1)} %get-tuple-element.230.refs_1_.refs_4_), channel_id=1, source_target_pairs={{0,8},{4,12},{8,0},{12,4},{16,24},{20,28},{24,16},{28,20},{1,9},{5... | collective-permute-start | bytes 786440 | tf_op jit(solution)/shard_map/ppermute | solution.py:58
  86.3 16.2 %collective-permute-start.23 = (bf16[128,1024]{1,0:T(8,128)(2,1)}, bf16[128,1024]{1,0:T(8,128)(2,1)}, u32[]{:S(2)}, u32[]{:S(2)}) collective-permute-start(bf16[128,1024]{1,0:T(8,128)(2,1)} %get-tuple-element.231.refs_2_.refs_5_), channel_id=1, source_target_pairs={{0,4},{4,0},{8,12},{12,8},{16,20},{20,16},{24,28},{28,24},{1,5},{5... | collective-permute-start | bytes 786440 | tf_op jit(solution)/shard_map/ppermute | solution.py:58
  87.5 15.0 %collective-permute-start.24 = (bf16[128,1024]{1,0:T(8,128)(2,1)}, bf16[128,1024]{1,0:T(8,128)(2,1)}, u32[]{:S(2)}, u32[]{:S(2)}) collective-permute-start(bf16[128,1024]{1,0:T(8,128)(2,1)} %get-tuple-element.232.refs_3_.refs_6_), channel_id=1, source_target_pairs={{0,4},{4,0},{8,12},{12,8},{16,20},{20,16},{24,28},{28,24},{1,5},{5... | collective-permute-start | bytes 786440 | tf_op jit(solution)/shard_map/ppermute | solution.py:58
  110.8 8.5 %collective-permute-start.27 = (bf16[128,1024]{1,0:T(8,128)(2,1)S(1)}, bf16[128,1024]{1,0:T(8,128)(2,1)}, u32[]{:S(2)}, u32[]{:S(2)}) collective-permute-start(bf16[128,1024]{1,0:T(8,128)(2,1)S(1)} %add_convert_fusion.2), channel_id=1, source_target_pairs={{0,2},{1,3},{2,0},{3,1},{4,6},{5,7},{6,4},{7,5},{8,10},{9,11},{10,... | collective-permute-start | bytes 786440 | tf_op jit(solution)/shard_map/ppermute | solution.py:58
  137.1 19.8 %collective-permute-start.34 = (bf16[256,1024]{1,0:T(8,128)(2,1)}, bf16[256,1024]{1,0:T(8,128)(2,1)}, u32[]{:S(2)}, u32[]{:S(2)}) collective-permute-start(bf16[256,1024]{1,0:T(8,128)(2,1)} %get-tuple-element.253), channel_id=1, source_target_pairs={{0,4},{4,0},{8,12},{12,8},{16,20},{20,16},{24,28},{28,24},{1,5},{5... | collective-permute-start | bytes 1572872 | tf_op jit(solution)/shard_map/ppermute | solution.py:58
  138.3 18.5 %collective-permute-start.35 = (bf16[256,1024]{1,0:T(8,128)(2,1)}, bf16[256,1024]{1,0:T(8,128)(2,1)}, u32[]{:S(2)}, u32[]{:S(2)}) collective-permute-start(bf16[256,1024]{1,0:T(8,128)(2,1)} %get-tuple-element.255), channel_id=1, source_target_pairs={{0,8},{4,12},{8,0},{12,4},{16,24},{20,28},{24,16},{28,20},{1,9},{5... | collective-permute-start | bytes 1572872 | tf_op jit(solution)/shard_map/ppermute | solution.py:58
  150.6 12.2 %collective-permute-start.33 = (bf16[128,1024]{1,0:T(8,128)(2,1)}, bf16[128,1024]{1,0:T(8,128)(2,1)}, u32[]{:S(2)}, u32[]{:S(2)}) collective-permute-start(bf16[128,1024]{1,0:T(8,128)(2,1)} %shard_map.327), channel_id=1, source_target_pairs={{0,2},{1,3},{2,0},{3,1},{4,6},{5,7},{6,4},{7,5},{8,10},{9,11},{10,... | collective-permute-start | bytes 786440 | tf_op jit(solution)/shard_map/ppermute | solution.py:58
  156.0 34.4 %collective-permute-start.38 = (bf16[256,1024]{1,0:T(8,128)(2,1)}, bf16[256,1024]{1,0:T(8,128)(2,1)}, u32[]{:S(2)}, u32[]{:S(2)}) collective-permute-start(bf16[256,1024]{1,0:T(8,128)(2,1)} %get-tuple-element.272), channel_id=1, source_target_pairs={{0,4},{4,0},{8,12},{12,8},{16,20},{20,16},{24,28},{28,24},{1,5},{5... | collective-permute-start | bytes 1572872 | tf_op jit(solution)/shard_map/ppermute | solution.py:58
  156.9 34.8 %collective-permute-start.39 = (bf16[256,1024]{1,0:T(8,128)(2,1)}, bf16[256,1024]{1,0:T(8,128)(2,1)}, u32[]{:S(2)}, u32[]{:S(2)}) collective-permute-start(bf16[256,1024]{1,0:T(8,128)(2,1)} %get-tuple-element.274), channel_id=1, source_target_pairs={{0,8},{4,12},{8,0},{12,4},{16,24},{20,28},{24,16},{28,20},{1,9},{5... | collective-permute-start | bytes 1572872 | tf_op jit(solution)/shard_map/ppermute | solution.py:58
  159.2 32.5 %collective-permute-start.40 = (bf16[128,1024]{1,0:T(8,128)(2,1)}, bf16[128,1024]{1,0:T(8,128)(2,1)}, u32[]{:S(2)}, u32[]{:S(2)}) collective-permute-start(bf16[128,1024]{1,0:T(8,128)(2,1)} %get-tuple-element.275), channel_id=1, source_target_pairs={{0,24},{4,28},{8,16},{12,20},{16,8},{20,12},{24,0},{28,4},{1,25},{... | collective-permute-start | bytes 786440 | tf_op jit(solution)/shard_map/ppermute | solution.py:58
  161.2 30.4 %collective-permute-start.41 = (bf16[128,1024]{1,0:T(8,128)(2,1)}, bf16[128,1024]{1,0:T(8,128)(2,1)}, u32[]{:S(2)}, u32[]{:S(2)}) collective-permute-start(bf16[128,1024]{1,0:T(8,128)(2,1)} %get-tuple-element.276), channel_id=1, source_target_pairs={{0,16},{4,20},{8,24},{12,28},{16,0},{20,4},{24,8},{28,12},{1,17},{... | collective-permute-start | bytes 786440 | tf_op jit(solution)/shard_map/ppermute | solution.py:58
  189.2 30.1 %collective-permute-start.36 = (bf16[272,1024]{1,0:T(8,128)(2,1)}, bf16[272,1024]{1,0:T(8,128)(2,1)S(1)}, u32[]{:S(2)}, u32[]{:S(2)}) collective-permute-start(bf16[272,1024]{1,0:T(8,128)(2,1)} %get-tuple-element.266), channel_id=1, source_target_pairs={{0,8},{4,12},{8,0},{12,4},{16,24},{20,28},{24,16},{28,20},{1,9},{5... | collective-permute-start | bytes 1671176 | tf_op jit(solution)/shard_map/ppermute | solution.py:58
  190.4 28.9 %collective-permute-start.37 = (bf16[272,1024]{1,0:T(8,128)(2,1)}, bf16[272,1024]{1,0:T(8,128)(2,1)}, u32[]{:S(2)}, u32[]{:S(2)}) collective-permute-start(bf16[272,1024]{1,0:T(8,128)(2,1)} %get-tuple-element.268), channel_id=1, source_target_pairs={{0,4},{4,0},{8,12},{12,8},{16,20},{20,16},{24,28},{28,24},{1,5},{5... | collective-permute-start | bytes 1671176 | tf_op jit(solution)/shard_map/ppermute | solution.py:58
  193.9 17.8 %collective-permute-start.42 = (bf16[128,1024]{1,0:T(8,128)(2,1)}, bf16[128,1024]{1,0:T(8,128)(2,1)}, u32[]{:S(2)}, u32[]{:S(2)}) collective-permute-start(bf16[128,1024]{1,0:T(8,128)(2,1)} %get-tuple-element.278), channel_id=1, source_target_pairs={{0,24},{4,28},{8,16},{12,20},{16,8},{20,12},{24,0},{28,4},{1,25},{... | collective-permute-start | bytes 786440 | tf_op jit(solution)/shard_map/ppermute | solution.py:58
  196.2 23.1 %collective-permute-start.43 = (bf16[128,1024]{1,0:T(8,128)(2,1)}, bf16[128,1024]{1,0:T(8,128)(2,1)}, u32[]{:S(2)}, u32[]{:S(2)}) collective-permute-start(bf16[128,1024]{1,0:T(8,128)(2,1)} %get-tuple-element.279), channel_id=1, source_target_pairs={{0,16},{4,20},{8,24},{12,28},{16,0},{20,4},{24,8},{28,12},{1,17},{... | collective-permute-start | bytes 786440 | tf_op jit(solution)/shard_map/ppermute | solution.py:58
  200.3 8.5 %collective-permute-start.10 = (bf16[128,1024]{1,0:T(8,128)(2,1)S(1)}, bf16[128,1024]{1,0:T(8,128)(2,1)}, u32[]{:S(2)}, u32[]{:S(2)}) collective-permute-start(bf16[128,1024]{1,0:T(8,128)(2,1)S(1)} %add_convert_fusion.1), channel_id=1, source_target_pairs={{0,2},{1,3},{2,0},{3,1},{4,6},{5,7},{6,4},{7,5},{8,10},{9,11},{10,... | collective-permute-start | bytes 786440 | tf_op jit(solution)/shard_map/cond/branch_1_fun/ppermute | solution.py:58
  222.9 19.2 %collective-permute-start.46 = (bf16[400,1024]{1,0:T(8,128)(2,1)}, bf16[400,1024]{1,0:T(8,128)(2,1)}, u32[]{:S(2)}, u32[]{:S(2)}) collective-permute-start(bf16[400,1024]{1,0:T(8,128)(2,1)} %get-tuple-element.282), channel_id=1, source_target_pairs={{0,4},{4,0},{8,12},{12,8},{16,20},{20,16},{24,28},{28,24},{1,5},{5... | collective-permute-start | bytes 2457608 | tf_op jit(solution)/shard_map/ppermute | solution.py:58
  223.7 22.9 %collective-permute-start.44 = (bf16[144,1024]{1,0:T(8,128)(2,1)}, bf16[144,1024]{1,0:T(8,128)(2,1)S(1)}, u32[]{:S(2)}, u32[]{:S(2)}) collective-permute-start(bf16[144,1024]{1,0:T(8,128)(2,1)} %get-tuple-element.280), channel_id=1, source_target_pairs={{0,24},{4,28},{8,16},{12,20},{16,8},{20,12},{24,0},{28,4},{1,25},{... | collective-permute-start | bytes 884744 | tf_op jit(solution)/shard_map/ppermute | solution.py:58
  225.7 23.1 %collective-permute-start.45 = (bf16[144,1024]{1,0:T(8,128)(2,1)}, bf16[144,1024]{1,0:T(8,128)(2,1)S(1)}, u32[]{:S(2)}, u32[]{:S(2)}) collective-permute-start(bf16[144,1024]{1,0:T(8,128)(2,1)} %get-tuple-element.281.refs_5_), channel_id=1, source_target_pairs={{0,16},{4,20},{8,24},{12,28},{16,0},{20,4},{24,8},{28,12},{1,17},{... | collective-permute-start | bytes 884744 | tf_op jit(solution)/shard_map/ppermute | solution.py:58
  (33 other events, 227.9 us)

commit v6 on v5

--- a/solution.py
+++ b/solution.py
@@ -875,7 +875,9 @@
     )
     norm_rows = [first_low, *other_rows]
     near, far = kernel_call(
-        outer_kernel, partial_sums, pieces=[[active], outer_weights]
+        outer_kernel,
+        [partial_sums[0], [shaped(own)] * 2],
+        pieces=[[active], outer_weights],
     )
     terms = scatter_rows(near, far)
     layer_out, second_grad, branch_grad, second_sums = kernel_call(

time: 253 us -> 253 us (level)
    pallas_call x25 -> x26, Pallas kernels: 85 us -> 86.9 us  [kernel_call(): pl.pallas_call(run, out_shape=flat_out, in_specs=[pl.BlockSpec(memory_spa...]
    ppermute x47 -> x48, waiting for transfers between devices: 110 us -> 110 us  [swap(): lax.ppermute(block, axis_name, [(i, i ^ offset) for i in range(count)])]
    ppermute x47 -> x48, starting transfers between devices: 44.8 us -> 45.1 us  [swap(): lax.ppermute(block, axis_name, [(i, i ^ offset) for i in range(count)])]
  transfers between devices with their start and end apart: 47 -> 48, of which waited for: 22 -> 22; matrix products, arithmetic and copies ran while one was open for 1% -> 1% of each run, Pallas kernels for 25% -> 26%
where the time goes in v6:
time: 253 us; the launch traced here: 252 us
  waiting for transfers between devices  110 us (43%)
  Pallas kernels  86.9 us (34%)
  starting transfers between devices  45.1 us (18%)
  local copies, waits for them, and re-layouts  5.94 us (2%)
    ppermute x48, waiting for transfers between devices, swap(): lax.ppermute(block, axis_name, [(i, i ^ offset) for i in range(count)])  110 us
    pallas_call x26, Pallas kernels, kernel_call(): pl.pallas_call(run, out_shape=flat_out, in_specs=[pl.BlockSpec(memory_spa...  86.9 us
    ppermute x48, starting transfers between devices, swap(): lax.ppermute(block, axis_name, [(i, i ^ offset) for i in range(count)])  45.1 us
  transfers between devices with their start and end apart: 48, of which 22 were waited for; matrix products, arithmetic and copies ran while one was open for 1% of the time, Pallas kernels for 26%

profile of v6, /device:TPU:0, one launch (start us, length us, event | category | flops | bytes accessed | tf_op | source)
XLA Modules:
  0.0 252.0 jit_solution(13260024407925961204)
XLA Ops:
  2.5 3.0 %collective-permute-start.13 = (bf16[128,1024]{1,0:T(8,128)(2,1)}, bf16[128,1024]{1,0:T(8,128)(2,1)}, u32[]{:S(2)}, u32[]{:S(2)}) collective-permute-start(bf16[128,1024]{1,0:T(8,128)(2,1)} %shard_map.317.refs_0_.refs_6_.refs_1_), channel_id=1, source_target_pairs={{0,8},{4,12},{8,0},{12,4},{16,24},{20,28},{24,16},{28,20},{1,9},{5... | collective-permute-start | bytes 786440 | tf_op jit(solution)/shard_map/ppermute | solution.py:58
  12.1 13.7 %conditional.5 = (bf16[128,1024]{1,0:T(8,128)(2,1)}, bf16[128,1024]{1,0:T(8,128)(2,1)}, f32[8,1024]{1,0:T(8,128)S(1)}, bf16[256,1024]{1,0:T(8,128)(2,1)}, bf16[256,1024]{1,0:T(8,128)(2,1)}) conditional(s32[]{:T(128)} %bitcast.3, () %tuple.45, (s32[2]{0:T(128)S(1)}, bf16[128,1024]{1,0:T(8,128)(2,1)}, bf16[128,1024]{1,0:T(8,128)(2,1)}, ...), branch_computations={%region_0.0_spmd, %region_1.0_spmd} | conditional | flops 22000000 | bytes 3215848 | solution.py:151
  15.6 6.0 %collective-permute-done.refs_1_ = bf16[128,1024]{1,0:T(8,128)(2,1)} collective-permute-done((bf16[128,1024]{1,0:T(8,128)(2,1)}, bf16[128,1024]{1,0:T(8,128)(2,1)}, u32[]{:S(2)}, u32[]{:S(2)}) %collective-permute-start) | collective-permute-done | bytes 262176 | tf_op jit(solution)/shard_map/cond/branch_1_fun/ppermute | solution.py:58
  25.8 5.6 %collective-permute-done.11.refs_1_.refs_7_.refs_2_ = bf16[128,1024]{1,0:T(8,128)(2,1)} collective-permute-done((bf16[128,1024]{1,0:T(8,128)(2,1)}, bf16[128,1024]{1,0:T(8,128)(2,1)}, u32[]{:S(2)}, u32[]{:S(2)}) %collective-permute-start.11) | collective-permute-done | bytes 262176 | tf_op jit(solution)/shard_map/ppermute | solution.py:58
  35.1 2.6 %collective-permute-start.17 = (bf16[128,1024]{1,0:T(8,128)(2,1)}, bf16[128,1024]{1,0:T(8,128)(2,1)}, u32[]{:S(2)}, u32[]{:S(2)}) collective-permute-start(bf16[128,1024]{1,0:T(8,128)(2,1)} %get-tuple-element.223.refs_12_.refs_13_), channel_id=1, source_target_pairs={{0,24},{4,28},{8,16},{12,20},{16,8},{20,12},{24,0},{28,4},{1,25},{... | collective-permute-start | bytes 786440 | tf_op jit(solution)/shard_map/ppermute | solution.py:58
  40.8 11.5 %collective-permute-done.14.refs_9_.refs_4_ = bf16[384,1024]{1,0:T(8,128)(2,1)} collective-permute-done((bf16[384,1024]{1,0:T(8,128)(2,1)}, bf16[384,1024]{1,0:T(8,128)(2,1)}, u32[]{:S(2)}, u32[]{:S(2)}) %collective-permute-start.14) | collective-permute-done | bytes 786464 | tf_op jit(solution)/shard_map/ppermute | solution.py:58
  52.3 6.9 %shard_map.320 = (bf16[512,768]{1,0:T(8,128)(2,1)}, bf16[4,512,512]{2,1,0:T(8,128)(2,1)}, bf16[512,256]{1,0:T(8,128)(2,1)}) custom-call(s32[2]{0:T(128)S(1)} %pad_add_fusion.refs_0_, s32[1,4]{1,0:T(1,128)} %refs_1_.7, s32[4,128]{1,0:T(4,128)} %bitcast.21, f32[1,768]{1,0:T(1,128)} %broadcast_in_dim.10.refs_3_, bf16[256,1024]{1,0:T(8,128)(2,1)} %get-tuple-element.219.refs_4_, ...), custom_call_target="tpu_custom_call" | custom-call | flops 11000000 | bytes 35000 | tf_op jit(solution)/shard_map/pallas_call | solution.py:118
  60.4 3.3 %shard_map.321 = (f32[256,1024]{1,0:T(8,128)}, bf16[256,1024]{1,0:T(8,128)(2,1)}, bf16[128,1024]{1,0:T(8,128)(2,1)}, bf16[384,1024]{1,0:T(8,128)(2,1)}) custom-call(bf16[512,256]{1,0:T(8,128)(2,1)} %get-tuple-element.224.refs_0_, bf16[128,1024]{1,0:T(8,128)(2,1)} %shard_map.317.refs_0_.refs_6_.refs_1_, ...), custom_call_target="tpu_custom_call" | custom-call | flops 11000000 | bytes 35000 | tf_op jit(solution)/shard_map/pallas_call | solution.py:118
  66.5 15.9 %conditional.6 = ((f32[128,1024]{1,0:T(8,128)}, f32[128,1024]{1,0:T(8,128)}, f32[128,1]{1,0:T(8,128)S(1)}, bf16[128,1024]{1,0:T(8,128)(2,1)})) conditional(s32[]{:T(128)} %bitcast.3, () %tuple.48, (bf16[256,1024]{1,0:T(8,128)(2,1)}, f32[256,1024]{1,0:T(8,128)}, f32[8,1024]{1,0:T(8,128)S(1)}, bf16[128,1024]{1,0:T(8,128)(2,1)}) %tuple.49), branch_computations={%region_2.0_spmd, %region_3.0_spmd} | conditional | flops 11393216 | bytes 7375176 | solution.py:151
  72.2 6.9 %collective-permute-done.8.refs_3_ = bf16[128,1024]{1,0:T(8,128)(2,1)S(1)} collective-permute-done((bf16[128,1024]{1,0:T(8,128)(2,1)S(1)}, bf16[128,1024]{1,0:T(8,128)(2,1)S(1)}, u32[]{:S(2)}, u32[]{:S(2)}) %collective-permute-start.8) | collective-permute-done | bytes 262176 | tf_op jit(solution)/shard_map/cond/branch_1_fun/ppermute | solution.py:58
  79.7 2.7 %branch_1_fun.9 = (f32[128,1024]{1,0:T(8,128)}, f32[128,1024]{1,0:T(8,128)}, f32[128,1]{1,0:T(8,128)S(1)}, bf16[128,1024]{1,0:T(8,128)(2,1)}) custom-call(f32[8,1024]{1,0:T(8,128)S(1)} %get-tuple-element.80.refs_0_, f32[256,1024]{1,0:T(8,128)} %get-tuple-element.81.refs_1_, bf16[256,1024]{1,0:T(8,128)(2,1)} %copy-done.3, bf16[128,1024]{1,0:T(8,128)(2,1)} %copy-done.6, ...), custom_call_target="tpu_custom_call" | custom-call | flops 11000000 | bytes 35000 | tf_op jit(solution)/shard_map/cond/branch_1_fun/pallas_call | solution.py:118
  82.4 3.8 %collective-permute-done.21.refs_0_ = bf16[128,1024]{1,0:T(8,128)(2,1)} collective-permute-done((bf16[128,1024]{1,0:T(8,128)(2,1)}, bf16[128,1024]{1,0:T(8,128)(2,1)}, u32[]{:S(2)}, u32[]{:S(2)}) %collective-permute-start.21) | collective-permute-done | bytes 262176 | tf_op jit(solution)/shard_map/ppermute | solution.py:58
  88.3 14.2 %conditional.7 = (bf16[128,1024]{1,0:T(8,128)(2,1)}, bf16[128,1024]{1,0:T(8,128)(2,1)}, bf16[128,1024]{1,0:T(8,128)(2,1)}, bf16[512,1024]{1,0:T(8,128)(2,1)}, f32[512,1024]{1,0:T(8,128)}) conditional(s32[]{:T(128)} %bitcast.3, () %tuple.47, (bf16[128,1024]{1,0:T(8,128)(2,1)}, f32[1024]{0:T(1024)S(1)}, bf16[128,1024]{1,0:T(8,128)(2,1)}, ...), branch_computations={%region_4.0_spmd, %region_5.0_spmd} | conditional | flops 11000000 | bytes 3932212 | solution.py:151
  89.8 5.2 %collective-permute-done.2.refs_2_ = bf16[128,1024]{1,0:T(8,128)(2,1)} collective-permute-done((bf16[128,1024]{1,0:T(8,128)(2,1)}, bf16[128,1024]{1,0:T(8,128)(2,1)}, u32[]{:S(2)}, u32[]{:S(2)}) %collective-permute-start.2) | collective-permute-done | bytes 262176 | tf_op jit(solution)/shard_map/cond/branch_1_fun/ppermute | solution.py:58
  96.9 5.4 %branch_1_fun.10 = (bf16[512,1024]{1,0:T(8,128)(2,1)}, f32[512,1024]{1,0:T(8,128)}) custom-call(f32[1,1024]{1,0:T(1,128)S(1)} %bitcast.20, bf16[128,1024]{1,0:T(8,128)(2,1)} %get-tuple-element.84.refs_1_, bf16[128,1024]{1,0:T(8,128)(2,1)} %collective-permute-done.2.refs_2_, bf16[128,1024]{1,0:T(8,128)(2,1)} %collective-permute-done.3.refs_3_, ...), custom_call_target="tpu_custom_call" | custom-call | flops 11000000 | bytes 35000 | tf_op jit(solution)/shard_map/cond/branch_1_fun/pallas_call | solution.py:118
  102.5 4.2 %shard_map.323 = (f32[256,1024]{1,0:T(8,128)}, bf16[128,1024]{1,0:T(8,128)(2,1)}, bf16[128,1024]{1,0:T(8,128)(2,1)}) custom-call(bf16[512,1024]{1,0:T(8,128)(2,1)} %get-tuple-element.229.refs_0_.refs_4_, bf16[128,1024]{1,0:T(8,128)(2,1)} %get-tuple-element.231.refs_1_.refs_4_, bf16[128,1024]{1,0:T(8,128)(2,1)} %get-tuple-element.232.refs_2_.refs_5_, ...), custom_call_target="tpu_custom_call" | custom-call | flops 11000000 | bytes 35000 | tf_op jit(solution)/shard_map/pallas_call | solution.py:118
  112.1 7.2 %collective-permute-done.28.refs_5_ = bf16[128,1024]{1,0:T(8,128)(2,1)} collective-permute-done((bf16[128,1024]{1,0:T(8,128)(2,1)}, bf16[128,1024]{1,0:T(8,128)(2,1)}, u32[]{:S(2)}, u32[]{:S(2)}) %collective-permute-start.28) | collective-permute-done | bytes 262176 | tf_op jit(solution)/shard_map/ppermute | solution.py:58
  119.3 3.7 %shard_map.325 = (bf16[128,1024]{1,0:T(8,128)(2,1)}, f32[128,1024]{1,0:T(8,128)}, bf16[128,1024]{1,0:T(8,128)(2,1)}, f32[8,1024]{1,0:T(8,128)}) custom-call(s32[2]{0:T(128)S(1)} %pad_add_fusion.refs_0_, s32[1,4]{1,0:T(1,128)} %refs_1_.7, f32[8,1024]{1,0:T(8,128)S(1)} %get-tuple-element.218.refs_2_, f32[256,1024]{1,0:T(8,128)} %get-tuple-element.234.refs_0_.refs_3_, ...), custom_call_target="tpu_custom_call" | custom-call | flops 11000000 | bytes 35000 | tf_op jit(solution)/shard_map/pallas_call | solution.py:118
  124.6 6.2 %collective-permute-done.29.refs_1_ = bf16[128,1024]{1,0:T(8,128)(2,1)S(1)} collective-permute-done((bf16[128,1024]{1,0:T(8,128)(2,1)}, bf16[128,1024]{1,0:T(8,128)(2,1)S(1)}, u32[]{:S(2)}, u32[]{:S(2)}) %collective-permute-start.29) | collective-permute-done | bytes 262176 | tf_op jit(solution)/shard_map/ppermute | solution.py:58
  133.2 3.8 %shard_map.326 = (f32[128,1024]{1,0:T(8,128)}, bf16[256,1024]{1,0:T(8,128)(2,1)}, bf16[256,1024]{1,0:T(8,128)(2,1)}, bf16[256,1024]{1,0:T(8,128)(2,1)}, bf16[128,1024]{1,0:T(8,128)(2,1)}) custom-call(bf16[128,1024]{1,0:T(8,128)(2,1)} %get-tuple-element.242.refs_0_, bf16[128,1024]{1,0:T(8,128)(2,1)} %copy-done.5, ...), custom_call_target="tpu_custom_call" | custom-call | flops 11000000 | bytes 35000 | tf_op jit(solution)/shard_map/pallas_call | solution.py:118
  140.3 6.4 %shard_map.327 = (bf16[512,1024]{1,0:T(8,128)(2,1)}, f32[256,1024]{1,0:T(8,128)}, bf16[128,1024]{1,0:T(8,128)(2,1)}, bf16[128,1024]{1,0:T(8,128)(2,1)}, f32[1,1024]{1,0:T(1,128)S(1)}) custom-call(bf16[128,1024]{1,0:T(8,128)(2,1)} %get-tuple-element.242.refs_0_, bf16[128,1024]{1,0:T(8,128)(2,1)} %copy-done.5, ...), custom_call_target="tpu_custom_call" | custom-call | flops 11000000 | bytes 35000 | tf_op jit(solution)/shard_map/pallas_call | solution.py:118
  152.1 3.9 %shard_map.330 = (f32[128,1024]{1,0:T(8,128)}, bf16[256,1024]{1,0:T(8,128)(2,1)}, bf16[256,1024]{1,0:T(8,128)(2,1)}, bf16[256,1024]{1,0:T(8,128)(2,1)}, bf16[128,1024]{1,0:T(8,128)(2,1)}) custom-call(bf16[128,1024]{1,0:T(8,128)(2,1)} %get-tuple-element.227.refs_3_.refs_0_, bf16[128,1024]{1,0:T(8,128)(2,1)} %get-tuple-element.258.refs_1_, ...), custom_call_target="tpu_custom_call" | custom-call | flops 11000000 | bytes 35000 | tf_op jit(solution)/shard_map/pallas_call | solution.py:118
  162.7 3.7 %shard_map.329 = (f32[128,1024]{1,0:T(8,128)}, bf16[144,1024]{1,0:T(8,128)(2,1)}) custom-call(s32[2]{0:T(128)S(1)} %pad_add_fusion.refs_0_, f32[128,1]{1,0:T(8,128)S(1)} %get-tuple-element.240.refs_1_, f32[8,1024]{1,0:T(8,128)S(1)} %get-tuple-element.218.refs_2_, f32[8,1024]{1,0:T(8,128)} %get-tuple-element.241.refs_3_, ...), custom_call_target="tpu_custom_call" | custom-call | flops 8800000000 | bytes 28000000 | tf_op jit(solution)/shard_map/pallas_call | solution.py:118
  166.4 22.8 %conditional.8 = (f32[256,1024]{1,0:T(8,128)}, bf16[256,1024]{1,0:T(8,128)(2,1)}, f32[128,1024]{1,0:T(8,128)}, bf16[256,1024]{1,0:T(8,128)(2,1)}, bf16[272,1024]...) conditional(s32[]{:T(128)} %bitcast.3, () %tuple.52, ...), branch_computations={%region_6.0_spmd, %region_7.0_spmd} | conditional | flops 22000000 | bytes 4030548 | solution.py:151
  167.2 7.4 %collective-permute-done.5.refs_1_ = bf16[144,1024]{1,0:T(8,128)(2,1)} collective-permute-done((bf16[144,1024]{1,0:T(8,128)(2,1)}, bf16[144,1024]{1,0:T(8,128)(2,1)}, u32[]{:S(2)}, u32[]{:S(2)}) %collective-permute-start.5) | collective-permute-done | bytes 294944 | tf_op jit(solution)/shard_map/cond/branch_1_fun/ppermute | solution.py:58
  179.0 10.1 %branch_1_fun.12 = (bf16[512,768]{1,0:T(8,128)(2,1)}, f32[256,1024]{1,0:T(8,128)}, bf16[256,1024]{1,0:T(8,128)(2,1)}, f32[128,1024]{1,0:T(8,128)}, bf16[256,1024...) custom-call(f32[1,1024]{1,0:T(1,128)S(1)} %get-tuple-element.94.refs, ...), custom_call_target="tpu_custom_call" | custom-call | flops 11000000 | bytes 35000 | tf_op jit(solution)/shard_map/cond/branch_1_fun/pallas_call | solution.py:118
  196.3 15.4 %conditional.9 = (f32[128,1024]{1,0:T(8,128)}) conditional(s32[]{:T(128)} %bitcast.3, () %tuple.51, (bf16[256,1024]{1,0:T(8,128)(2,1)}, f32[256,1024]{1,0:T(8,128)}, s32[2]{0:T(128)S(1)}, f32[128,1024]{1,0:T(8,128)}, f32[128,1024]{1,0:T(8,128)}) %tuple.54), branch_computations={%region_8.0_spmd, %region_9.0_spmd} | conditional | flops 11393216 | bytes 6326572 | solution.py:151
  200.9 7.9 %collective-permute-done.10.refs_3_ = bf16[128,1024]{1,0:T(8,128)(2,1)} collective-permute-done((bf16[128,1024]{1,0:T(8,128)(2,1)S(1)}, bf16[128,1024]{1,0:T(8,128)(2,1)}, u32[]{:S(2)}, u32[]{:S(2)}) %collective-permute-start.10) | collective-permute-done | bytes 262176 | tf_op jit(solution)/shard_map/cond/branch_1_fun/ppermute | solution.py:58
  208.8 2.9 %branch_1_fun.13 = f32[128,1024]{1,0:T(8,128)} custom-call(s32[2]{0:T(128)S(1)} %get-tuple-element.116.refs_0_, f32[256,1024]{1,0:T(8,128)} %get-tuple-element.117.refs_1_, bf16[256,1024]{1,0:T(8,128)(2,1)} %copy-done.4, bf16[128,1024]{1,0:T(8,128)(2,1)} %collective-permute-done.10.refs_3_, f32[128,1024]{1,0:T(8,128)} %get-tuple-element.119.refs_4_, ...), custom_call_target="tpu_custom_call" | custom-call | flops 11000000 | bytes 35000 | tf_op jit(solution)/shard_map/cond/branch_1_fun/pallas_call | solution.py:118
  211.7 7.5 %collective-permute-done.44.refs_10_.refs_3_ = bf16[128,1024]{1,0:T(8,128)(2,1)} collective-permute-done((bf16[128,1024]{1,0:T(8,128)(2,1)}, bf16[128,1024]{1,0:T(8,128)(2,1)}, u32[]{:S(2)}, u32[]{:S(2)}) %collective-permute-start.44) | collective-permute-done | bytes 262176 | tf_op jit(solution)/shard_map/ppermute | solution.py:58
  220.1 2.8 %shard_map.333 = (bf16[144,1024]{1,0:T(8,128)(2,1)}, bf16[144,1024]{1,0:T(8,128)(2,1)}, bf16[400,1024]{1,0:T(8,128)(2,1)}) custom-call(bf16[256,1024]{1,0:T(8,128)(2,1)} %get-tuple-element.269.refs_0_, bf16[272,1024]{1,0:T(8,128)(2,1)} %collective-permute-done.38.refs_1_, bf16[128,1024]{1,0:T(8,128)(2,1)} %get-tuple-element.271.refs_2_, ...), custom_call_target="tpu_custom_call" | custom-call | flops 11000000 | bytes 35000 | tf_op jit(solution)/shard_map/pallas_call | solution.py:118
  225.7 16.4 %collective-permute-done.47.refs_4_.refs_9_ = bf16[400,1024]{1,0:T(8,128)(2,1)} collective-permute-done((bf16[400,1024]{1,0:T(8,128)(2,1)}, bf16[400,1024]{1,0:T(8,128)(2,1)}, u32[]{:S(2)}, u32[]{:S(2)}) %collective-permute-start.47) | collective-permute-done | bytes 819232 | tf_op jit(solution)/shard_map/ppermute | solution.py:58
  (138 shorter events, 93.4 us)
Async XLA Ops:
  2.5 23.3 %collective-permute-start.13 = (bf16[128,1024]{1,0:T(8,128)(2,1)}, bf16[128,1024]{1,0:T(8,128)(2,1)}, u32[]{:S(2)}, u32[]{:S(2)}) collective-permute-start(bf16[128,1024]{1,0:T(8,128)(2,1)} %shard_map.317.refs_0_.refs_6_.refs_1_), channel_id=1, source_target_pairs={{0,8},{4,12},{8,0},{12,4},{16,24},{20,28},{24,16},{28,20},{1,9},{5... | collective-permute-start | bytes 786440 | tf_op jit(solution)/shard_map/ppermute | solution.py:58
  5.5 20.3 %collective-permute-start.12 = (bf16[128,1024]{1,0:T(8,128)(2,1)}, bf16[128,1024]{1,0:T(8,128)(2,1)}, u32[]{:S(2)}, u32[]{:S(2)}) collective-permute-start(bf16[128,1024]{1,0:T(8,128)(2,1)} %shard_map.317.refs_0_.refs_6_.refs_1_), channel_id=1, source_target_pairs={{0,24},{4,28},{8,16},{12,20},{16,8},{20,12},{24,0},{28,4},{1,25},{... | collective-permute-start | bytes 786440 | tf_op jit(solution)/shard_map/ppermute | solution.py:58
  8.0 23.3 %collective-permute-start.11 = (bf16[128,1024]{1,0:T(8,128)(2,1)}, bf16[128,1024]{1,0:T(8,128)(2,1)}, u32[]{:S(2)}, u32[]{:S(2)}) collective-permute-start(bf16[128,1024]{1,0:T(8,128)(2,1)} %shard_map.317.refs_0_.refs_6_.refs_1_), channel_id=1, source_target_pairs={{0,16},{4,20},{8,24},{12,28},{16,0},{20,4},{24,8},{28,12},{1,17},{... | collective-permute-start | bytes 786440 | tf_op jit(solution)/shard_map/ppermute | solution.py:58
  10.3 28.3 %collective-permute-start.15 = (bf16[384,1024]{1,0:T(8,128)(2,1)}, bf16[384,1024]{1,0:T(8,128)(2,1)S(1)}, u32[]{:S(2)}, u32[]{:S(2)}) collective-permute-start(bf16[384,1024]{1,0:T(8,128)(2,1)} %shard_map.318.refs_0_.refs_7_), channel_id=1, source_target_pairs={{0,4},{4,0},{8,12},{12,8},{16,20},{20,16},{24,28},{28,24},{1,5},{5... | collective-permute-start | bytes 2359304 | tf_op jit(solution)/shard_map/ppermute | solution.py:58
  33.5 18.8 %collective-permute-start.14 = (bf16[384,1024]{1,0:T(8,128)(2,1)}, bf16[384,1024]{1,0:T(8,128)(2,1)}, u32[]{:S(2)}, u32[]{:S(2)}) collective-permute-start(bf16[384,1024]{1,0:T(8,128)(2,1)} %get-tuple-element.222), channel_id=1, source_target_pairs={{0,4},{4,0},{8,12},{12,8},{16,20},{20,16},{24,28},{28,24},{1,5},{5... | collective-permute-start | bytes 2359304 | tf_op jit(solution)/shard_map/ppermute | solution.py:58
  35.1 24.1 %collective-permute-start.18 = (bf16[128,1024]{1,0:T(8,128)(2,1)}, bf16[128,1024]{1,0:T(8,128)(2,1)}, u32[]{:S(2)}, u32[]{:S(2)}) collective-permute-start(bf16[128,1024]{1,0:T(8,128)(2,1)} %get-tuple-element.223.refs_12_.refs_13_), channel_id=1, source_target_pairs={{0,8},{4,12},{8,0},{12,4},{16,24},{20,28},{24,16},{28,20},{1,9},{5... | collective-permute-start | bytes 786440 | tf_op jit(solution)/shard_map/ppermute | solution.py:58
  35.1 24.1 %collective-permute-start.17 = (bf16[128,1024]{1,0:T(8,128)(2,1)}, bf16[128,1024]{1,0:T(8,128)(2,1)}, u32[]{:S(2)}, u32[]{:S(2)}) collective-permute-start(bf16[128,1024]{1,0:T(8,128)(2,1)} %get-tuple-element.223.refs_12_.refs_13_), channel_id=1, source_target_pairs={{0,24},{4,28},{8,16},{12,20},{16,8},{20,12},{24,0},{28,4},{1,25},{... | collective-permute-start | bytes 786440 | tf_op jit(solution)/shard_map/ppermute | solution.py:58
  37.7 22.6 %collective-permute-start.16 = (bf16[128,1024]{1,0:T(8,128)(2,1)}, bf16[128,1024]{1,0:T(8,128)(2,1)}, u32[]{:S(2)}, u32[]{:S(2)}) collective-permute-start(bf16[128,1024]{1,0:T(8,128)(2,1)} %get-tuple-element.223.refs_12_.refs_13_), channel_id=1, source_target_pairs={{0,16},{4,20},{8,24},{12,28},{16,0},{20,4},{24,8},{28,12},{1,17},{... | collective-permute-start | bytes 786440 | tf_op jit(solution)/shard_map/ppermute | solution.py:58
  39.3 21.0 %collective-permute-start.19 = (bf16[128,1024]{1,0:T(8,128)(2,1)}, bf16[128,1024]{1,0:T(8,128)(2,1)}, u32[]{:S(2)}, u32[]{:S(2)}) collective-permute-start(bf16[128,1024]{1,0:T(8,128)(2,1)} %slice.22), channel_id=1, source_target_pairs={{0,8},{4,12},{8,0},{12,4},{16,24},{20,28},{24,16},{28,20},{1,9},{5... | collective-permute-start | bytes 786440 | tf_op jit(solution)/shard_map/ppermute | solution.py:58
  63.7 24.6 %collective-permute-start.20 = (bf16[384,1024]{1,0:T(8,128)(2,1)}, bf16[384,1024]{1,0:T(8,128)(2,1)}, u32[]{:S(2)}, u32[]{:S(2)}) collective-permute-start(bf16[384,1024]{1,0:T(8,128)(2,1)} %get-tuple-element.228), channel_id=1, source_target_pairs={{0,4},{4,0},{8,12},{12,8},{16,20},{20,16},{24,28},{28,24},{1,5},{5... | collective-permute-start | bytes 2359304 | tf_op jit(solution)/shard_map/ppermute | solution.py:58
  64.2 18.2 %collective-permute-start.22 = (bf16[128,1024]{1,0:T(8,128)(2,1)}, bf16[128,1024]{1,0:T(8,128)(2,1)}, u32[]{:S(2)}, u32[]{:S(2)}) collective-permute-start(bf16[128,1024]{1,0:T(8,128)(2,1)} %get-tuple-element.230.refs_2_), channel_id=1, source_target_pairs={{0,24},{4,28},{8,16},{12,20},{16,8},{20,12},{24,0},{28,4},{1,25},{... | collective-permute-start | bytes 786440 | tf_op jit(solution)/shard_map/ppermute | solution.py:58
  66.5 19.7 %collective-permute-start.21 = (bf16[128,1024]{1,0:T(8,128)(2,1)}, bf16[128,1024]{1,0:T(8,128)(2,1)}, u32[]{:S(2)}, u32[]{:S(2)}) collective-permute-start(bf16[128,1024]{1,0:T(8,128)(2,1)} %get-tuple-element.230.refs_2_), channel_id=1, source_target_pairs={{0,16},{4,20},{8,24},{12,28},{16,0},{20,4},{24,8},{28,12},{1,17},{... | collective-permute-start | bytes 786440 | tf_op jit(solution)/shard_map/ppermute | solution.py:58
  70.6 8.4 %collective-permute-start.8 = (bf16[128,1024]{1,0:T(8,128)(2,1)S(1)}, bf16[128,1024]{1,0:T(8,128)(2,1)S(1)}, u32[]{:S(2)}, u32[]{:S(2)}) collective-permute-start(bf16[128,1024]{1,0:T(8,128)(2,1)S(1)} %add_convert_fusion), channel_id=1, source_target_pairs={{0,2},{1,3},{2,0},{3,1},{4,6},{5,7},{6,4},{7,5},{8,10},{9,11},{10,... | collective-permute-start | bytes 786440 | tf_op jit(solution)/shard_map/cond/branch_1_fun/ppermute | solution.py:58
  86.3 16.2 %collective-permute-start.25 = (bf16[128,1024]{1,0:T(8,128)(2,1)}, bf16[128,1024]{1,0:T(8,128)(2,1)}, u32[]{:S(2)}, u32[]{:S(2)}) collective-permute-start(bf16[128,1024]{1,0:T(8,128)(2,1)} %get-tuple-element.231.refs_1_.refs_4_), channel_id=1, source_target_pairs={{0,8},{4,12},{8,0},{12,4},{16,24},{20,28},{24,16},{28,20},{1,9},{5... | collective-permute-start | bytes 786440 | tf_op jit(solution)/shard_map/ppermute | solution.py:58
  86.3 16.3 %collective-permute-start.23 = (bf16[128,1024]{1,0:T(8,128)(2,1)}, bf16[128,1024]{1,0:T(8,128)(2,1)}, u32[]{:S(2)}, u32[]{:S(2)}) collective-permute-start(bf16[128,1024]{1,0:T(8,128)(2,1)} %get-tuple-element.232.refs_2_.refs_5_), channel_id=1, source_target_pairs={{0,4},{4,0},{8,12},{12,8},{16,20},{20,16},{24,28},{28,24},{1,5},{5... | collective-permute-start | bytes 786440 | tf_op jit(solution)/shard_map/ppermute | solution.py:58
  87.5 15.0 %collective-permute-start.24 = (bf16[128,1024]{1,0:T(8,128)(2,1)}, bf16[128,1024]{1,0:T(8,128)(2,1)}, u32[]{:S(2)}, u32[]{:S(2)}) collective-permute-start(bf16[128,1024]{1,0:T(8,128)(2,1)} %get-tuple-element.233.refs_3_.refs_6_), channel_id=1, source_target_pairs={{0,4},{4,0},{8,12},{12,8},{16,20},{20,16},{24,28},{28,24},{1,5},{5... | collective-permute-start | bytes 786440 | tf_op jit(solution)/shard_map/ppermute | solution.py:58
  110.5 8.7 %collective-permute-start.28 = (bf16[128,1024]{1,0:T(8,128)(2,1)}, bf16[128,1024]{1,0:T(8,128)(2,1)}, u32[]{:S(2)}, u32[]{:S(2)}) collective-permute-start(bf16[128,1024]{1,0:T(8,128)(2,1)} %shard_map.324), channel_id=1, source_target_pairs={{0,2},{1,3},{2,0},{3,1},{4,6},{5,7},{6,4},{7,5},{8,10},{9,11},{10,... | collective-permute-start | bytes 786440 | tf_op jit(solution)/shard_map/ppermute | solution.py:58
  137.0 19.8 %collective-permute-start.35 = (bf16[256,1024]{1,0:T(8,128)(2,1)}, bf16[256,1024]{1,0:T(8,128)(2,1)}, u32[]{:S(2)}, u32[]{:S(2)}) collective-permute-start(bf16[256,1024]{1,0:T(8,128)(2,1)} %get-tuple-element.255), channel_id=1, source_target_pairs={{0,4},{4,0},{8,12},{12,8},{16,20},{20,16},{24,28},{28,24},{1,5},{5... | collective-permute-start | bytes 1572872 | tf_op jit(solution)/shard_map/ppermute | solution.py:58
  138.3 18.5 %collective-permute-start.36 = (bf16[256,1024]{1,0:T(8,128)(2,1)}, bf16[256,1024]{1,0:T(8,128)(2,1)}, u32[]{:S(2)}, u32[]{:S(2)}) collective-permute-start(bf16[256,1024]{1,0:T(8,128)(2,1)} %get-tuple-element.257), channel_id=1, source_target_pairs={{0,8},{4,12},{8,0},{12,4},{16,24},{20,28},{24,16},{28,20},{1,9},{5... | collective-permute-start | bytes 1572872 | tf_op jit(solution)/shard_map/ppermute | solution.py:58
  150.5 12.2 %collective-permute-start.34 = (bf16[128,1024]{1,0:T(8,128)(2,1)}, bf16[128,1024]{1,0:T(8,128)(2,1)}, u32[]{:S(2)}, u32[]{:S(2)}) collective-permute-start(bf16[128,1024]{1,0:T(8,128)(2,1)} %shard_map.328), channel_id=1, source_target_pairs={{0,2},{1,3},{2,0},{3,1},{4,6},{5,7},{6,4},{7,5},{8,10},{9,11},{10,... | collective-permute-start | bytes 786440 | tf_op jit(solution)/shard_map/ppermute | solution.py:58
  156.0 34.4 %collective-permute-start.39 = (bf16[256,1024]{1,0:T(8,128)(2,1)}, bf16[256,1024]{1,0:T(8,128)(2,1)}, u32[]{:S(2)}, u32[]{:S(2)}) collective-permute-start(bf16[256,1024]{1,0:T(8,128)(2,1)} %get-tuple-element.274), channel_id=1, source_target_pairs={{0,4},{4,0},{8,12},{12,8},{16,20},{20,16},{24,28},{28,24},{1,5},{5... | collective-permute-start | bytes 1572872 | tf_op jit(solution)/shard_map/ppermute | solution.py:58
  156.8 34.8 %collective-permute-start.40 = (bf16[256,1024]{1,0:T(8,128)(2,1)}, bf16[256,1024]{1,0:T(8,128)(2,1)}, u32[]{:S(2)}, u32[]{:S(2)}) collective-permute-start(bf16[256,1024]{1,0:T(8,128)(2,1)} %get-tuple-element.276), channel_id=1, source_target_pairs={{0,8},{4,12},{8,0},{12,4},{16,24},{20,28},{24,16},{28,20},{1,9},{5... | collective-permute-start | bytes 1572872 | tf_op jit(solution)/shard_map/ppermute | solution.py:58
  159.2 32.4 %collective-permute-start.41 = (bf16[128,1024]{1,0:T(8,128)(2,1)}, bf16[128,1024]{1,0:T(8,128)(2,1)}, u32[]{:S(2)}, u32[]{:S(2)}) collective-permute-start(bf16[128,1024]{1,0:T(8,128)(2,1)} %get-tuple-element.277), channel_id=1, source_target_pairs={{0,24},{4,28},{8,16},{12,20},{16,8},{20,12},{24,0},{28,4},{1,25},{... | collective-permute-start | bytes 786440 | tf_op jit(solution)/shard_map/ppermute | solution.py:58
  161.2 30.4 %collective-permute-start.42 = (bf16[128,1024]{1,0:T(8,128)(2,1)}, bf16[128,1024]{1,0:T(8,128)(2,1)}, u32[]{:S(2)}, u32[]{:S(2)}) collective-permute-start(bf16[128,1024]{1,0:T(8,128)(2,1)} %get-tuple-element.278), channel_id=1, source_target_pairs={{0,16},{4,20},{8,24},{12,28},{16,0},{20,4},{24,8},{28,12},{1,17},{... | collective-permute-start | bytes 786440 | tf_op jit(solution)/shard_map/ppermute | solution.py:58
  189.1 30.1 %collective-permute-start.37 = (bf16[272,1024]{1,0:T(8,128)(2,1)}, bf16[272,1024]{1,0:T(8,128)(2,1)S(1)}, u32[]{:S(2)}, u32[]{:S(2)}) collective-permute-start(bf16[272,1024]{1,0:T(8,128)(2,1)} %get-tuple-element.268), channel_id=1, source_target_pairs={{0,8},{4,12},{8,0},{12,4},{16,24},{20,28},{24,16},{28,20},{1,9},{5... | collective-permute-start | bytes 1671176 | tf_op jit(solution)/shard_map/ppermute | solution.py:58
  190.4 28.9 %collective-permute-start.38 = (bf16[272,1024]{1,0:T(8,128)(2,1)}, bf16[272,1024]{1,0:T(8,128)(2,1)}, u32[]{:S(2)}, u32[]{:S(2)}) collective-permute-start(bf16[272,1024]{1,0:T(8,128)(2,1)} %get-tuple-element.270), channel_id=1, source_target_pairs={{0,4},{4,0},{8,12},{12,8},{16,20},{20,16},{24,28},{28,24},{1,5},{5... | collective-permute-start | bytes 1671176 | tf_op jit(solution)/shard_map/ppermute | solution.py:58
  193.9 17.8 %collective-permute-start.43 = (bf16[128,1024]{1,0:T(8,128)(2,1)}, bf16[128,1024]{1,0:T(8,128)(2,1)}, u32[]{:S(2)}, u32[]{:S(2)}) collective-permute-start(bf16[128,1024]{1,0:T(8,128)(2,1)} %get-tuple-element.280), channel_id=1, source_target_pairs={{0,24},{4,28},{8,16},{12,20},{16,8},{20,12},{24,0},{28,4},{1,25},{... | collective-permute-start | bytes 786440 | tf_op jit(solution)/shard_map/ppermute | solution.py:58
  196.2 23.1 %collective-permute-start.44 = (bf16[128,1024]{1,0:T(8,128)(2,1)}, bf16[128,1024]{1,0:T(8,128)(2,1)}, u32[]{:S(2)}, u32[]{:S(2)}) collective-permute-start(bf16[128,1024]{1,0:T(8,128)(2,1)} %get-tuple-element.281), channel_id=1, source_target_pairs={{0,16},{4,20},{8,24},{12,28},{16,0},{20,4},{24,8},{28,12},{1,17},{... | collective-permute-start | bytes 786440 | tf_op jit(solution)/shard_map/ppermute | solution.py:58
  200.3 8.5 %collective-permute-start.10 = (bf16[128,1024]{1,0:T(8,128)(2,1)S(1)}, bf16[128,1024]{1,0:T(8,128)(2,1)}, u32[]{:S(2)}, u32[]{:S(2)}) collective-permute-start(bf16[128,1024]{1,0:T(8,128)(2,1)S(1)} %add_convert_fusion.1), channel_id=1, source_target_pairs={{0,2},{1,3},{2,0},{3,1},{4,6},{5,7},{6,4},{7,5},{8,10},{9,11},{10,... | collective-permute-start | bytes 786440 | tf_op jit(solution)/shard_map/cond/branch_1_fun/ppermute | solution.py:58
  222.8 19.2 %collective-permute-start.47 = (bf16[400,1024]{1,0:T(8,128)(2,1)}, bf16[400,1024]{1,0:T(8,128)(2,1)}, u32[]{:S(2)}, u32[]{:S(2)}) collective-permute-start(bf16[400,1024]{1,0:T(8,128)(2,1)} %get-tuple-element.284), channel_id=1, source_target_pairs={{0,4},{4,0},{8,12},{12,8},{16,20},{20,16},{24,28},{28,24},{1,5},{5... | collective-permute-start | bytes 2457608 | tf_op jit(solution)/shard_map/ppermute | solution.py:58
  223.7 22.9 %collective-permute-start.45 = (bf16[144,1024]{1,0:T(8,128)(2,1)}, bf16[144,1024]{1,0:T(8,128)(2,1)S(1)}, u32[]{:S(2)}, u32[]{:S(2)}) collective-permute-start(bf16[144,1024]{1,0:T(8,128)(2,1)} %get-tuple-element.282), channel_id=1, source_target_pairs={{0,24},{4,28},{8,16},{12,20},{16,8},{20,12},{24,0},{28,4},{1,25},{... | collective-permute-start | bytes 884744 | tf_op jit(solution)/shard_map/ppermute | solution.py:58
  225.7 23.1 %collective-permute-start.46 = (bf16[144,1024]{1,0:T(8,128)(2,1)}, bf16[144,1024]{1,0:T(8,128)(2,1)S(1)}, u32[]{:S(2)}, u32[]{:S(2)}) collective-permute-start(bf16[144,1024]{1,0:T(8,128)(2,1)} %get-tuple-element.283.refs_5_), channel_id=1, source_target_pairs={{0,16},{4,20},{8,24},{12,28},{16,0},{20,4},{24,8},{28,12},{1,17},{... | collective-permute-start | bytes 884744 | tf_op jit(solution)/shard_map/ppermute | solution.py:58
  (33 other events, 232.1 us)
